TPU v7x, 128 devices: a whole 4x4x4 slice. The times are simulated.
128 devices in a mesh: lat: 8 (over x, core), lon: 16 (over y, z).
Axes of the slice: x: 4, y: 4, z: 4, core: 2. Of those that a mesh axis runs over, the one named last changes fastest.
Arguments:
- grid_tokens: bfloat16 [128, 256, 512], P('lat', 'lon'), may hold values from -30 to 30
- obs_tokens: bfloat16 [2048, 128, 512], P(('lat', 'lon')), may hold values from -30 to 30
- destinations: int32 [2048, 1], P(('lat', 'lon')), may hold values from 0 to 15; in each aligned block of 16 rows (0 to 15, 16 to 31, ...) at most 2 rows name the same one
- valid_counts: int32 [128, 16], P(('lat', 'lon')), may hold values from 1 to 128, 1536 in all within a row
- w_query: bfloat16 [512, 512], replicated, may hold values from -0.25 to 0.25
- w_key: bfloat16 [512, 512], replicated, may hold values from -0.25 to 0.25
- w_value: bfloat16 [512, 512], replicated, may hold values from -0.25 to 0.25
- w_out: bfloat16 [512, 512], replicated, may hold values from -0.25 to 0.25
- stencil_taps: float32 [5, 512], replicated, may hold values from -3 to 3
- cotangent: bfloat16 [128, 256, 512], P('lat', 'lon'), may hold values from -6 to 6
Outputs:
- encoded: bfloat16 [128, 256, 512], P('lat', 'lon')
- grad_grid: bfloat16 [128, 256, 512], P('lat', 'lon')
- grad_obs: bfloat16 [2048, 128, 512], P(('lat', 'lon'))
- grad_w_query: float32 [512, 512], replicated
- grad_w_key: float32 [512, 512], replicated
- grad_w_value: float32 [512, 512], replicated
- grad_w_out: float32 [512, 512], replicated
- grad_taps: float32 [5, 512], replicated
Inputs may be any that keep to these rules, and one draw needn't show every extreme that they name: `destinations`: within one ingest device's 16 blocks no tile column is named more than 2 times, and some device names one exactly 2 times. `valid_counts`: each ingest device's 16 counts sum to 1536, and one of them is 128.
All inputs are finite; a program needn't handle non-finite values.
Results may differ from a plain program's by a relative error of at most 0.012.
The roundings to bfloat16 on the way count: a program that leaves them out, or rounds other values in their place, can miss the bound.
Values may be sent and summed in bfloat16 or wider, within the bound.
A program may use at most 192 MiB of HBM per device.

v0:
```python
import jax
import jax.numpy as jnp
from jax import lax
from jax.sharding import PartitionSpec as P

D = 512
HEADS = 8
BLK = 128
CAP = 2


def padded(cells, sides, width, closed):
    for axis, dim in sides:
        count = lax.axis_size(axis)
        ends = count if closed else count - 1
        head = lax.slice_in_dim(cells, 0, width, axis=dim)
        tail = lax.slice_in_dim(cells, cells.shape[dim] - width, cells.shape[dim], axis=dim)
        cells = jnp.concatenate(
            [
                lax.ppermute(tail, axis, [(i, (i + 1) % count) for i in range(ends)]),
                cells,
                lax.ppermute(head, axis, [((i + 1) % count, i) for i in range(ends)]),
            ],
            axis=dim,
        )
    return cells


def product(former, latter):
    return jnp.dot(former, latter, preferred_element_type=jnp.float32)


def product_tn(former, latter):
    return lax.dot_general(
        former, latter, (((0,), (0,)), ((), ())), preferred_element_type=jnp.float32
    )


def product_nt(former, latter):
    return lax.dot_general(
        former, latter, (((1,), (1,)), ((), ())), preferred_element_type=jnp.float32
    )


def head_slices(source, number, column_span):
    picked = lax.dynamic_slice_in_dim(source, number * column_span, column_span, 1)
    return picked.reshape(source.shape[0], 2, column_span // 2)


def pair_weights(query_pair, key_pair, live_keys, scaling):
    scores = (
        jnp.einsum("qhd,khd->hqk", query_pair, key_pair, preferred_element_type=jnp.float32)
        * scaling
    )
    scores = jnp.where(live_keys[None, None, :], scores, -1e30)
    largest = jnp.max(scores, 2, keepdims=True)
    raised = jnp.exp(scores - largest)
    return raised / jnp.sum(raised, 2, keepdims=True)


def rejoin(pieces):
    return pieces.transpose(1, 0, 2).reshape(pieces.shape[1], pieces.shape[0] * pieces.shape[2])


def attend(queries, key_rows, value_rows, live_keys):
    column_span = 2 * (D // HEADS)
    scaling = (D // HEADS) ** (-0.5)

    def one_pair(number):
        query_pair = head_slices(queries, number, column_span)
        key_pair = head_slices(key_rows, number, column_span)
        value_pair = head_slices(value_rows, number, column_span)
        weights = pair_weights(query_pair, key_pair, live_keys, scaling)
        mixture = jnp.einsum(
            "hqk,khd->qhd",
            weights.astype(jnp.bfloat16),
            value_pair,
            preferred_element_type=jnp.float32,
        )
        return mixture.reshape(queries.shape[0], column_span).astype(jnp.bfloat16)

    return rejoin(lax.map(one_pair, jnp.arange(HEADS // 2, dtype=jnp.int32)))


def attend_back(queries, key_rows, value_rows, live_keys, upstream):
    column_span = 2 * (D // HEADS)
    scaling = (D // HEADS) ** (-0.5)

    def one_pair(number):
        query_pair = head_slices(queries, number, column_span)
        key_pair = head_slices(key_rows, number, column_span)
        value_pair = head_slices(value_rows, number, column_span)
        grad_pair = head_slices(upstream, number, column_span)
        weights = pair_weights(query_pair, key_pair, live_keys, scaling)
        grad_weights = jnp.einsum(
            "qhd,khd->hqk", grad_pair, value_pair, preferred_element_type=jnp.float32
        )
        inner_sum = jnp.sum(weights * grad_weights, 2, keepdims=True)
        grad_scores = (weights * (grad_weights - inner_sum) * scaling).astype(jnp.bfloat16)
        grad_query = jnp.einsum(
            "hqk,khd->qhd", grad_scores, key_pair, preferred_element_type=jnp.float32
        )
        grad_key = jnp.einsum(
            "hqk,qhd->khd", grad_scores, query_pair, preferred_element_type=jnp.float32
        )
        grad_value = jnp.einsum(
            "hqk,qhd->khd",
            weights.astype(jnp.bfloat16),
            grad_pair,
            preferred_element_type=jnp.float32,
        )
        return (
            grad_query.reshape(queries.shape[0], column_span).astype(jnp.bfloat16),
            grad_key.reshape(key_rows.shape[0], column_span).astype(jnp.bfloat16),
            grad_value.reshape(key_rows.shape[0], column_span).astype(jnp.bfloat16),
        )

    query_parts, key_parts, value_parts = lax.map(one_pair, jnp.arange(HEADS // 2, dtype=jnp.int32))
    return (rejoin(query_parts), rejoin(key_parts), rejoin(value_parts))


def on_device(
    grid_tokens,
    obs_tokens,
    destinations,
    valid_counts,
    w_query,
    w_key,
    w_value,
    w_out,
    stencil_taps,
    cotangent,
):
    tile_rows, tile_columns = (grid_tokens.shape[0], grid_tokens.shape[1])
    cell_count = tile_rows * tile_columns
    block_count = obs_tokens.shape[0]
    peer_count = lax.axis_size("lon")
    slot_count = peer_count * CAP
    flat_grid = grid_tokens.reshape(cell_count, D)
    w_pair = jnp.concatenate([w_key, w_value], 1)
    queries = product(flat_grid, w_query).astype(jnp.bfloat16)
    own_pairs = product(flat_grid, w_pair).astype(jnp.bfloat16)
    target = destinations[:, 0]
    order_ids = jnp.arange(block_count, dtype=jnp.int32)
    earlier = (target[:, None] == target[None, :]) & (order_ids[None, :] < order_ids[:, None])
    rank_ids = jnp.sum(earlier.astype(jnp.int32), 1)
    slot_ids = target * CAP + rank_ids
    chooser = slot_ids[None, :] == jnp.arange(slot_count, dtype=jnp.int32)[:, None]
    selector = chooser.astype(jnp.bfloat16)
    sent_counts = (
        jnp.sum(jnp.where(chooser, valid_counts[0][None, :], 0), 1)
        .astype(jnp.bfloat16)
        .reshape(peer_count, CAP)
    )
    outgoing = jnp.einsum(
        "sb,btd->std", selector, obs_tokens, preferred_element_type=jnp.float32
    ).astype(jnp.bfloat16)
    arrived, arrived_counts = (
        lax.all_to_all(
            outgoing.reshape(peer_count, CAP * BLK, D),
            "lon",
            split_axis=0,
            concat_axis=0,
            tiled=True,
        ),
        lax.all_to_all(sent_counts, "lon", split_axis=0, concat_axis=0, tiled=True),
    )
    obs_rows = arrived.reshape(slot_count * BLK, D)
    obs_pairs = product(obs_rows, w_pair).astype(jnp.bfloat16)
    positions = jnp.arange(BLK, dtype=jnp.float32)
    live_obs = (
        positions[None, :] < arrived_counts.reshape(slot_count, 1).astype(jnp.float32)
    ).reshape(slot_count * BLK)
    live_keys = jnp.concatenate([jnp.ones((cell_count,), jnp.bool_), live_obs])
    key_rows = jnp.concatenate([own_pairs[:, :D], obs_pairs[:, :D]], 0)
    value_rows = jnp.concatenate([own_pairs[:, D:], obs_pairs[:, D:]], 0)
    attended = attend(queries, key_rows, value_rows, live_keys)
    middle = (flat_grid.astype(jnp.float32) + product(attended, w_out)).astype(jnp.bfloat16)
    stacked = jnp.stack([middle.reshape(tile_rows, tile_columns, D), cotangent])
    lat_ext = padded(stacked, (("lat", 1),), 1, False)
    lon_ext = padded(stacked, (("lon", 2),), 1, True)
    centre = stacked.astype(jnp.float32)
    northern = lat_ext[:, :-2].astype(jnp.float32)
    southern = lat_ext[:, 2:].astype(jnp.float32)
    western = lon_ext[:, :, :-2].astype(jnp.float32)
    eastern = lon_ext[:, :, 2:].astype(jnp.float32)
    encoded = (
        (1.0 + stencil_taps[0]) * centre[0]
        + stencil_taps[1] * northern[0]
        + stencil_taps[2] * southern[0]
        + stencil_taps[3] * western[0]
        + stencil_taps[4] * eastern[0]
    ).astype(jnp.bfloat16)
    grad_middle = (
        (1.0 + stencil_taps[0]) * centre[1]
        + stencil_taps[1] * southern[1]
        + stencil_taps[2] * northern[1]
        + stencil_taps[3] * eastern[1]
        + stencil_taps[4] * western[1]
    ).astype(jnp.bfloat16)
    tap_terms = jnp.stack(
        [
            jnp.sum(centre[1] * centre[0], (0, 1)),
            jnp.sum(centre[1] * northern[0], (0, 1)),
            jnp.sum(centre[1] * southern[0], (0, 1)),
            jnp.sum(centre[1] * western[0], (0, 1)),
            jnp.sum(centre[1] * eastern[0], (0, 1)),
        ]
    )
    grad_flat_mid = grad_middle.reshape(cell_count, D)
    grad_wout = product_tn(attended, grad_flat_mid)
    grad_attended = product_nt(grad_flat_mid, w_out).astype(jnp.bfloat16)
    grad_queries, grad_keys, grad_values = attend_back(
        queries, key_rows, value_rows, live_keys, grad_attended
    )
    grad_pairs = jnp.concatenate([grad_keys, grad_values], 1)
    own_grads = grad_pairs[:cell_count]
    obs_grads = grad_pairs[cell_count:]
    grad_grid = (
        grad_flat_mid.astype(jnp.float32)
        + product_nt(grad_queries, w_query)
        + product_nt(own_grads, w_pair)
    ).astype(jnp.bfloat16)
    grad_wquery = product_tn(flat_grid, grad_queries)
    grad_wpair = product_tn(flat_grid, own_grads)
    slot_grads = product_nt(obs_grads, w_pair).astype(jnp.bfloat16)
    returned = lax.all_to_all(
        slot_grads.reshape(peer_count, CAP * BLK, D), "lon", split_axis=0, concat_axis=0, tiled=True
    )
    grad_obs = jnp.einsum(
        "sb,std->btd",
        selector,
        returned.reshape(slot_count, BLK, D),
        preferred_element_type=jnp.float32,
    ).astype(jnp.bfloat16)
    grad_wpair = grad_wpair + product_tn(obs_rows, obs_grads)
    summed = lax.psum((grad_wquery, grad_wpair, grad_wout, tap_terms), ("lat", "lon"))
    return (
        encoded,
        grad_grid.reshape(tile_rows, tile_columns, D),
        grad_obs,
        summed[0],
        summed[1][:, :D],
        summed[1][:, D:],
        summed[2],
        summed[3],
    )


def solution(mesh):
    in_specs = (
        P("lat", "lon", None),
        P(("lat", "lon"), None, None),
        P(("lat", "lon"), None),
        P(("lat", "lon"), None),
        P(),
        P(),
        P(),
        P(),
        P(),
        P("lat", "lon", None),
    )
    out_specs = (
        P("lat", "lon", None),
        P("lat", "lon", None),
        P(("lat", "lon"), None, None),
        P(),
        P(),
        P(),
        P(),
        P(),
    )
    return jax.shard_map(
        on_device, mesh=mesh, in_specs=in_specs, out_specs=out_specs, check_vma=False
    )
```

profile of v0, /device:TPU:1, one launch (start us, length us, event | category | flops | bytes accessed | tf_op | source)
XLA Modules:
  0.0 567.0 jit_solution(8761133354569125924)
XLA Ops:
  10.3 8.6 %all-to-all-start.1 = ((bf16[16,1,2]{2,1,0:T(2,128)(2,1)}), bf16[16,1,2]{2,1,0:T(2,128)(2,1)S(1)}, u32[]{:S(2)}, u32[]{:S(2)}) async-start(bf16[16,1,2]{2,1,0:T(2,128)(2,1)} %convert_element_type.192), calls=%async_computation.1 | async-start | bytes 16384 | tf_op jit(solution)/shard_map/all_to_all | solution.py:166
  18.9 1.6 convolution_convert_fusion.5
  20.5 4.3 copy.63
  25.2 6.8 %all-to-all-start = ((bf16[16,256,512]{2,1,0:T(8,128)(2,1)}), bf16[16,256,512]{2,1,0:T(8,128)(2,1)}, u32[]{:S(2)}, u32[]{:S(2)}) async-start(bf16[16,256,512]{2,1,0:T(8,128)(2,1)} %bitcast.240), calls=%async_computation | async-start | bytes 8388608 | tf_op jit(solution)/shard_map/all_to_all | solution.py:159
  33.4 50.5 %all-to-all-done = bf16[16,256,512]{2,1,0:T(8,128)(2,1)} async-done(((bf16[16,256,512]{2,1,0:T(8,128)(2,1)}), bf16[16,256,512]{2,1,0:T(8,128)(2,1)}, u32[]{:S(2)}, u32[]{:S(2)}) %all-to-all-start) | async-done | bytes 4194336 | tf_op jit(solution)/shard_map/all_to_all | solution.py:159
  83.9 6.9 %convolution_convert_fusion.3 = bf16[4096,1024]{1,0:T(8,128)(2,1)S(1)} fusion(bf16[4096,512]{1,0:T(8,128)(2,1)} %bitcast.23, bf16[512,1024]{1,0:T(8,128)(2,1)S(1)} %constant_dynamic-update-slice_fusion.4), kind=kOutput, calls=%fused_computation.32 | convolution fusion | flops 4299161600 | bytes 13631488 | tf_op jit(solution)/shard_map/dot_general | solution.py:30
  91.9 3.8 pad_maximum_fusion.3
  95.6 6.5 %copy.65 = bf16[4352,512]{0,1:T(8,128)(2,1)} copy(bf16[4352,512]{1,0:T(8,128)(2,1)} %get-tuple-element.280) | data formatting | bytes 8912896 | tf_op jit(solution)/shard_map/while | solution.py:82
  102.1 6.5 %copy.67 = bf16[4352,512]{0,1:T(8,128)(2,1)} copy(bf16[4352,512]{1,0:T(8,128)(2,1)} %get-tuple-element.281) | data formatting | bytes 8912896 | tf_op jit(solution)/shard_map/while | solution.py:82
  108.7 37.2 %while.24 = (s32[]{:T(128)}, bf16[4,256,128]{1,2,0:T(8,128)(2,1)S(1)}, s32[4]{0:T(128)S(1)}, bf16[4352,512]{0,1:T(8,128)(2,1)}, pred[4352]{0:T(1024)(128)(4,1)S(...) while((s32[]{:T(128)}, ...), condition=%wide.region_5.6_spmd, body=%wide.region_2.5_spmd.sunk | while | flops 583831808 | bytes 47194572 | solution.py:82
  109.9 2.7 constant_dynamic-slice_fusion.13
  114.0 2.3 exponential_reduce_fusion.4
  116.3 1.6 fusion.112
  119.2 2.7 constant_dynamic-slice_fusion.13
  123.3 2.3 exponential_reduce_fusion.4
  125.6 1.6 fusion.112
  128.5 2.7 constant_dynamic-slice_fusion.13
  132.6 2.3 exponential_reduce_fusion.4
  134.9 1.6 fusion.112
  137.8 2.7 constant_dynamic-slice_fusion.13
  141.9 2.3 exponential_reduce_fusion.4
  144.2 1.6 fusion.112
  146.9 4.3 collective-permute-start.3
  151.2 7.6 %collective-permute-start = (bf16[2,1,16,512]{3,2,1,0:T(8,128)(2,1)S(1)}, bf16[2,1,16,512]{3,2,1,0:T(8,128)(2,1)S(1)}, u32[]{:S(2)}, u32[]{:S(2)}) collective-permute-start(bf16[2,1,16,512]{3,2,1,0:T(8,128)(2,1)S(1)} %get-tuple-element.272), channel_id=1, source_target_pairs={{0,16},{16,32},{32,48},{48,64},{64,80},{80,96},{96,112},{1,17},{17... | collective-permute-start | bytes 98312 | tf_op jit(solution)/shard_map/ppermute | solution.py:20
  158.9 2.4 collective-permute-start.1
  161.4 2.6 collective-permute-done.1
  164.9 1.5 add_convert_fusion
  167.5 157.8 %while.25 = (s32[]{:T(128)}, bf16[4,256,128]{1,2,0:T(8,128)(2,1)S(1)}, bf16[4,4352,128]{1,2,0:T(8,128)(2,1)}, bf16[4,4352,128]{1,2,0:T(8,128)(2,1)}, s32[4]{0:T(...) while((s32[]{:T(128)}, ...), condition=%wide.region_10.11_spmd, body=%wide.region_6.10_spmd.sunk | while | flops 1456186368 | bytes 91106264 | solution.py:118
  171.6 5.0 exponential_reduce_fusion.5
  176.7 5.1 convolution_convert_fusion.13
  183.1 4.8 fusion.125
  187.9 15.1 %multiply_convert_fusion.2 = bf16[2,256,4352]{2,1,0:T(8,128)(2,1)S(1)} fusion(f32[2,256,4352]{2,1,0:T(8,128)} %fusion.125, f32[2,256]{1,0:T(2,128)S(1)} %get-tuple-element.398, f32[2,256,4352]{2,1,0:T(8,128)} %get-tuple-element.399), kind=kOutput, calls=%fused_computation.14.clone.1 | output fusion | flops 15602431 | bytes 22284288 | tf_op jit(solution)/shard_map/while/body/eval_jaxpr/sub | solution.py:99
  203.9 1.5 constant_dynamic-update-slice_fusion.11
  205.4 1.5 convolution_convert_fusion.12
  211.0 5.0 exponential_reduce_fusion.5
  216.1 5.1 convolution_convert_fusion.13
  222.5 4.8 fusion.125
  227.3 15.1 %multiply_convert_fusion.2 = bf16[2,256,4352]{2,1,0:T(8,128)(2,1)S(1)} fusion(f32[2,256,4352]{2,1,0:T(8,128)} %fusion.125, f32[2,256]{1,0:T(2,128)S(1)} %get-tuple-element.398, f32[2,256,4352]{2,1,0:T(8,128)} %get-tuple-element.399), kind=kOutput, calls=%fused_computation.14.clone.1 | output fusion | flops 15602431 | bytes 22284288 | tf_op jit(solution)/shard_map/while/body/eval_jaxpr/sub | solution.py:99
  243.3 1.5 constant_dynamic-update-slice_fusion.11
  244.8 1.4 convolution_convert_fusion.12
  250.4 5.0 exponential_reduce_fusion.5
  255.5 5.1 convolution_convert_fusion.13
  261.9 4.8 fusion.125
  266.7 15.1 %multiply_convert_fusion.2 = bf16[2,256,4352]{2,1,0:T(8,128)(2,1)S(1)} fusion(f32[2,256,4352]{2,1,0:T(8,128)} %fusion.125, f32[2,256]{1,0:T(2,128)S(1)} %get-tuple-element.398, f32[2,256,4352]{2,1,0:T(8,128)} %get-tuple-element.399), kind=kOutput, calls=%fused_computation.14.clone.1 | output fusion | flops 15602431 | bytes 22284288 | tf_op jit(solution)/shard_map/while/body/eval_jaxpr/sub | solution.py:99
  282.7 1.6 constant_dynamic-update-slice_fusion.11
  284.3 1.5 convolution_convert_fusion.12
  289.9 5.0 exponential_reduce_fusion.5
  295.0 5.1 convolution_convert_fusion.13
  301.4 4.8 fusion.125
  306.2 15.1 %multiply_convert_fusion.2 = bf16[2,256,4352]{2,1,0:T(8,128)(2,1)S(1)} fusion(f32[2,256,4352]{2,1,0:T(8,128)} %fusion.125, f32[2,256]{1,0:T(2,128)S(1)} %get-tuple-element.398, f32[2,256,4352]{2,1,0:T(8,128)} %get-tuple-element.399), kind=kOutput, calls=%fused_computation.14.clone.1 | output fusion | flops 15602431 | bytes 22284288 | tf_op jit(solution)/shard_map/while/body/eval_jaxpr/sub | solution.py:99
  322.2 1.5 constant_dynamic-update-slice_fusion.11
  323.7 1.5 convolution_convert_fusion.12
  326.7 1.4 copy-done.9
  328.1 8.9 %convolution_convert_fusion.4 = bf16[4096,512]{1,0:T(8,128)(2,1)} fusion(bf16[512,1024]{1,0:T(8,128)(2,1)S(1)} %copy-done.4, bf16[4352,512]{0,1:T(8,128)(2,1)} %bitcast.254, bf16[4352,512]{0,1:T(8,128)(2,1)S(1)} %bitcast.252), kind=kOutput, calls=%fused_computation.33 | convolution fusion | flops 4313841664 | bytes 14155776 | tf_op jit(solution)/shard_map/dot_general | solution.py:40
  339.6 6.6 %all-to-all-start.2 = ((bf16[16,256,512]{2,1,0:T(8,128)(2,1)}), bf16[16,256,512]{2,1,0:T(8,128)(2,1)}, u32[]{:S(2)}, u32[]{:S(2)}) async-start(bf16[16,256,512]{2,1,0:T(8,128)(2,1)} %bitcast.259), calls=%async_computation.2 | async-start | bytes 8388608 | tf_op jit(solution)/shard_map/all_to_all | solution.py:227
  346.3 9.1 %fusion.11 = f32[512,1024]{0,1:T(8,128)S(1)} fusion(bf16[4096,512]{1,0:T(8,128)(2,1)} %bitcast.23, bf16[4352,512]{0,1:T(8,128)(2,1)} %bitcast.255, bf16[4352,512]{0,1:T(8,128)(2,1)} %bitcast.251), kind=kOutput, calls=%fused_computation.34 | convolution fusion | flops 4311744512 | bytes 15204352 | tf_op jit(solution)/shard_map/dot_general | solution.py:34
  355.5 1.7 bitcast_add_fusion
  357.4 2.6 fusion.30
  359.9 113.2 %psum.31 = f32[5,512]{1,0:T(8,128)} all-reduce(f32[5,512]{1,0:T(8,128)S(1)} %stack.31), channel_id=1, replica_groups=mesh['lat'=8,'lon'=16] {'lat','lon'}, use_global_device_ids=true, to_apply=%region_19.20 | all-reduce | flops 2560 | bytes 20480 | tf_op jit(solution)/shard_map/psum | solution.py:237
  473.2 1.4 convolution_add_fusion.1
  475.8 69.7 %all-reduce.4.cloned.1.call-done = (f32[512,512]{0,1:T(8,128)}, f32[512,1024]{0,1:T(8,128)}, f32[512,512]{1,0:T(8,128)}) async-done(((f32[512,512]{0,1:T(8,128)}, f32[512,1024]{0,1:T(8,128)}, f32[512,512]{1,0:T(8,128)}), (f32[512,512]{0,1:T(8,128)}, f32[512,1024]{0,1:T(8,128)}, f32[512,512]{1,0:T(8,128)})) %all-reduce.4.cloned.1.call-update) | async-done | bytes 4194320 | tf_op jit(solution)/shard_map/psum | solution.py:237
  545.5 1.8 fusion.50
  551.2 5.2 fusion.15
  556.4 2.5 copy.74
  (181 shorter events, 49.6 us)
Async XLA Ops:
  7.2 11.7 %copy-start = (bf16[16,128,512]{2,1,0:T(8,128)(2,1)S(1)}, bf16[16,128,512]{2,1,0:T(8,128)(2,1)}, u32[]{:S(2)}) copy-start(bf16[16,128,512]{2,1,0:T(8,128)(2,1)} %param.15) | copy-start | bytes 6291460
  8.8 16.0 %copy-start.37 = (s32[16]{0:T(128)}, s32[16]{0:T(128)S(1)}, u32[]{:S(2)}) copy-start(s32[16]{0:T(128)S(1)} %multiply_add_fusion) | copy-start | bytes 196
  10.3 14.9 %all-to-all-start.1 = ((bf16[16,1,2]{2,1,0:T(2,128)(2,1)}), bf16[16,1,2]{2,1,0:T(2,128)(2,1)S(1)}, u32[]{:S(2)}, u32[]{:S(2)}) async-start(bf16[16,1,2]{2,1,0:T(2,128)(2,1)} %convert_element_type.192), calls=%async_computation.1 | async-start | bytes 16384 | tf_op jit(solution)/shard_map/all_to_all | solution.py:166
  24.9 7.2 %copy-start.5 = (bf16[16,16,512]{2,1,0:T(8,128)(2,1)S(1)}, bf16[16,16,512]{2,1,0:T(8,128)(2,1)}, u32[]{:S(2)}) copy-start(bf16[16,16,512]{2,1,0:T(8,128)(2,1)} %param.14) | copy-start | bytes 786436
  24.9 7.2 %copy-start.19 = (bf16[512,512]{1,0:T(8,128)(2,1)S(1)}, bf16[512,512]{1,0:T(8,128)(2,1)}, u32[]{:S(2)}) copy-start(bf16[512,512]{1,0:T(8,128)(2,1)} %param.18) | copy-start | bytes 1572868
  25.2 7.3 %copy-start.24 = (bf16[512,512]{1,0:T(8,128)(2,1)S(1)}, bf16[512,512]{1,0:T(8,128)(2,1)}, u32[]{:S(2)}) copy-start(bf16[512,512]{1,0:T(8,128)(2,1)} %param.19) | copy-start | bytes 1572868
  25.2 7.4 %copy-start.25 = (bf16[512,512]{1,0:T(8,128)(2,1)S(1)}, bf16[512,512]{1,0:T(8,128)(2,1)}, u32[]{:S(2)}) copy-start(bf16[512,512]{1,0:T(8,128)(2,1)} %param.20) | copy-start | bytes 1572868
  25.2 58.6 %all-to-all-start = ((bf16[16,256,512]{2,1,0:T(8,128)(2,1)}), bf16[16,256,512]{2,1,0:T(8,128)(2,1)}, u32[]{:S(2)}, u32[]{:S(2)}) async-start(bf16[16,256,512]{2,1,0:T(8,128)(2,1)} %bitcast.240), calls=%async_computation | async-start | bytes 8388608 | tf_op jit(solution)/shard_map/all_to_all | solution.py:159
  32.7 58.1 %copy-start.3 = (bf16[512,1024]{1,0:T(8,128)(2,1)}, bf16[512,1024]{1,0:T(8,128)(2,1)S(1)}, u32[]{:S(2)}) copy-start(bf16[512,1024]{1,0:T(8,128)(2,1)S(1)} %constant_dynamic-update-slice_fusion.4) | copy-start | bytes 3145732
  108.6 37.2 %copy-start.20 = (bf16[512,512]{1,0:T(8,128)(2,1)S(1)}, bf16[512,512]{1,0:T(8,128)(2,1)}, u32[]{:S(2)}) copy-start(bf16[512,512]{1,0:T(8,128)(2,1)} %param.21) | copy-start | bytes 1572868
  108.6 37.5 %copy-start.14 = (bf16[16,16,512]{2,1,0:T(8,128)(2,1)S(1)}, bf16[16,16,512]{2,1,0:T(8,128)(2,1)}, u32[]{:S(2)}) copy-start(bf16[16,16,512]{2,1,0:T(8,128)(2,1)} %param.23) | copy-start | bytes 786436
  108.7 52.7 %copy-start.36 = (f32[5,512]{1,0:T(8,128)S(1)}, f32[5,512]{1,0:T(8,128)}, u32[]{:S(2)}) copy-start(f32[5,512]{1,0:T(8,128)} %param.22) | copy-start | bytes 30724
  114.0 2.3 copy-start.2
  123.3 2.3 copy-start.2
  132.6 2.3 copy-start.2
  141.9 2.3 copy-start.2
  145.8 20.6 %copy-start.15 = (bf16[4,256,128]{1,2,0:T(8,128)(2,1)}, bf16[4,256,128]{1,2,0:T(8,128)(2,1)S(1)}, u32[]{:S(2)}) copy-start(bf16[4,256,128]{1,2,0:T(8,128)(2,1)S(1)} %get-tuple-element.99) | copy-start | bytes 786436
  146.4 15.1 %collective-permute-start.2 = (bf16[2,16,1,512]{3,2,1,0:T(2,128)(2,1)S(1)}, bf16[2,16,1,512]{3,2,1,0:T(2,128)(2,1)S(1)}, u32[]{:S(2)}, u32[]{:S(2)}) collective-permute-start(bf16[2,16,1,512]{3,2,1,0:T(2,128)(2,1)S(1)} %get-tuple-element.270), channel_id=1, source_target_pairs={{0,1},{1,2},{2,3},{3,4},{4,5},{5,6},{6,7},{7,8},{8,9},{9,10},{10,1... | collective-permute-start | bytes 98312 | tf_op jit(solution)/shard_map/ppermute | solution.py:20
  146.9 14.5 %collective-permute-start.3 = (bf16[2,16,1,512]{3,2,1,0:T(2,128)(2,1)S(1)}, bf16[2,16,1,512]{3,2,1,0:T(2,128)(2,1)S(1)}, u32[]{:S(2)}, u32[]{:S(2)}) collective-permute-start(bf16[2,16,1,512]{3,2,1,0:T(2,128)(2,1)S(1)} %get-tuple-element.269), channel_id=1, source_target_pairs={{1,0},{2,1},{3,2},{4,3},{5,4},{6,5},{7,6},{8,7},{9,8},{10,9},{11,1... | collective-permute-start | bytes 98312 | tf_op jit(solution)/shard_map/ppermute | solution.py:22
  151.2 10.2 %collective-permute-start = (bf16[2,1,16,512]{3,2,1,0:T(8,128)(2,1)S(1)}, bf16[2,1,16,512]{3,2,1,0:T(8,128)(2,1)S(1)}, u32[]{:S(2)}, u32[]{:S(2)}) collective-permute-start(bf16[2,1,16,512]{3,2,1,0:T(8,128)(2,1)S(1)} %get-tuple-element.272), channel_id=1, source_target_pairs={{0,16},{16,32},{32,48},{48,64},{64,80},{80,96},{96,112},{1,17},{17... | collective-permute-start | bytes 98312 | tf_op jit(solution)/shard_map/ppermute | solution.py:20
  158.9 5.2 collective-permute-start.1
  161.3 5.1 copy-start.26
  161.4 5.1 copy-start.28
  161.4 5.1 copy-start.30
  161.4 5.1 copy-start.32
  161.4 5.1 copy-start.34
  164.8 2.3 copy-start.7
  164.8 2.3 copy-start.10
  164.9 2.3 copy-start.11
  164.9 2.3 copy-start.12
  164.9 2.4 copy-start.13
  166.8 0.7 copy-start.17
  325.4 1.4 copy-start.4
  325.4 2.7 copy-start.9
  328.1 8.9 %copy-start.16 = (bf16[4,256,128]{1,2,0:T(8,128)(2,1)S(1)}, bf16[4,256,128]{1,2,0:T(8,128)(2,1)}, u32[]{:S(2)}) copy-start(bf16[4,256,128]{1,2,0:T(8,128)(2,1)} %copy-done.15) | copy-start | bytes 786436
  328.1 8.9 %copy-start.23 = (bf16[1,16,16,512]{3,2,1,0:T(8,128)(2,1)S(1)}, bf16[1,16,16,512]{3,2,1,0:T(8,128)(2,1)}, u32[]{:S(2)}) copy-start(bf16[1,16,16,512]{3,2,1,0:T(8,128)(2,1)} %get-tuple-element.258) | copy-start | bytes 786436
  328.1 10.2 %copy-start.6 = (bf16[16,16,512]{2,1,0:T(8,128)(2,1)S(1)}, bf16[16,16,512]{2,1,0:T(8,128)(2,1)}, u32[]{:S(2)}) copy-start(bf16[16,16,512]{2,1,0:T(8,128)(2,1)} %param.14) | copy-start | bytes 786436
  339.6 211.6 %all-to-all-start.2 = ((bf16[16,256,512]{2,1,0:T(8,128)(2,1)}), bf16[16,256,512]{2,1,0:T(8,128)(2,1)}, u32[]{:S(2)}, u32[]{:S(2)}) async-start(bf16[16,256,512]{2,1,0:T(8,128)(2,1)} %bitcast.259), calls=%async_computation.2 | async-start | bytes 8388608 | tf_op jit(solution)/shard_map/all_to_all | solution.py:227
  346.3 199.2 %all-reduce.4.cloned.1.call-start = ((), (), s32[]{:S(2)}) async-start(), calls=%async_computation.3 | async-start | bytes 8388608 | tf_op jit(solution)/shard_map/psum | solution.py:237
  355.5 1.8 copy-start.8
  355.5 1.8 copy-start.27
  355.5 1.8 copy-start.29
  355.5 1.8 copy-start.31
  355.5 1.8 copy-start.33
  355.5 1.8 copy-start.35
  357.3 115.9 %copy-start.18 = (bf16[256,512]{1,0:T(8,128)(2,1)S(1)}, bf16[256,512]{1,0:T(8,128)(2,1)}, u32[]{:S(2)}) copy-start(bf16[256,512]{1,0:T(8,128)(2,1)} %copy-done.17) | copy-start | bytes 786436
  545.5 4.4 copy-start.22
  545.5 5.7 %copy-start.38 = (s32[16]{0:T(128)S(1)}, s32[16]{0:T(128)}, u32[]{:S(2)}) copy-start(s32[16]{0:T(128)} %copy-done.37) | copy-start | bytes 196
  551.2 7.7 %copy-start.21 = (f32[512,512]{1,0:T(8,128)S(1)}, f32[512,512]{1,0:T(8,128)}, u32[]{:S(2)}) copy-start(f32[512,512]{1,0:T(8,128)} %get-tuple-element.483) | copy-start | bytes 3145732
  551.2 8.7 %copy-start.1 = (bf16[16,128,512]{2,1,0:T(8,128)(2,1)S(1)}, bf16[16,128,512]{2,1,0:T(8,128)(2,1)}, u32[]{:S(2)}) copy-start(bf16[16,128,512]{2,1,0:T(8,128)(2,1)} %param.15) | copy-start | bytes 6291460
Sparse Core Ops, SparseCore 0:
  357.4 188.0 all-reduce.3
where the time goes:
time: 572 us; the launch traced here: 567 us
  waiting for transfers between devices  123 us (22%)
  blocking collectives  113 us (20%)
  matrix products  106 us (19%)
  other arithmetic  102 us (18%)
  local copies, waits for them, and re-layouts  63.9 us (11%)
  starting transfers between devices  37 us (6%)
  between operations  14.9 us (3%)
  loops' own time  6.11 us (1%)
    psum x1, blocking collectives, on_device(): lax.psum((grad_wquery, grad_wpair, grad_wout, tap_terms), ('lat', 'lon'))  113 us
    psum x1, waiting for transfers between devices, on_device(): lax.psum((grad_wquery, grad_wpair, grad_wout, tap_terms), ('lat', 'lon'))  69.7 us
    sub x4, other arithmetic, one_pair(): grad_weights - inner_sum  60.3 us
    all_to_all x1, waiting for transfers between devices, on_device(): lax.all_to_all(outgoing.reshape(peer_count, CAP * BLK, D), 'lon', split_a...  50.5 us
    sub x8, other arithmetic, pair_weights(): raised = jnp.exp(scores - largest)  29 us
    dynamic_slice x28, local copies, waits for them, and re-layouts, head_slices(): lax.dynamic_slice_in_dim(source, number * column_span, column_span, 1)  22 us
    dot_general x4, matrix products, one_pair(): jnp.einsum('hqk,qhd->khd', weights.astype(jnp.bfloat16), grad_pair, prefe...  20.2 us
    dot_general x4, matrix products, one_pair(): jnp.einsum('qhd,khd->hqk', grad_pair, value_pair, preferred_element_type=...  19.3 us
  transfers between devices with their start and end apart: 8, of which 4 were waited for; matrix products, arithmetic and copies ran while one was open for 5% of the time, Pallas kernels for 0%

commit v1 on v0

v1 whole, which is shorter than its diff:
```python
import functools

import jax
import jax.numpy as jnp
from jax import lax
from jax.experimental import pallas as pl
from jax.experimental.pallas import tpu as pltpu
from jax.sharding import PartitionSpec as P

D = 512
HEADS = 8
HD = D // HEADS
BLK = 128
CAP = 2
ROWS = CAP * BLK
CELLS = 256
SCALING = HD ** (-0.5)
MESH = pl.DeviceIdType.MESH
BF = jnp.bfloat16
F32 = jnp.float32


def padded(cells, sides, width, closed):
    for axis, dim in sides:
        count = lax.axis_size(axis)
        ends = count if closed else count - 1
        head = lax.slice_in_dim(cells, 0, width, axis=dim)
        tail = lax.slice_in_dim(cells, cells.shape[dim] - width, cells.shape[dim], axis=dim)
        cells = jnp.concatenate(
            [
                lax.ppermute(tail, axis, [(i, (i + 1) % count) for i in range(ends)]),
                cells,
                lax.ppermute(head, axis, [((i + 1) % count, i) for i in range(ends)]),
            ],
            axis=dim,
        )
    return cells


def dot(a, b):
    return jnp.dot(a, b, preferred_element_type=F32)


def dot_nt(a, b):
    return lax.dot_general(a, b, (((1,), (1,)), ((), ())), preferred_element_type=F32)


def attention_kernel(
    n, blk_ref, cnt_ref, slot_ref, obs_ref, grid_ref, gm_ref, wq_ref, wk_ref, wv_ref, wo_ref,
    mid_ref, gobs_ref, ggrid_ref, dwq_ref, dwkv_ref, dwo_ref,
    send, xs, ret, cnt_send, cnt_recv, kv, kt, vt, xt, bias, wkv, wkvt, qz, qzt, doz, dozt, dot_t,
    acc_o, acc_q, m_ref, l_ref, d_ref, dkv, dxo, own,
    x_ssem, x_rsem, c_ssem, c_rsem, g_ssem, g_rsem,
):
    me = lax.axis_index("lon")
    chunks = n + 1

    def peer(d):
        return {"lon": lax.rem(me + d, n)}

    barrier = pltpu.get_barrier_semaphore()

    def greet(d, carry):
        pl.semaphore_signal(barrier, inc=1, device_id=peer(d), device_id_type=MESH)
        return carry

    lax.fori_loop(1, n, greet, 0)

    row_ids = lax.broadcasted_iota(jnp.int32, (8, CELLS), 0)

    def pack(d, carry):
        s = 2 * d
        send[d, 0] = obs_ref[blk_ref[s]]
        send[d, 1] = obs_ref[blk_ref[s + 1]]
        cnt_send[d] = jnp.where(row_ids == 0, cnt_ref[s], cnt_ref[s + 1]).astype(F32)
        return carry

    lax.fori_loop(0, n, pack, 0)
    pl.semaphore_wait(barrier, n - 1)

    def x_copy(d):
        return pltpu.make_async_remote_copy(
            src_ref=send.at[d], dst_ref=xs.at[d + 1], send_sem=x_ssem.at[d], recv_sem=x_rsem.at[d],
            device_id=peer(d), device_id_type=MESH,
        )

    def c_copy(d):
        return pltpu.make_async_remote_copy(
            src_ref=cnt_send.at[d], dst_ref=cnt_recv.at[d], send_sem=c_ssem.at[d], recv_sem=c_rsem.at[d],
            device_id=peer(d), device_id_type=MESH,
        )

    def g_copy(d):
        return pltpu.make_async_remote_copy(
            src_ref=send.at[d], dst_ref=ret.at[pl.ds(CAP * d, CAP)], send_sem=g_ssem.at[d], recv_sem=g_rsem.at[d],
            device_id=peer(n - d), device_id_type=MESH,
        )

    def ship(d, carry):
        c_copy(d).start()
        x_copy(d).start()
        return carry

    lax.fori_loop(1, n, ship, 0)

    xs[0] = grid_ref[...].reshape(CAP, BLK, D)
    xs[1] = send[0]
    cnt_recv[0] = cnt_send[0]
    wkv[:, :D] = wk_ref[...]
    wkv[:, D:] = wv_ref[...]
    wkvt[:D, :] = wk_ref[...].astype(F32).T.astype(BF)
    wkvt[D:, :] = wv_ref[...].astype(F32).T.astype(BF)
    lanes = lax.broadcasted_iota(jnp.int32, (CELLS, 2 * HD), 1)
    queries = dot(grid_ref[...], wq_ref[...]).astype(BF).astype(F32) * SCALING
    ups = dot_nt(gm_ref[...], wo_ref[...]).astype(BF).astype(F32)
    dot_t[...] = ups.T
    for h in range(HEADS):
        p, e = h // 2, h % 2
        mine = (lanes >= HD) if e else (lanes < HD)
        picked = jnp.where(mine, queries[:, p * 2 * HD : (p + 1) * 2 * HD], 0.0)
        qz[h] = picked.astype(BF)
        qzt[h] = picked.T.astype(BF)
        picked = jnp.where(mine, ups[:, p * 2 * HD : (p + 1) * 2 * HD], 0.0)
        doz[h] = picked.astype(BF)
        dozt[h] = picked.T.astype(BF)
    bias[0] = jnp.zeros((ROWS, CELLS), F32)
    acc_o[...] = jnp.zeros_like(acc_o)
    acc_q[...] = jnp.zeros_like(acc_q)
    dwkv_ref[...] = jnp.zeros_like(dwkv_ref)
    m_ref[...] = jnp.full(m_ref.shape, -1e30, F32)
    l_ref[...] = jnp.zeros_like(l_ref)
    key_ids = lax.broadcasted_iota(jnp.int32, (BLK, CELLS), 0).astype(F32)

    def forward(c, carry):
        @pl.when(c >= 2)
        def _():
            c_copy(c - 1).wait_recv()
            x_copy(c - 1).wait_recv()

        @pl.when(c >= 1)
        def _():
            tile = cnt_recv[c - 1]
            bias[c, 0:BLK, :] = jnp.where(key_ids < tile[0:1, :], 0.0, -1e30)
            bias[c, BLK:ROWS, :] = jnp.where(key_ids < tile[1:2, :], 0.0, -1e30)

        for j in range(4):
            cols = slice(j * 256, (j + 1) * 256)
            part = dot(xs[c].reshape(ROWS, D), wkv[:, cols]).astype(BF)
            kv[c, :, cols] = part
            if j < 2:
                kt[c, cols, :] = part.T
            else:
                vt[j * 256 - D : (j + 1) * 256 - D, :] = part.T

        def pair(p, inner):
            keys = kv[c, :, pl.ds(pl.multiple_of(p * 128, 128), 128)]
            for e in range(2):
                h = 2 * p + e
                rows = pl.ds(pl.multiple_of(h * HD, HD), HD)
                scores = dot(keys, qzt[h]) + bias[c]
                old = m_ref[h]
                new = jnp.maximum(old, jnp.max(scores, 0, keepdims=True))
                raised = jnp.exp(scores - new)
                shrink = jnp.exp(old - new)
                l_ref[h] = l_ref[h] * shrink + jnp.sum(raised, 0, keepdims=True)
                m_ref[h] = new
                acc_o[rows, :] = acc_o[rows, :] * shrink + dot(vt[rows, :], raised.astype(BF))
            return inner

        lax.fori_loop(0, HEADS // 2, pair, 0)
        return carry

    lax.fori_loop(0, chunks, forward, 0)

    def finish(h, carry):
        rows = pl.ds(pl.multiple_of(h * HD, HD), HD)
        total = l_ref[h]
        mixed = acc_o[rows, :] / total
        acc_o[rows, :] = mixed
        m_ref[h] = m_ref[h] + jnp.log(total)
        d_ref[h] = jnp.sum(mixed * dot_t[rows, :], 0, keepdims=True)
        return carry

    lax.fori_loop(0, HEADS, finish, 0)
    attended = acc_o[...].astype(BF)
    mid_ref[...] = (
        grid_ref[...].astype(F32) + dot(acc_o[...].T.astype(BF), wo_ref[...])
    ).astype(BF)
    dwo_ref[...] = dot(attended, gm_ref[...])

    def sent(d, carry):
        c_copy(d).wait_send()
        x_copy(d).wait_send()
        return carry

    lax.fori_loop(1, n, sent, 0)

    def backward(step, carry):
        c = lax.rem(step + 2, chunks)

        def pair(p, inner):
            here = pl.ds(pl.multiple_of(p * 128, 128), 128)
            there = pl.ds(pl.multiple_of(D + p * 128, 128), 128)
            keys = kv[c, :, here]
            values = kv[c, :, there]
            grad_k = jnp.zeros((ROWS, 128), F32)
            grad_v = jnp.zeros((ROWS, 128), F32)
            for e in range(2):
                h = 2 * p + e
                rows = pl.ds(pl.multiple_of(h * HD, HD), HD)
                weights = jnp.exp(dot(keys, qzt[h]) + bias[c] - m_ref[h])
                grads = (weights * (dot(values, dozt[h]) - d_ref[h])).astype(BF)
                grad_k = grad_k + dot(grads, qz[h])
                grad_v = grad_v + dot(weights.astype(BF), doz[h])
                acc_q[rows, :] += dot(kt[c, rows, :], grads)
            dkv[:, here] = grad_k.astype(BF)
            dkv[:, there] = grad_v.astype(BF)
            return inner

        lax.fori_loop(0, HEADS // 2, pair, 0)
        xt[...] = xs[c].reshape(ROWS, D).T
        for j in range(4):
            cols = slice(j * 256, (j + 1) * 256)
            dwkv_ref[:, cols] += dot(xt[...], dkv[:, cols])
        for j in range(2):
            cols = slice(j * 256, (j + 1) * 256)
            dxo[:, cols] = dot(dkv[...], wkvt[:, cols])

        @pl.when(c == 0)
        def _():
            own[...] = dxo[...]

        @pl.when(c == 1)
        def _():
            ret[0:CAP] = dxo[...].astype(BF).reshape(CAP, BLK, D)

        @pl.when(c >= 2)
        def _():
            send[c - 1] = dxo[...].astype(BF).reshape(CAP, BLK, D)
            g_copy(c - 1).start()

        return carry

    lax.fori_loop(0, chunks, backward, 0)

    grad_q = (acc_q[...].T * SCALING).astype(BF)
    ggrid_ref[...] = (
        gm_ref[...].astype(F32) + dot_nt(grad_q, wq_ref[...]) + own[...]
    ).astype(BF)
    dwq_ref[...] = dot(grid_ref[...].T, grad_q)

    def returned(d, carry):
        g_copy(d).wait_recv()
        g_copy(d).wait_send()
        return carry

    lax.fori_loop(1, n, returned, 0)

    def unpack(b, carry):
        gobs_ref[b] = ret[slot_ref[b]]
        return carry

    lax.fori_loop(0, gobs_ref.shape[0], unpack, 0)


def attention(n, tables, obs, grid, grad_mid, weights):
    vmem = pl.BlockSpec(memory_space=pltpu.VMEM)
    smem = pl.BlockSpec(memory_space=pltpu.SMEM)
    blocks = obs.shape[0]
    dma = pltpu.SemaphoreType.DMA((n,))
    return pl.pallas_call(
        functools.partial(attention_kernel, n),
        out_shape=(
            jax.ShapeDtypeStruct((CELLS, D), BF),
            jax.ShapeDtypeStruct((blocks, BLK, D), BF),
            jax.ShapeDtypeStruct((CELLS, D), BF),
            jax.ShapeDtypeStruct((D, D), F32),
            jax.ShapeDtypeStruct((D, 2 * D), F32),
            jax.ShapeDtypeStruct((D, D), F32),
        ),
        in_specs=[smem] * 3 + [vmem] * 7,
        out_specs=(vmem,) * 6,
        scratch_shapes=[
            pltpu.VMEM((n, CAP, BLK, D), BF),
            pltpu.VMEM((n + 1, CAP, BLK, D), BF),
            pltpu.VMEM((n * CAP, BLK, D), BF),
            pltpu.VMEM((n, 8, CELLS), F32),
            pltpu.VMEM((n, 8, CELLS), F32),
            pltpu.VMEM((n + 1, ROWS, 2 * D), BF),
            pltpu.VMEM((n + 1, D, ROWS), BF),
            pltpu.VMEM((D, ROWS), BF),
            pltpu.VMEM((D, ROWS), BF),
            pltpu.VMEM((n + 1, ROWS, CELLS), F32),
            pltpu.VMEM((D, 2 * D), BF),
            pltpu.VMEM((2 * D, D), BF),
            pltpu.VMEM((HEADS, CELLS, 2 * HD), BF),
            pltpu.VMEM((HEADS, 2 * HD, CELLS), BF),
            pltpu.VMEM((HEADS, CELLS, 2 * HD), BF),
            pltpu.VMEM((HEADS, 2 * HD, CELLS), BF),
            pltpu.VMEM((D, CELLS), F32),
            pltpu.VMEM((D, CELLS), F32),
            pltpu.VMEM((D, CELLS), F32),
            pltpu.VMEM((HEADS, 1, CELLS), F32),
            pltpu.VMEM((HEADS, 1, CELLS), F32),
            pltpu.VMEM((HEADS, 1, CELLS), F32),
            pltpu.VMEM((ROWS, 2 * D), BF),
            pltpu.VMEM((ROWS, D), F32),
            pltpu.VMEM((ROWS, D), F32),
            dma, dma, dma, dma, dma, dma,
        ],
        compiler_params=pltpu.CompilerParams(
            collective_id=0, has_side_effects=True, vmem_limit_bytes=60 * 2**20
        ),
        name="attention",
    )(*tables, obs, grid, grad_mid, *weights)


def sum_kernel(
    nlat, nlon, dwq_ref, dwkv_ref, dwo_ref, taps_ref, wq_out, wk_out, wv_out, wo_out, taps_out,
    a0, b0, a1, b1, a2, b2, a3, b3, a4, b4, t0, t1,
    a1s, a1r, b1s, b1r, a2s, a2r, b2s, b2r, a3s, a3r, b3s, b3r, a4s, a4r, b4s, b4r,
    t1s, t1r, t2s, t2r,
):
    sizes = {"lat": nlat, "lon": nlon}
    place = {axis: lax.axis_index(axis) for axis in sizes}
    barrier = pltpu.get_barrier_semaphore()

    def every(axis, body):
        count, me = sizes[axis], place[axis]

        def step(o, carry):
            body(lax.rem(me + o, count))
            return carry

        lax.fori_loop(1, count, step, 0)

    for axis in sizes:
        every(axis, lambda at, axis=axis: pl.semaphore_signal(
            barrier, inc=1, device_id={axis: at}, device_id_type=MESH))

    def piece(j):
        rows = pl.ds(pl.multiple_of((j // 2) * 16, 16), 16)
        cols = pl.ds(pl.multiple_of(lax.rem(j, 2) * 256, 256), 256)
        return rows, cols

    def cut(j, carry):
        rows, cols = piece(j)
        right = pl.ds(pl.multiple_of(D + lax.rem(j, 2) * 256, 256), 256)
        low, high = j, j + 64
        a0[low // nlon, lax.rem(low, nlon)] = dwq_ref[rows, cols].astype(BF)
        a0[high // nlon, lax.rem(high, nlon)] = dwkv_ref[rows, cols].astype(BF)
        b0[low // nlat, lax.rem(low, nlat)] = dwkv_ref[rows, right].astype(BF)
        b0[high // nlat, lax.rem(high, nlat)] = dwo_ref[rows, cols].astype(BF)
        return carry

    lax.fori_loop(0, 64, cut, 0)
    t0[place["lat"]] = taps_ref[...]
    pl.semaphore_wait(barrier, nlat + nlon - 2)

    def scatter(axis, src, dst, ssem, rsem):
        me = place[axis]

        def copy(to, frm):
            return pltpu.make_async_remote_copy(
                src_ref=src.at[to], dst_ref=dst.at[frm], send_sem=ssem.at[to], recv_sem=rsem.at[frm],
                device_id={axis: to}, device_id_type=MESH,
            )

        return (
            lambda: every(axis, lambda at: copy(at, me).start()),
            lambda: every(axis, lambda at: copy(at, at).wait_recv()),
            lambda: every(axis, lambda at: copy(at, me).wait_send()),
        )

    def gather(axis, buf, ssem, rsem):
        me = place[axis]

        def copy(to, frm):
            return pltpu.make_async_remote_copy(
                src_ref=buf.at[me], dst_ref=buf.at[frm], send_sem=ssem.at[to], recv_sem=rsem.at[frm],
                device_id={axis: to}, device_id_type=MESH,
            )

        return (
            lambda: every(axis, lambda at: copy(at, me).start()),
            lambda: every(axis, lambda at: copy(at, at).wait_recv()),
            lambda: every(axis, lambda at: copy(at, me).wait_send()),
        )

    def total(axis, src, dst):
        value = src[place[axis]].astype(F32)
        count, me = sizes[axis], place[axis]
        return lax.fori_loop(
            1, count, lambda o, held: held + dst[lax.rem(me + o, count)].astype(F32), value
        )

    sa1 = scatter("lat", a0, a1, a1s, a1r)
    sb1 = scatter("lon", b0, b1, b1s, b1r)
    gt1 = gather("lat", t0, t1s, t1r)
    gt1[0]()
    sa1[0]()
    sb1[0]()
    gt1[1]()
    summed = t0[0]
    for i in range(1, nlat):
        summed = summed + t0[i]
    t1[place["lon"]] = summed
    gt2 = gather("lon", t1, t2s, t2r)
    gt2[0]()

    sa1[1]()
    sa2 = scatter("lon", a2, a3, a2s, a2r)

    def add_a(k, carry):
        held = a0[place["lat"], k].astype(F32)
        for o in range(1, nlat):
            held = held + a1[lax.rem(place["lat"] + o, nlat), k].astype(F32)
        a2[k] = held.astype(BF)
        return carry

    lax.fori_loop(0, nlon, add_a, 0)
    sa2[0]()
    sb1[1]()
    sb2 = scatter("lat", b2, b3, b2s, b2r)

    def add_b(k, carry):
        held = b0[place["lon"], k].astype(F32)
        for o in range(1, nlon):
            held = held + b1[lax.rem(place["lon"] + o, nlon), k].astype(F32)
        b2[k] = held.astype(BF)
        return carry

    lax.fori_loop(0, nlat, add_b, 0)
    sb2[0]()
    sa2[1]()
    la, lo = place["lat"], place["lon"]
    a4[la, lo] = total("lon", a2, a3).astype(BF)
    ga3 = gather("lon", a4.at[la], a3s, a3r)
    ga3[0]()
    sb2[1]()
    b4[lo, la] = total("lat", b2, b3).astype(BF)
    gb3 = gather("lat", b4.at[lo], b3s, b3r)
    gb3[0]()
    ga3[1]()
    ga4 = gather("lat", a4, a4s, a4r)
    ga4[0]()
    gb3[1]()
    gb4 = gather("lon", b4, b4s, b4r)
    gb4[0]()
    gt2[1]()
    summed = t1[0]
    for i in range(1, nlon):
        summed = summed + t1[i]
    taps_out[...] = summed
    ga4[1]()

    def join_a(j, carry):
        rows, cols = piece(j)
        low, high = j, j + 64
        wq_out[rows, cols] = a4[low // nlon, lax.rem(low, nlon)].astype(F32)
        wk_out[rows, cols] = a4[high // nlon, lax.rem(high, nlon)].astype(F32)
        return carry

    lax.fori_loop(0, 64, join_a, 0)
    gb4[1]()

    def join_b(j, carry):
        rows, cols = piece(j)
        low, high = j, j + 64
        wv_out[rows, cols] = b4[low // nlat, lax.rem(low, nlat)].astype(F32)
        wo_out[rows, cols] = b4[high // nlat, lax.rem(high, nlat)].astype(F32)
        return carry

    lax.fori_loop(0, 64, join_b, 0)
    for done in (gt1, sa1, sb1, gt2, sa2, sb2, ga3, gb3, ga4, gb4):
        done[2]()


def sum_gradients(nlat, nlon, dwq, dwkv, dwo, taps):
    vmem = pl.BlockSpec(memory_space=pltpu.VMEM)
    matrix = jax.ShapeDtypeStruct((D, D), F32)
    lat, lon = pltpu.SemaphoreType.DMA((nlat,)), pltpu.SemaphoreType.DMA((nlon,))

    def buf(*lead):
        return pltpu.VMEM((*lead, 16, 256), BF)

    return pl.pallas_call(
        functools.partial(sum_kernel, nlat, nlon),
        out_shape=(matrix, matrix, matrix, matrix, jax.ShapeDtypeStruct(taps.shape, F32)),
        in_specs=[vmem] * 4,
        out_specs=(vmem,) * 5,
        scratch_shapes=[
            buf(nlat, nlon), buf(nlon, nlat), buf(nlat, nlon), buf(nlon, nlat),
            buf(nlon), buf(nlat), buf(nlon), buf(nlat), buf(nlat, nlon), buf(nlon, nlat),
            pltpu.VMEM((nlat, *taps.shape), F32), pltpu.VMEM((nlon, *taps.shape), F32),
            lat, lat, lon, lon, lon, lon, lat, lat, lon, lon, lat, lat, lat, lat, lon, lon,
            lat, lat, lon, lon,
        ],
        compiler_params=pltpu.CompilerParams(
            collective_id=1, has_side_effects=True, vmem_limit_bytes=40 * 2**20
        ),
        name="sum_gradients",
    )(dwq, dwkv, dwo, taps)


def on_device(
    grid_tokens, obs_tokens, destinations, valid_counts, w_query, w_key, w_value, w_out,
    stencil_taps, cotangent,
):
    tile_rows, tile_columns = (grid_tokens.shape[0], grid_tokens.shape[1])
    cell_count = tile_rows * tile_columns
    block_count = obs_tokens.shape[0]
    nlat, nlon = lax.axis_size("lat"), lax.axis_size("lon")
    flat_grid = grid_tokens.reshape(cell_count, D)
    target = lax.rem(destinations[:, 0] - lax.axis_index("lon") + nlon, nlon)
    order_ids = jnp.arange(block_count, dtype=jnp.int32)
    earlier = (target[:, None] == target[None, :]) & (order_ids[None, :] < order_ids[:, None])
    slot_ids = target * CAP + jnp.sum(earlier.astype(jnp.int32), 1)
    chooser = slot_ids[None, :] == jnp.arange(nlon * CAP, dtype=jnp.int32)[:, None]
    block_ids = jnp.sum(jnp.where(chooser, order_ids[None, :], 0), 1)
    counts = jnp.sum(jnp.where(chooser, valid_counts[0][None, :], 0), 1)

    taps = stencil_taps[:, None, None, :]
    lat_ext = padded(cotangent, (("lat", 0),), 1, False).astype(F32)
    lon_ext = padded(cotangent, (("lon", 1),), 1, True).astype(F32)
    up = cotangent.astype(F32)
    up_north, up_south, up_west, up_east = lat_ext[:-2], lat_ext[2:], lon_ext[:, :-2], lon_ext[:, 2:]
    grad_middle = (
        (1.0 + taps[0]) * up + taps[1] * up_south + taps[2] * up_north
        + taps[3] * up_east + taps[4] * up_west
    ).astype(BF)

    middle, grad_obs, grad_grid, dwq, dwkv, dwo = attention(
        nlon, (block_ids, counts, slot_ids), obs_tokens, flat_grid,
        grad_middle.reshape(cell_count, D), (w_query, w_key, w_value, w_out),
    )
    middle = middle.reshape(tile_rows, tile_columns, D)
    centre = middle.astype(F32)
    terms = [jnp.sum(centre * side, (0, 1)) for side in (up, up_south, up_north, up_east, up_west)]
    terms = jnp.concatenate([jnp.stack(terms), jnp.zeros((3, D), F32)])
    lat_mid = padded(middle, (("lat", 0),), 1, False).astype(F32)
    lon_mid = padded(middle, (("lon", 1),), 1, True).astype(F32)
    sums = sum_gradients(nlat, nlon, dwq, dwkv, dwo, terms)
    encoded = (
        (1.0 + taps[0]) * centre + taps[1] * lat_mid[:-2] + taps[2] * lat_mid[2:]
        + taps[3] * lon_mid[:, :-2] + taps[4] * lon_mid[:, 2:]
    ).astype(BF)
    return (
        encoded, grad_grid.reshape(tile_rows, tile_columns, D), grad_obs,
        *sums[:4], sums[4][:5],
    )


def solution(mesh):
    in_specs = (
        P("lat", "lon", None),
        P(("lat", "lon"), None, None),
        P(("lat", "lon"), None),
        P(("lat", "lon"), None),
        P(),
        P(),
        P(),
        P(),
        P(),
        P("lat", "lon", None),
    )
    out_specs = (
        P("lat", "lon", None),
        P("lat", "lon", None),
        P(("lat", "lon"), None, None),
        P(),
        P(),
        P(),
        P(),
        P(),
    )
    return jax.shard_map(
        on_device, mesh=mesh, in_specs=in_specs, out_specs=out_specs, check_vma=False
    )
```

time: 572 us -> 306 us (0.53)
  Pallas kernels: 0 us -> 256 us
  waiting for transfers between devices: 123 us -> 0.02 us
  blocking collectives: 113 us -> 0 us
  matrix products: 106 us -> 0 us
  other arithmetic: 102 us -> 11.1 us
  local copies, waits for them, and re-layouts: 63.9 us -> 14.1 us
  between operations: 14.9 us -> 0.86 us
  starting transfers between devices: 37 us -> 23.6 us
  loops' own time: 6.11 us -> 0 us
    pallas_call x0 -> x2, Pallas kernels: none -> 256 us  [the longest x1 194 us: attention(): pl.pallas_call(functools.partial(attention_kernel, n), out_shape=(jax.Sha...]
    psum x1 -> x0, blocking collectives: 113 us -> none  [on_device(): lax.psum((grad_wquery, grad_wpair, grad_wout, tap_terms), ('lat', 'lon'))]
    dot_general x42 -> x0, matrix products: 106 us -> none  [the longest x4 20.2 us: one_pair(): jnp.einsum('hqk,qhd->khd', weights.astype(jnp.bfloat16), grad_pair, prefe...]
    sub x12 -> x0, other arithmetic: 89.3 us -> none  [the longest x4 60.3 us: one_pair(): grad_weights - inner_sum]
    psum x1 -> x0, waiting for transfers between devices: 69.7 us -> none  [on_device(): lax.psum((grad_wquery, grad_wpair, grad_wout, tap_terms), ('lat', 'lon'))]
    all_to_all x3 -> x0, waiting for transfers between devices: 50.9 us -> none  [the longest x1 50.5 us: on_device(): lax.all_to_all(outgoing.reshape(peer_count, CAP * BLK, D), 'lon', split_a...]
    dynamic_slice x36 -> x0, local copies, waits for them, and re-layouts: 27.1 us -> none  [the longest x28 22 us: head_slices(): lax.dynamic_slice_in_dim(source, number * column_span, column_span, 1)]
    all_to_all x3 -> x0, starting transfers between devices: 22 us -> none  [the longest x1 8.6 us: on_device(): lax.all_to_all(sent_counts, 'lon', split_axis=0, concat_axis=0, tiled=True)]
  transfers between devices with their start and end apart: 8 -> 8, of which waited for: 4 -> 0; matrix products, arithmetic and copies ran while one was open for 5% -> 4% of each run, Pallas kernels for 0% -> 20%
where the time goes in v1:
time: 306 us
  Pallas kernels  256 us (84%)
  starting transfers between devices  23.6 us (8%)
  local copies, waits for them, and re-layouts  14.1 us (5%)
  other arithmetic  11.1 us (4%)
    pallas_call x1, Pallas kernels, attention(): pl.pallas_call(functools.partial(attention_kernel, n), out_shape=(jax.Sha...  194 us
    pallas_call x1, Pallas kernels, sum_gradients(): pl.pallas_call(functools.partial(sum_kernel, nlat, nlon), out_shape=(matr...  61.5 us
    ppermute x4, starting transfers between devices, padded(): lax.ppermute(head, axis, [((i + 1) % count, i) for i in range(ends)])  13.3 us
    ppermute x4, starting transfers between devices, padded(): lax.ppermute(tail, axis, [(i, (i + 1) % count) for i in range(ends)])  10.3 us
    unnamed x29, local copies, waits for them, and re-layouts  8.99 us
  transfers between devices with their start and end apart: 8, of which 0 were waited for; matrix products, arithmetic and copies ran while one was open for 4% of the time, Pallas kernels for 20%

profile of v1, /device:TPU:1, one launch (start us, length us, event | category | flops | bytes accessed | tf_op | source)
XLA Modules:
  0.0 305.6 jit_solution(6361240701126902937)
XLA Ops:
  0.6 0.0 copy-start.3
  0.6 0.8 fusion.20
  1.4 4.5 %collective-permute-start = (bf16[1,16,512]{2,1,0:T(8,128)(2,1)S(1)}, bf16[1,16,512]{2,1,0:T(8,128)(2,1)S(1)}, u32[]{:S(2)}, u32[]{:S(2)}) collective-permute-start(bf16[1,16,512]{2,1,0:T(8,128)(2,1)S(1)} %get-tuple-element.43), channel_id=1, source_target_pairs={{0,16},{16,32},{32,48},{48,64},{64,80},{80,96},{96,112},{1,17},{17... | collective-permute-start | bytes 49160 | tf_op jit(solution)/shard_map/ppermute | solution.py:31
  5.9 1.9 collective-permute-start.1
  7.9 1.0 fusion.21
  8.9 1.7 collective-permute-start.2
  10.6 4.7 %collective-permute-start.3 = (bf16[16,1,512]{2,1,0:T(2,128)(2,1)S(1)}, bf16[16,1,512]{2,1,0:T(2,128)(2,1)S(1)}, u32[]{:S(2)}, u32[]{:S(2)}) collective-permute-start(bf16[16,1,512]{2,1,0:T(2,128)(2,1)S(1)} %get-tuple-element.46), channel_id=1, source_target_pairs={{1,0},{2,1},{3,2},{4,3},{5,4},{6,5},{7,6},{8,7},{9,8},{10,9},{11,1... | collective-permute-start | bytes 49160 | tf_op jit(solution)/shard_map/ppermute | solution.py:33
  15.3 0.7 fusion.18
  15.9 0.7 compare_select_fusion.2
  16.6 0.2 convert_reduce_fusion
  16.8 0.7 multiply_add_fusion.slot_ref
  17.4 0.0 copy-start.10
  17.4 0.9 slice_add_fusion
  18.3 0.0 copy-start.8
  18.4 1.3 select_reduce_fusion
  19.6 0.0 collective-permute-done
  19.6 0.0 collective-permute-done.1
  19.6 1.0 maximum_convert_fusion.2
  20.6 0.0 collective-permute-done.2
  20.6 0.0 collective-permute-done.3
  20.7 1.1 maximum_convert_fusion
  21.8 0.0 copy-done.3
  21.8 0.9 fusion.4
  22.7 0.0 copy-done.10
  22.7 0.0 copy-done.8
  22.7 0.0 copy-start.4
  22.7 194.5 %attention.1 = (bf16[256,512]{1,0:T(8,128)(2,1)}, bf16[16,128,512]{2,1,0:T(8,128)(2,1)}, bf16[256,512]{1,0:T(8,128)(2,1)}, f32[512,512]{1,0:T(8,128)}, f32[512,1024]{1,0:T(8,128)}, /*index=5*/f32[512,512]{1,0:T(8,128)}) custom-call(s32[32]{0:T(128)} %get-tuple-element.38.blk_ref, s32[32]{0:T(128)} %get-tuple-element.37.cnt_ref, s32[16]{0:T(128)} %copy-done.10, ...), custom_call_target="tpu_custom_call" | custom-call | tf_op jit(solution)/shard_map/attention/pallas_call | solution.py:271
  217.2 0.0 copy-start
  217.2 1.5 slice_bitcast_fusion.1
  218.7 4.1 %collective-permute-start.4 = (bf16[1,16,512]{2,1,0:T(8,128)(2,1)}, bf16[1,16,512]{2,1,0:T(8,128)(2,1)}, u32[]{:S(2)}, u32[]{:S(2)}) collective-permute-start(bf16[1,16,512]{2,1,0:T(8,128)(2,1)} %get-tuple-element.39), channel_id=1, source_target_pairs={{0,16},{16,32},{32,48},{48,64},{64,80},{80,96},{96,112},{1,17},{17... | collective-permute-start | bytes 49160 | tf_op jit(solution)/shard_map/ppermute | solution.py:31
  222.8 1.9 collective-permute-start.5
  224.7 1.0 fusion.19
  225.8 0.0 copy-done.4
  225.8 1.8 fusion.14
  227.6 0.0 collective-permute-start.6
  227.6 4.8 %collective-permute-start.7 = (bf16[16,1,512]{2,1,0:T(2,128)(2,1)S(1)}, bf16[16,1,512]{2,1,0:T(2,128)(2,1)S(1)}, u32[]{:S(2)}, u32[]{:S(2)}) collective-permute-start(bf16[16,1,512]{2,1,0:T(2,128)(2,1)S(1)} %get-tuple-element.42), channel_id=1, source_target_pairs={{1,0},{2,1},{3,2},{4,3},{5,4},{6,5},{7,6},{8,7},{9,8},{10,9},{11,1... | collective-permute-start | bytes 49160 | tf_op jit(solution)/shard_map/ppermute | solution.py:33
  232.4 0.8 concatenate.19.taps_ref
  233.2 0.0 copy-done
  233.2 0.0 copy-start.1
  233.2 1.2 copy-done.1
  234.4 0.0 copy-start.2
  234.4 1.2 copy-done.2
  235.6 0.0 copy-start.5
  235.6 61.5 %sum_gradients.1 = (f32[512,512]{1,0:T(8,128)S(1)}, f32[512,512]{1,0:T(8,128)S(1)}, f32[512,512]{1,0:T(8,128)S(1)}, f32[512,512]{1,0:T(8,128)S(1)}, f32[8,512]{1,0:T(8,128)S(1)}) custom-call(f32[512,512]{1,0:T(8,128)S(1)} %copy-done.1, f32[512,1024]{1,0:T(8,128)S(1)} %copy-done, f32[512,512]{1,0:T(8,128)S(1)} %copy-done.2, f32[8,512]{1,0:T(8,128)S(1)} %concatenate.19.taps_ref), custom_call_target="tpu_custom_call" | custom-call | tf_op jit(solution)/shard_map/sum_gradients/pallas_call | solution.py:487
  297.1 0.0 copy-start.7
  297.1 0.0 collective-permute-done.4
  297.1 0.0 collective-permute-done.5
  297.1 0.0 copy-done.5
  297.2 0.8 maximum_convert_fusion.3
  298.0 0.0 copy-start.6
  298.0 0.0 collective-permute-done.6
  298.0 0.0 collective-permute-done.7
  298.0 0.1 maximum_convert_fusion.1
  298.2 0.0 copy-done.9
  298.2 0.9 fusion.9
  299.1 0.0 copy-done.7
  299.1 0.7 copy.25
  299.8 0.0 copy-done.6
  299.8 1.3 copy.26
  301.1 1.0 copy.27
  302.1 1.0 copy.28
  303.1 1.0 copy.29
  304.1 1.0 copy.30
  305.0 0.6 copy.31
  (2 shorter events, 0.0 us)
Async XLA Ops:
  0.6 21.1 %copy-start.3 = (bf16[16,16,512]{2,1,0:T(8,128)(2,1)S(1)}, bf16[16,16,512]{2,1,0:T(8,128)(2,1)}, u32[]{:S(2)}) copy-start(bf16[16,16,512]{2,1,0:T(8,128)(2,1)} %param.19) | copy-start | bytes 786436
  1.4 18.2 %collective-permute-start = (bf16[1,16,512]{2,1,0:T(8,128)(2,1)S(1)}, bf16[1,16,512]{2,1,0:T(8,128)(2,1)S(1)}, u32[]{:S(2)}, u32[]{:S(2)}) collective-permute-start(bf16[1,16,512]{2,1,0:T(8,128)(2,1)S(1)} %get-tuple-element.43), channel_id=1, source_target_pairs={{0,16},{16,32},{32,48},{48,64},{64,80},{80,96},{96,112},{1,17},{17... | collective-permute-start | bytes 49160 | tf_op jit(solution)/shard_map/ppermute | solution.py:31
  5.9 13.7 %collective-permute-start.1 = (bf16[1,16,512]{2,1,0:T(8,128)(2,1)S(1)}, bf16[1,16,512]{2,1,0:T(8,128)(2,1)S(1)}, u32[]{:S(2)}, u32[]{:S(2)}) collective-permute-start(bf16[1,16,512]{2,1,0:T(8,128)(2,1)S(1)} %get-tuple-element.44), channel_id=1, source_target_pairs={{16,0},{32,16},{48,32},{64,48},{80,64},{96,80},{112,96},{17,1},{33... | collective-permute-start | bytes 49160 | tf_op jit(solution)/shard_map/ppermute | solution.py:33
  8.9 11.7 %collective-permute-start.2 = (bf16[16,1,512]{2,1,0:T(2,128)(2,1)S(1)}, bf16[16,1,512]{2,1,0:T(2,128)(2,1)S(1)}, u32[]{:S(2)}, u32[]{:S(2)}) collective-permute-start(bf16[16,1,512]{2,1,0:T(2,128)(2,1)S(1)} %get-tuple-element.45), channel_id=1, source_target_pairs={{0,1},{1,2},{2,3},{3,4},{4,5},{5,6},{6,7},{7,8},{8,9},{9,10},{10,1... | collective-permute-start | bytes 49160 | tf_op jit(solution)/shard_map/ppermute | solution.py:31
  10.6 10.0 %collective-permute-start.3 = (bf16[16,1,512]{2,1,0:T(2,128)(2,1)S(1)}, bf16[16,1,512]{2,1,0:T(2,128)(2,1)S(1)}, u32[]{:S(2)}, u32[]{:S(2)}) collective-permute-start(bf16[16,1,512]{2,1,0:T(2,128)(2,1)S(1)} %get-tuple-element.46), channel_id=1, source_target_pairs={{1,0},{2,1},{3,2},{4,3},{5,4},{6,5},{7,6},{8,7},{9,8},{10,9},{11,1... | collective-permute-start | bytes 49160 | tf_op jit(solution)/shard_map/ppermute | solution.py:33
  17.4 5.3 %copy-start.10 = (s32[16]{0:T(128)}, s32[16]{0:T(128)S(1)}, u32[]{:S(2)}) copy-start(s32[16]{0:T(128)S(1)} %multiply_add_fusion.slot_ref) | copy-start | bytes 196
  18.3 4.4 %copy-start.8 = (f32[1,512]{1,0:T(1,128)}, f32[1,512]{1,0:T(1,128)S(1)}, u32[]{:S(2)}) copy-start(f32[1,512]{1,0:T(1,128)S(1)} %get-tuple-element.51) | copy-start | bytes 6148
  22.7 203.1 %copy-start.4 = (bf16[16,16,512]{2,1,0:T(8,128)(2,1)S(1)}, bf16[16,16,512]{2,1,0:T(8,128)(2,1)}, u32[]{:S(2)}) copy-start(bf16[16,16,512]{2,1,0:T(8,128)(2,1)} %param.19) | copy-start | bytes 786436
  217.2 16.0 %copy-start = (f32[512,1024]{1,0:T(8,128)S(1)}, f32[512,1024]{1,0:T(8,128)}, u32[]{:S(2)}) copy-start(f32[512,1024]{1,0:T(8,128)} %get-tuple-element.23.dwkv_ref) | copy-start | bytes 6291460
  218.7 78.4 %collective-permute-start.4 = (bf16[1,16,512]{2,1,0:T(8,128)(2,1)}, bf16[1,16,512]{2,1,0:T(8,128)(2,1)}, u32[]{:S(2)}, u32[]{:S(2)}) collective-permute-start(bf16[1,16,512]{2,1,0:T(8,128)(2,1)} %get-tuple-element.39), channel_id=1, source_target_pairs={{0,16},{16,32},{32,48},{48,64},{64,80},{80,96},{96,112},{1,17},{17... | collective-permute-start | bytes 49160 | tf_op jit(solution)/shard_map/ppermute | solution.py:31
  222.8 74.3 %collective-permute-start.5 = (bf16[1,16,512]{2,1,0:T(8,128)(2,1)}, bf16[1,16,512]{2,1,0:T(8,128)(2,1)}, u32[]{:S(2)}, u32[]{:S(2)}) collective-permute-start(bf16[1,16,512]{2,1,0:T(8,128)(2,1)} %get-tuple-element.40), channel_id=1, source_target_pairs={{16,0},{32,16},{48,32},{64,48},{80,64},{96,80},{112,96},{17,1},{33... | collective-permute-start | bytes 49160 | tf_op jit(solution)/shard_map/ppermute | solution.py:33
  227.6 70.4 %collective-permute-start.6 = (bf16[16,1,512]{2,1,0:T(2,128)(2,1)S(1)}, bf16[16,1,512]{2,1,0:T(2,128)(2,1)S(1)}, u32[]{:S(2)}, u32[]{:S(2)}) collective-permute-start(bf16[16,1,512]{2,1,0:T(2,128)(2,1)S(1)} %get-tuple-element.41), channel_id=1, source_target_pairs={{0,1},{1,2},{2,3},{3,4},{4,5},{5,6},{6,7},{7,8},{8,9},{9,10},{10,1... | collective-permute-start | bytes 49160 | tf_op jit(solution)/shard_map/ppermute | solution.py:31
  227.6 70.4 %collective-permute-start.7 = (bf16[16,1,512]{2,1,0:T(2,128)(2,1)S(1)}, bf16[16,1,512]{2,1,0:T(2,128)(2,1)S(1)}, u32[]{:S(2)}, u32[]{:S(2)}) collective-permute-start(bf16[16,1,512]{2,1,0:T(2,128)(2,1)S(1)} %get-tuple-element.42), channel_id=1, source_target_pairs={{1,0},{2,1},{3,2},{4,3},{5,4},{6,5},{7,6},{8,7},{9,8},{10,9},{11,1... | collective-permute-start | bytes 49160 | tf_op jit(solution)/shard_map/ppermute | solution.py:33
  233.2 1.2 copy-start.1
  234.4 1.2 copy-start.2
  235.6 61.5 %copy-start.5 = (bf16[256,512]{1,0:T(8,128)(2,1)S(1)}, bf16[256,512]{1,0:T(8,128)(2,1)}, u32[]{:S(2)}) copy-start(bf16[256,512]{1,0:T(8,128)(2,1)} %get-tuple-element.19) | copy-start | bytes 786436
  235.6 62.6 %copy-start.9 = (f32[1,512]{1,0:T(1,128)S(1)}, f32[1,512]{1,0:T(1,128)}, u32[]{:S(2)}) copy-start(f32[1,512]{1,0:T(1,128)} %copy-done.8) | copy-start | bytes 6148
  297.1 2.0 copy-start.7
  298.0 1.8 copy-start.6

commit v2 on v1

v2 whole, which is shorter than its diff:
```python
import functools

import jax
import jax.numpy as jnp
from jax import lax
from jax.experimental import pallas as pl
from jax.experimental.pallas import tpu as pltpu
from jax.sharding import PartitionSpec as P

D = 512
HEADS = 8
HD = D // HEADS
BLK = 128
CAP = 2
ROWS = CAP * BLK
CELLS = 256
TILE = 16
SCALING = HD ** (-0.5)
MESH = pl.DeviceIdType.MESH
BF = jnp.bfloat16
F32 = jnp.float32


def dot(a, b):
    return jnp.dot(a, b, preferred_element_type=F32)


def dot_nt(a, b):
    return lax.dot_general(a, b, (((1,), (1,)), ((), ())), preferred_element_type=F32)


def onehot(rows, cols, hit):
    at = [lax.broadcasted_iota(jnp.int32, (rows, cols), k) for k in range(2)]
    return jnp.where(hit(*at), 1.0, 0.0).astype(BF)


def around(cells, halo, first, last):
    top = jnp.where(first, 0.0, halo[0].astype(F32)).astype(BF)
    bottom = jnp.where(last, 0.0, halo[1].astype(F32)).astype(BF)
    side = TILE
    west = dot(onehot(CELLS, CELLS, lambda q, k: (k == q - 1) & (lax.rem(q, side) != 0)), cells)
    west = west + dot(onehot(CELLS, side, lambda q, k: q == k * side), halo[2])
    east = dot(onehot(CELLS, CELLS, lambda q, k: (k == q + 1) & (lax.rem(q, side) != side - 1)), cells)
    east = east + dot(onehot(CELLS, side, lambda q, k: q == k * side + side - 1), halo[3])
    return (
        jnp.concatenate([top, cells[:-side]], 0).astype(F32),
        jnp.concatenate([cells[side:], bottom], 0).astype(F32),
        west,
        east,
    )


def edges(cells, out):
    out[0] = cells[CELLS - TILE :]
    out[1] = cells[:TILE]
    out[2] = dot(onehot(TILE, CELLS, lambda k, q: q == k * TILE + TILE - 1), cells).astype(BF)
    out[3] = dot(onehot(TILE, CELLS, lambda k, q: q == k * TILE), cells).astype(BF)


class Exchange:
    def __init__(self, axis, count, copy):
        self.axis, self.count, self.copy = axis, count, copy
        self.me = lax.axis_index(axis)

    def each(self, body):
        def step(o, carry):
            body(lax.rem(self.me + o, self.count))
            return carry

        lax.fori_loop(1, self.count, step, 0)

    def start(self):
        self.each(lambda at: self.copy(at, self.me).start())

    def wait(self):
        self.each(lambda at: self.copy(at, at).wait_recv())

    def sent(self):
        self.each(lambda at: self.copy(at, self.me).wait_send())


def scatter(axis, count, src, dst, ssem, rsem):
    return Exchange(axis, count, lambda to, frm: pltpu.make_async_remote_copy(
        src_ref=src.at[to], dst_ref=dst.at[frm], send_sem=ssem.at[to], recv_sem=rsem.at[frm],
        device_id={axis: to}, device_id_type=MESH))


def gather(axis, count, buf, ssem, rsem):
    me = lax.axis_index(axis)
    return Exchange(axis, count, lambda to, frm: pltpu.make_async_remote_copy(
        src_ref=buf.at[me], dst_ref=buf.at[frm], send_sem=ssem.at[to], recv_sem=rsem.at[frm],
        device_id={axis: to}, device_id_type=MESH))


class MatrixSum:
    def __init__(self, sizes, first, second, scratch, out):
        self.nf, self.ns = sizes[first], sizes[second]
        self.mf, self.ms = lax.axis_index(first), lax.axis_index(second)
        self.whole, self.got, self.part, self.got2 = scratch[:4]
        self.out = out
        s1, r1, s2, r2, s3, r3, s4, r4 = scratch[4:]
        self.first = scatter(first, self.nf, self.whole, self.got, s1, r1)
        self.second = scatter(second, self.ns, self.part, self.got2, s2, r2)
        self.third = gather(second, self.ns, out.at[self.mf], s3, r3)
        self.fourth = gather(first, self.nf, out, s4, r4)

    def begin(self, source):
        span = self.ns * 16
        per = D // span
        for f in range(self.nf):
            rows = slice((f % per) * span, (f % per + 1) * span)
            cols = slice((f // per) * 128, (f // per + 1) * 128)
            self.whole[f] = source(rows, cols).astype(BF).reshape(self.ns, 16, 128)
        self.first.start()

    def step2(self):
        self.first.wait()
        held = self.whole[self.mf].astype(F32)
        for o in range(1, self.nf):
            held = held + self.got[lax.rem(self.mf + o, self.nf)].astype(F32)
        self.part[...] = held.astype(BF)
        self.second.start()

    def step3(self):
        self.second.wait()
        held = self.part[self.ms].astype(F32)
        for o in range(1, self.ns):
            held = held + self.got2[lax.rem(self.ms + o, self.ns)].astype(F32)
        self.out[self.mf, self.ms] = held.astype(BF)
        self.third.start()

    def step4(self):
        self.third.wait()
        self.fourth.start()

    def step5(self):
        self.fourth.wait()

    def close(self):
        for part in (self.first, self.second, self.third, self.fourth):
            part.sent()


def kernel(
    nlat, n, dest_ref, count_ref, obs_ref, grid_ref, cot_ref, wq_ref, wk_ref, wv_ref, wo_ref, sten_ref,
    enc_ref, gobs_ref, ggrid_ref, sq_ref, sk_ref, sv_ref, so_ref, taps_ref,
    send, xs, ret, cnt_send, cnt_recv, kv, kt, vt, xt, bias, wkv, wkvt, qz, qzt, doz, dozt, dot_t,
    acc_o, acc_q, m_ref, l_ref, d_ref, dkv, dwkv, gm_ref, mid_ref, sides, edge, halo, t0, t1,
    x_ssem, x_rsem, c_ssem, c_rsem, g_ssem, g_rsem, h_ssem, h_rsem, t1s, t1r, t2s, t2r,
    *sum_scratch,
):
    sizes = {"lat": nlat, "lon": n}
    lat, me = lax.axis_index("lat"), lax.axis_index("lon")
    groups = n // 2
    blocks = obs_ref.shape[0]
    sum_q, sum_k, sum_v, sum_o = (
        MatrixSum(sizes, *axes, sum_scratch[12 * i : 12 * (i + 1)], out)
        for i, (axes, out) in enumerate((
            (("lat", "lon"), sq_ref), (("lon", "lat"), sk_ref), (("lat", "lon"), sv_ref),
            (("lat", "lon"), so_ref)))
    )
    tap1 = gather("lat", nlat, t0, t1s, t1r)
    tap2 = gather("lon", n, t1, t2s, t2r)

    def peer(d):
        return {"lon": lax.rem(me + d, n)}

    barrier = pltpu.get_barrier_semaphore()
    for whom in (tap1, tap2):
        whom.each(lambda at, axis=whom.axis: pl.semaphore_signal(
            barrier, inc=1, device_id={axis: at}, device_id_type=MESH))

    row_ids = lax.broadcasted_iota(jnp.int32, (8, CELLS), 0)

    def pack(d, carry):
        tile = lax.rem(me + d, n)

        def look(b, found):
            number, b0, b1, c0, c1 = found
            hit = dest_ref[b, 0] == tile
            one, two = hit & (number == 0), hit & (number == 1)
            return (
                number + hit.astype(jnp.int32),
                jnp.where(one, b, b0), jnp.where(two, b, b1),
                jnp.where(one, count_ref[0, b], c0), jnp.where(two, count_ref[0, b], c1),
            )

        zero = jnp.int32(0)
        found = (zero,) * 5
        for b in range(blocks):
            found = look(b, found)
        _, b0, b1, c0, c1 = found
        send[d, 0] = obs_ref[b0]
        send[d, 1] = obs_ref[b1]
        cnt_send[d] = jnp.where(row_ids == 0, c0, c1).astype(F32)
        return carry

    edges(cot_ref[...], edge.at[0])
    lax.fori_loop(0, n, pack, 0)
    pl.semaphore_wait(barrier, nlat + n - 2)

    def x_copy(d):
        return pltpu.make_async_remote_copy(
            src_ref=send.at[d], dst_ref=xs.at[d + 1], send_sem=x_ssem.at[d], recv_sem=x_rsem.at[d],
            device_id=peer(d), device_id_type=MESH,
        )

    def c_copy(d):
        return pltpu.make_async_remote_copy(
            src_ref=cnt_send.at[d], dst_ref=cnt_recv.at[d], send_sem=c_ssem.at[d], recv_sem=c_rsem.at[d],
            device_id=peer(d), device_id_type=MESH,
        )

    def g_copy(d):
        return pltpu.make_async_remote_copy(
            src_ref=send.at[d], dst_ref=ret.at[pl.ds(CAP * d, CAP)], send_sem=g_ssem.at[d],
            recv_sem=g_rsem.at[d], device_id=peer(n - d), device_id_type=MESH,
        )

    def h_copies(which):
        whom = (
            {"lat": lax.rem(lat + 1, nlat)}, {"lat": lax.rem(lat + nlat - 1, nlat)}, peer(1), peer(n - 1),
        )
        return [
            pltpu.make_async_remote_copy(
                src_ref=edge.at[which, k], dst_ref=halo.at[which, k], send_sem=h_ssem.at[which, k],
                recv_sem=h_rsem.at[which, k], device_id=whom[k], device_id_type=MESH,
            )
            for k in range(4)
        ]

    for copy in h_copies(0):
        copy.start()

    def ship(d, carry):
        c_copy(d).start()
        x_copy(d).start()
        return carry

    lax.fori_loop(1, n, ship, 0)

    xs[0] = grid_ref[...].reshape(CAP, BLK, D)
    xs[1] = send[0]
    cnt_recv[0] = cnt_send[0]
    wkv[:, :D] = wk_ref[...]
    wkv[:, D:] = wv_ref[...]
    wkvt[:D, :] = wk_ref[...].astype(F32).T.astype(BF)
    wkvt[D:, :] = wv_ref[...].astype(F32).T.astype(BF)
    lanes = lax.broadcasted_iota(jnp.int32, (CELLS, 2 * HD), 1)
    queries = dot(grid_ref[...], wq_ref[...]).astype(BF).astype(F32) * SCALING
    for copy in h_copies(0):
        copy.wait_recv()
    up = cot_ref[...].astype(F32)
    around_up = around(cot_ref[...], halo.at[0], lat == 0, lat == nlat - 1)
    for k in range(4):
        sides[k] = around_up[k].astype(BF)
    up_north, up_south, up_west, up_east = around_up
    gm_ref[...] = (
        (1.0 + sten_ref[0:1, :]) * up + sten_ref[1:2, :] * up_south + sten_ref[2:3, :] * up_north
        + sten_ref[3:4, :] * up_east + sten_ref[4:5, :] * up_west
    ).astype(BF)
    ups = dot_nt(gm_ref[...], wo_ref[...]).astype(BF).astype(F32)
    dot_t[...] = ups.T
    for h in range(HEADS):
        p, e = h // 2, h % 2
        mine = (lanes >= HD) if e else (lanes < HD)
        picked = jnp.where(mine, queries[:, p * 2 * HD : (p + 1) * 2 * HD], 0.0)
        qz[h] = picked.astype(BF)
        qzt[h] = picked.T.astype(BF)
        picked = jnp.where(mine, ups[:, p * 2 * HD : (p + 1) * 2 * HD], 0.0)
        doz[h] = picked.astype(BF)
        dozt[h] = picked.T.astype(BF)
    bias[0:ROWS, :] = jnp.zeros((ROWS, 128), F32)
    acc_o[...] = jnp.zeros_like(acc_o)
    acc_q[...] = jnp.zeros_like(acc_q)
    dwkv[...] = jnp.zeros_like(dwkv)
    m_ref[...] = jnp.full(m_ref.shape, -1e30, F32)
    l_ref[...] = jnp.zeros_like(l_ref)
    key_ids = lax.broadcasted_iota(jnp.int32, (BLK, 128), 0).astype(F32)

    def masked(rows):
        part = bias[rows, :]
        return jnp.concatenate([part, part], 1)


    def project(c, w, g):
        width = w * ROWS
        rows = pl.ds(pl.multiple_of(c * ROWS, ROWS), width)
        tokens = xs[pl.ds(c, w)].reshape(width, D)
        for j in range(4):
            cols = slice(j * 256, (j + 1) * 256)
            part = dot(tokens, wkv[:, cols]).astype(BF)
            kv[rows, cols] = part
            if j < 2:
                kt[g, cols, :width] = part.T
            else:
                vt[j * 256 - D : (j + 1) * 256 - D, :width] = part.T

    def attend(c, w):
        width = w * ROWS
        rows = pl.ds(pl.multiple_of(c * ROWS, ROWS), width)
        for h in range(HEADS):
            p = h // 2
            mine = slice(h * HD, (h + 1) * HD)
            scores = dot(kv[rows, p * 128 : (p + 1) * 128], qzt[h]) + masked(rows)
            old = m_ref[h]
            new = jnp.maximum(old, jnp.max(scores, 0, keepdims=True))
            raised = jnp.exp(scores - new)
            shrink = jnp.exp(old - new)
            l_ref[h] = l_ref[h] * shrink + jnp.sum(raised, 0, keepdims=True)
            m_ref[h] = new
            acc_o[mine, :] = acc_o[mine, :] * shrink + dot(vt[mine, :width], raised.astype(BF))

    project(0, 1, 0)
    attend(0, 1)

    def forward(g, carry):
        c = CAP * g - 1

        @pl.when(g >= 2)
        def _():
            c_copy(c - 1).wait_recv()
            x_copy(c - 1).wait_recv()

        c_copy(c).wait_recv()
        x_copy(c).wait_recv()
        for k in range(2):
            tile = cnt_recv[c - 1 + k]
            for r in range(CAP):
                rows = pl.ds(pl.multiple_of((c + k) * ROWS + r * BLK, BLK), BLK)
                bias[rows, :] = jnp.where(key_ids < tile[r : r + 1, :128], 0.0, -1e30)
        project(c, 2, g)
        attend(c, 2)
        return carry

    lax.fori_loop(1, groups + 1, forward, 0)

    def up_of():
        return cot_ref[...].astype(F32)

    def finish(h, carry):
        rows = pl.ds(pl.multiple_of(h * HD, HD), HD)
        total = l_ref[h]
        mixed = acc_o[rows, :] / total
        acc_o[rows, :] = mixed
        m_ref[h] = m_ref[h] + jnp.log(total)
        d_ref[h] = jnp.sum(mixed * dot_t[rows, :], 0, keepdims=True)
        return carry

    lax.fori_loop(0, HEADS, finish, 0)
    mid_ref[...] = (
        grid_ref[...].astype(F32) + dot(acc_o[...].T.astype(BF), wo_ref[...])
    ).astype(BF)
    edges(mid_ref[...], edge.at[1])
    for copy in h_copies(1):
        copy.start()
    centre = mid_ref[...].astype(F32)
    t0[lat] = jnp.zeros((8, D), F32)
    for row, side in enumerate((up_of(), *(sides[k].astype(F32) for k in (1, 0, 3, 2)))):
        t0[lat, row : row + 1, :] = jnp.sum(centre * side, 0, keepdims=True)
    tap1.start()
    attended = acc_o[...].astype(BF)
    sum_o.begin(lambda rows, cols: dot(attended[rows, :], gm_ref[:, cols]))

    def sent(d, carry):
        c_copy(d).wait_send()
        x_copy(d).wait_send()
        return carry

    lax.fori_loop(1, n, sent, 0)

    def differentiate(c, w, g):
        width = w * ROWS
        rows = pl.ds(pl.multiple_of(c * ROWS, ROWS), width)
        for p in range(HEADS // 2):
            here = slice(p * 128, (p + 1) * 128)
            there = slice(D + p * 128, D + (p + 1) * 128)
            grad_k = jnp.zeros((width, 128), F32)
            grad_v = jnp.zeros((width, 128), F32)
            for e in range(2):
                h = 2 * p + e
                mine = slice(h * HD, (h + 1) * HD)
                weights = jnp.exp(dot(kv[rows, here], qzt[h]) + masked(rows) - m_ref[h])
                grads = (weights * (dot(kv[rows, there], dozt[h]) - d_ref[h])).astype(BF)
                grad_k = grad_k + dot(grads, qz[h])
                grad_v = grad_v + dot(weights.astype(BF), doz[h])
                acc_q[mine, :] += dot(kt[g, mine, :width], grads)
            dkv[:width, here] = grad_k.astype(BF)
            dkv[:width, there] = grad_v.astype(BF)
        xt[:, :width] = xs[pl.ds(c, w)].reshape(width, D).T
        for j in range(4):
            cols = slice(j * 256, (j + 1) * 256)
            dwkv[:, cols] += dot(xt[:, :width], dkv[:width, cols])

    def backward(step, carry):
        g = 1 + lax.rem(step + 1, groups)
        d = CAP * g - 2
        differentiate(d + 1, 2, g)
        for j in range(2):
            cols = slice(j * 256, (j + 1) * 256)
            part = dot(dkv[...], wkvt[:, cols]).astype(BF)
            send[pl.ds(d, 2), :, :, cols] = part.reshape(2, CAP, BLK, 256)
        g_copy(d + 1).start()

        @pl.when(g >= 2)
        def _():
            g_copy(d).start()

        @pl.when(g == 1)
        def _():
            ret[0:CAP] = send[0]

        @pl.when(step == 2)
        def _():
            tap1.wait()
            total = t0[0]
            for i in range(1, nlat):
                total = total + t0[i]
            t1[me] = total
            tap2.start()
            sum_o.step2()

        @pl.when(step == 4)
        def _():
            sum_o.step3()

        @pl.when(step == 6)
        def _():
            sum_o.step4()

        return carry

    lax.fori_loop(0, groups, backward, 0)
    differentiate(0, 1, 0)

    grad_q = (acc_q[...].T * SCALING).astype(BF)
    sum_k.begin(lambda rows, cols: dwkv[rows, cols])
    sum_v.begin(lambda rows, cols: dwkv[rows, D + cols.start : D + cols.stop])
    dwq = dot(grid_ref[...].T, grad_q)
    sum_q.begin(lambda rows, cols: dwq[rows, cols])
    ggrid_ref[...] = (
        gm_ref[...].astype(F32) + dot_nt(grad_q, wq_ref[...]) + dot(dkv[:CELLS, :], wkvt[...])
    ).astype(BF)
    for copy in h_copies(1):
        copy.wait_recv()
    north, south, west, east = around(mid_ref[...], halo.at[1], lat == 0, lat == nlat - 1)
    enc_ref[...] = (
        (1.0 + sten_ref[0:1, :]) * mid_ref[...].astype(F32) + sten_ref[1:2, :] * north
        + sten_ref[2:3, :] * south + sten_ref[3:4, :] * west + sten_ref[4:5, :] * east
    ).astype(BF)
    late = (sum_k, sum_v, sum_q)
    for part in late:
        part.step2()

    def returned(d, carry):
        g_copy(d).wait_recv()
        g_copy(d).wait_send()
        return carry

    lax.fori_loop(1, n, returned, 0)

    for part in late:
        part.step3()

    def unpack(b, carry):
        tile = dest_ref[b, 0]
        rank = jnp.int32(0)
        for other in range(blocks):
            rank = rank + ((dest_ref[other, 0] == tile) & (other < b)).astype(jnp.int32)
        gobs_ref[b] = ret[CAP * lax.rem(tile - me + n, n) + jnp.minimum(rank, CAP - 1)]
        return carry

    lax.fori_loop(0, blocks, unpack, 0)
    for part in late:
        part.step4()
    tap2.wait()
    total = t1[0]
    for i in range(1, n):
        total = total + t1[i]
    taps_ref[...] = total
    for part in (sum_o, *late):
        part.step5()
    for part in (tap1, tap2):
        part.sent()
    for part in (sum_o, *late):
        part.close()
    for which in range(2):
        for copy in h_copies(which):
            copy.wait_send()


def on_device(
    grid_tokens, obs_tokens, destinations, valid_counts, w_query, w_key, w_value, w_out,
    stencil_taps, cotangent,
):
    tile_shape = grid_tokens.shape
    blocks = obs_tokens.shape[0]
    nlat, n = lax.axis_size("lat"), lax.axis_size("lon")
    vmem = pl.BlockSpec(memory_space=pltpu.VMEM)
    smem = pl.BlockSpec(memory_space=pltpu.SMEM)
    lat_sem, lon_sem = pltpu.SemaphoreType.DMA((nlat,)), pltpu.SemaphoreType.DMA((n,))
    halo_sem = pltpu.SemaphoreType.DMA((2, 4))
    sums = []
    for nf, ns, f_sem, s_sem in (
        (nlat, n, lat_sem, lon_sem), (n, nlat, lon_sem, lat_sem), (nlat, n, lat_sem, lon_sem),
        (nlat, n, lat_sem, lon_sem),
    ):
        sums += [
            pltpu.VMEM((nf, ns, 16, 128), BF), pltpu.VMEM((nf, ns, 16, 128), BF),
            pltpu.VMEM((ns, 16, 128), BF), pltpu.VMEM((ns, 16, 128), BF),
            f_sem, f_sem, s_sem, s_sem, s_sem, s_sem, f_sem, f_sem,
        ]
    tile = jax.ShapeDtypeStruct((CELLS, D), BF)
    lat_first = jax.ShapeDtypeStruct((nlat, n, 16, 128), BF)
    lon_first = jax.ShapeDtypeStruct((n, nlat, 16, 128), BF)
    encoded, grad_obs, grad_grid, *summed, taps = pl.pallas_call(
        functools.partial(kernel, nlat, n),
        out_shape=(
            tile, jax.ShapeDtypeStruct((blocks, BLK, D), BF), tile,
            lat_first, lon_first, lat_first, lat_first, jax.ShapeDtypeStruct((8, D), F32),
        ),
        in_specs=[smem] * 2 + [vmem] * 8,
        out_specs=(vmem,) * 8,
        scratch_shapes=[
            pltpu.VMEM((n, CAP, BLK, D), BF),
            pltpu.VMEM((n + 1, CAP, BLK, D), BF),
            pltpu.VMEM((n * CAP, BLK, D), BF),
            pltpu.VMEM((n, 8, CELLS), F32),
            pltpu.VMEM((n, 8, CELLS), F32),
            pltpu.VMEM(((n + 1) * ROWS, 2 * D), BF),
            pltpu.VMEM((n // 2 + 1, D, 2 * ROWS), BF),
            pltpu.VMEM((D, 2 * ROWS), BF),
            pltpu.VMEM((D, 2 * ROWS), BF),
            pltpu.VMEM(((n + 1) * ROWS, 128), F32),
            pltpu.VMEM((D, 2 * D), BF),
            pltpu.VMEM((2 * D, D), BF),
            pltpu.VMEM((HEADS, CELLS, 2 * HD), BF),
            pltpu.VMEM((HEADS, 2 * HD, CELLS), BF),
            pltpu.VMEM((HEADS, CELLS, 2 * HD), BF),
            pltpu.VMEM((HEADS, 2 * HD, CELLS), BF),
            pltpu.VMEM((D, CELLS), F32),
            pltpu.VMEM((D, CELLS), F32),
            pltpu.VMEM((D, CELLS), F32),
            pltpu.VMEM((HEADS, 1, CELLS), F32),
            pltpu.VMEM((HEADS, 1, CELLS), F32),
            pltpu.VMEM((HEADS, 1, CELLS), F32),
            pltpu.VMEM((2 * ROWS, 2 * D), BF),
            pltpu.VMEM((D, 2 * D), F32),
            pltpu.VMEM((CELLS, D), BF),
            pltpu.VMEM((CELLS, D), BF),
            pltpu.VMEM((4, CELLS, D), BF),
            pltpu.VMEM((2, 4, TILE, D), BF),
            pltpu.VMEM((2, 4, TILE, D), BF),
            pltpu.VMEM((nlat, 8, D), F32),
            pltpu.VMEM((n, 8, D), F32),
            lon_sem, lon_sem, lon_sem, lon_sem, lon_sem, lon_sem, halo_sem, halo_sem,
            lat_sem, lat_sem, lon_sem, lon_sem,
            *sums,
        ],
        compiler_params=pltpu.CompilerParams(
            collective_id=0, has_side_effects=True, vmem_limit_bytes=62 * 2**20
        ),
        name="encoder_step",
    )(
        destinations, valid_counts, obs_tokens, grid_tokens.reshape(CELLS, D),
        cotangent.reshape(CELLS, D), w_query, w_key, w_value, w_out, stencil_taps,
    )
    matrices = [
        part.reshape(4, D, 128).transpose(1, 0, 2).reshape(D, D).astype(F32) for part in summed
    ]
    return (
        encoded.reshape(tile_shape), grad_grid.reshape(tile_shape), grad_obs, *matrices, taps[:5],
    )


def solution(mesh):
    in_specs = (
        P("lat", "lon", None),
        P(("lat", "lon"), None, None),
        P(("lat", "lon"), None),
        P(("lat", "lon"), None),
        P(),
        P(),
        P(),
        P(),
        P(),
        P("lat", "lon", None),
    )
    out_specs = (
        P("lat", "lon", None),
        P("lat", "lon", None),
        P(("lat", "lon"), None, None),
        P(),
        P(),
        P(),
        P(),
        P(),
    )
    return jax.shard_map(
        on_device, mesh=mesh, in_specs=in_specs, out_specs=out_specs, check_vma=False
    )
```

time: 306 us -> 283 us (0.925)
  starting transfers between devices: 23.6 us -> 0 us
  Pallas kernels: 256 us -> 273 us
  local copies, waits for them, and re-layouts: 14.1 us -> 4.68 us
  other arithmetic: 11.1 us -> 4.47 us
    ppermute x8 -> x0, starting transfers between devices: 23.6 us -> none  [the longest x4 13.3 us: padded(): lax.ppermute(head, axis, [((i + 1) % count, i) for i in range(ends)])]
    pallas_call x2 -> x1, Pallas kernels: 256 us -> 273 us  [on_device(): pl.pallas_call(functools.partial(kernel, nlat, n), out_shape=(tile, jax.S...]
    slice x4 -> x0, local copies, waits for them, and re-layouts: 4.33 us -> none  [padded(): lax.slice_in_dim(cells, cells.shape[dim] - width, cells.shape[dim], axis=...]
    unnamed x29 -> x17, local copies, waits for them, and re-layouts: 8.99 us -> 4.68 us
    reduce_sum x3 -> x0, other arithmetic: 3.25 us -> none  [the longest x1 1.81 us: on_device(): jnp.sum(centre * side, (0, 1))]
  transfers between devices with their start and end apart: 8 -> 0, of which waited for: 0 -> 0; matrix products, arithmetic and copies ran while one was open for 4% -> 0% of each run, Pallas kernels for 20% -> 0%
where the time goes in v2:
time: 283 us
  Pallas kernels  273 us (96%)
  local copies, waits for them, and re-layouts  4.68 us (2%)
  other arithmetic  4.47 us (2%)
    pallas_call x1, Pallas kernels, on_device(): pl.pallas_call(functools.partial(kernel, nlat, n), out_shape=(tile, jax.S...  273 us

profile of v2, /device:TPU:1, one launch (start us, length us, event | category | flops | bytes accessed | tf_op | source)
XLA Modules:
  0.0 282.6 jit_solution(8109329234628903775)
XLA Ops:
  0.6 1.3 copy.18.dest_ref
  2.0 272.7 %encoder_step.1 = (bf16[256,512]{1,0:T(8,128)(2,1)}, bf16[16,128,512]{2,1,0:T(8,128)(2,1)}, bf16[256,512]{1,0:T(8,128)(2,1)}, bf16[8,16,16,128]{3,2,1,0:T(8,128)...) custom-call(s32[16,1]{1,0:T(8,128)} %copy.18.dest_ref, ...), custom_call_target="tpu_custom_call" | custom-call | tf_op jit(solution)/shard_map/encoder_step/pallas_call | solution.py:516
  274.7 0.0 copy-start.1
  274.7 0.0 copy-start.2
  274.7 2.9 %copy_bitcast_fusion.2 = (f32[512,512]{1,0:T(8,128)}, f32[512,512]{1,0:T(8,128)}) fusion(bf16[4,512,128]{2,1,0:T(8,128)(2,1)} %bitcast.39, bf16[4,512,128]{2,1,0:T(8,128)(2,1)} %bitcast.40), kind=kLoop, calls=%fused_computation.2 | loop fusion | flops 524288 | bytes 3145728 | tf_op jit(solution)/shard_map/convert_element_type | solution.py:569
  277.6 0.0 copy-start.4
  277.6 0.0 copy-start.3
  277.6 0.0 copy-done.1
  277.6 0.0 copy-done.2
  277.6 0.0 copy-start
  277.6 1.6 copy_bitcast_fusion
  279.2 0.0 copy-done.4
  279.2 0.7 copy.35
  279.9 0.0 copy-done.3
  279.9 0.7 copy.36
  280.6 0.0 copy-done
  280.6 0.0 copy-start.5
  280.6 1.3 copy.37
  281.9 0.0 copy-done.5
  281.9 0.6 copy.38
Async XLA Ops:
  274.7 2.9 %copy-start.1 = (bf16[8,16,16,128]{3,2,1,0:T(8,128)(2,1)S(1)}, bf16[8,16,16,128]{3,2,1,0:T(8,128)(2,1)}, u32[]{:S(2)}) copy-start(bf16[8,16,16,128]{3,2,1,0:T(8,128)(2,1)} %get-tuple-element.21) | copy-start | bytes 1572868
  274.7 2.9 %copy-start.2 = (bf16[8,16,16,128]{3,2,1,0:T(8,128)(2,1)S(1)}, bf16[8,16,16,128]{3,2,1,0:T(8,128)(2,1)}, u32[]{:S(2)}) copy-start(bf16[8,16,16,128]{3,2,1,0:T(8,128)(2,1)} %get-tuple-element.22) | copy-start | bytes 1572868
  277.6 1.6 copy-start.4
  277.6 2.3 copy-start.3
  277.6 3.0 %copy-start = (bf16[16,128,512]{2,1,0:T(8,128)(2,1)S(1)}, bf16[16,128,512]{2,1,0:T(8,128)(2,1)}, u32[]{:S(2)}) copy-start(bf16[16,128,512]{2,1,0:T(8,128)(2,1)} %get-tuple-element.38) | copy-start | bytes 6291460
  280.6 1.3 copy-start.5

commit v3 on v2

v3 whole, which is shorter than its diff:
```python
import functools

import jax
import jax.numpy as jnp
from jax import lax
from jax.experimental import pallas as pl
from jax.experimental.pallas import tpu as pltpu
from jax.sharding import PartitionSpec as P

D = 512
HEADS = 8
HD = D // HEADS
BLK = 128
CAP = 2
ROWS = CAP * BLK
CELLS = 256
TILE = 16
SCALING = HD ** (-0.5)
MESH = pl.DeviceIdType.MESH
SIDE = 4
STEPS = (
    (0, 0), (0, 1), (0, 3), (1, 0), (3, 0), (1, 1), (1, 3), (3, 1), (3, 3),
    (0, 2), (2, 0), (1, 2), (3, 2), (2, 1), (2, 3), (2, 2),
)
NEAR = 9
EXTRA = 16
BF = jnp.bfloat16
F32 = jnp.float32


def dot(a, b):
    return jnp.dot(a, b, preferred_element_type=F32)


def dot_nt(a, b):
    return lax.dot_general(a, b, (((1,), (1,)), ((), ())), preferred_element_type=F32)


def onehot(rows, cols, hit):
    at = [lax.broadcasted_iota(jnp.int32, (rows, cols), k) for k in range(2)]
    return jnp.where(hit(*at), 1.0, 0.0).astype(BF)


def around(cells, halo, first, last):
    top = jnp.where(first, 0.0, halo[0].astype(F32)).astype(BF)
    bottom = jnp.where(last, 0.0, halo[1].astype(F32)).astype(BF)
    side = TILE
    west = dot(onehot(CELLS, CELLS, lambda q, k: (k == q - 1) & (lax.rem(q, side) != 0)), cells)
    west = west + dot(onehot(CELLS, side, lambda q, k: q == k * side), halo[2])
    east = dot(onehot(CELLS, CELLS, lambda q, k: (k == q + 1) & (lax.rem(q, side) != side - 1)), cells)
    east = east + dot(onehot(CELLS, side, lambda q, k: q == k * side + side - 1), halo[3])
    return (
        jnp.concatenate([top, cells[:-side]], 0).astype(F32),
        jnp.concatenate([cells[side:], bottom], 0).astype(F32),
        west,
        east,
    )


def edges(cells, out):
    out[0] = cells[CELLS - TILE :]
    out[1] = cells[:TILE]
    out[2] = dot(onehot(TILE, CELLS, lambda k, q: q == k * TILE + TILE - 1), cells).astype(BF)
    out[3] = dot(onehot(TILE, CELLS, lambda k, q: q == k * TILE), cells).astype(BF)


class Exchange:
    def __init__(self, count, me, whom, copy):
        self.count, self.me, self.whom, self.copy = count, me, whom, copy

    def each(self, body):
        def step(o, carry):
            body(lax.rem(self.me + o, self.count))
            return carry

        if self.count == 2:
            body(1 - self.me)
        else:
            lax.fori_loop(1, self.count, step, 0)

    def greet(self, barrier):
        self.each(lambda at: pl.semaphore_signal(
            barrier, inc=1, device_id=self.whom(at), device_id_type=MESH))

    def start(self):
        self.each(lambda at: self.copy(at, self.me).start())

    def wait(self):
        self.each(lambda at: self.copy(at, at).wait_recv())

    def sent(self):
        self.each(lambda at: self.copy(at, self.me).wait_send())


def scatter(group, src, dst, ssem, rsem):
    count, me, whom = group
    return Exchange(count, me, whom, lambda to, frm: pltpu.make_async_remote_copy(
        src_ref=src.at[to], dst_ref=dst.at[frm], send_sem=ssem.at[to], recv_sem=rsem.at[frm],
        device_id=whom(to), device_id_type=MESH))


def gather(group, buf, ssem, rsem):
    count, me, whom = group
    return Exchange(count, me, whom, lambda to, frm: pltpu.make_async_remote_copy(
        src_ref=buf.at[me], dst_ref=buf.at[frm], send_sem=ssem.at[to], recv_sem=rsem.at[frm],
        device_id=whom(to), device_id_type=MESH))


class MatrixSum:
    def __init__(self, groups, scratch, out):
        self.core, self.x, self.lon = (group[1] for group in groups)
        self.counts = [group[0] for group in groups]
        self.whole, self.got, self.half, self.got_half, self.piece, self.got_piece = scratch[:6]
        self.out = out
        sems = scratch[6:]
        self.stages = [
            scatter(groups[0], self.whole, self.got, *sems[0:2]),
            scatter(groups[1], self.half, self.got_half, *sems[2:4]),
            scatter(groups[2], self.piece, self.got_piece, *sems[4:6]),
            gather(groups[2], out.at[self.core, self.x], *sems[6:8]),
            gather(groups[1], out.at[self.core], *sems[8:10]),
            gather(groups[0], out, *sems[10:12]),
        ]

    def load(self, number, source):
        per = D // 256
        for c in range(2):
            for x in range(4):
                f = 4 * c + x
                rows = slice((f % per) * 256, (f % per + 1) * 256)
                cols = slice((f // per) * 128, (f // per + 1) * 128)
                self.whole[c, x, :, number] = source(rows, cols).astype(BF).reshape(16, 16, 128)

    def total(self, stage, own, got):
        group = self.stages[stage]
        held = own[group.me].astype(F32)
        for o in range(1, group.count):
            held = held + got[lax.rem(group.me + o, group.count)].astype(F32)
        return held.astype(BF)

    def begin(self):
        self.stages[0].start()

    def step(self, stage):
        self.stages[stage].wait()
        if stage == 0:
            for x in range(4):
                self.half[x] = (
                    self.whole[self.core, x].astype(F32) + self.got[1 - self.core, x].astype(F32)
                ).astype(BF)
        elif stage == 1:
            self.piece[...] = self.total(1, self.half, self.got_half)
        elif stage == 2:
            self.out[self.core, self.x, self.lon] = self.total(2, self.piece, self.got_piece)
        if stage < 5:
            self.stages[stage + 1].start()

    def close(self):
        for stage in self.stages:
            stage.sent()


def kernel(
    nlat, n, dest_ref, count_ref, obs_ref, grid_ref, cot_ref, wq_ref, wk_ref, wv_ref, wo_ref, sten_ref,
    enc_ref, gobs_ref, ggrid_ref, late_ref, early_ref, taps_ref,
    send, xs, ret, relay, relay_back, kv, kt, vt, xt, bias, wkv, wkvt, qz, qzt, doz, dozt, dot_t,
    acc_o, acc_q, m_ref, l_ref, d_ref, dkv, dwkv, gm_ref, mid_ref, sides, edge, halo, t0, t1,
    x_ssem, x_rsem, r_ssem, r_rsem, g_ssem, g_rsem, b_ssem, b_rsem, h_ssem, h_rsem, t1s, t1r, t2s, t2r,
    *sum_scratch,
):
    lat, me = lax.axis_index("lat"), lax.axis_index("lon")
    groups = n // 2
    blocks = obs_ref.shape[0]
    x_at, core = lat // 2, lax.rem(lat, 2)
    rings = (
        (2, core, lambda at: {"lat": 2 * x_at + at}),
        (nlat // 2, x_at, lambda at: {"lat": 2 * at + core}),
        (n, me, lambda at: {"lon": at}),
    )
    half = len(sum_scratch) // 2
    late = MatrixSum(rings, sum_scratch[:half], late_ref)
    early = MatrixSum(rings, sum_scratch[half:], early_ref)
    tap1 = gather((nlat, lat, lambda at: {"lat": at}), t0, t1s, t1r)
    tap2 = gather(rings[2], t1, t2s, t2r)

    y, z = me // SIDE, lax.rem(me, SIDE)
    way_y, way_z = 1 - 2 * lax.rem(y, 2), 1 - 2 * lax.rem(z, 2)

    def place(dy, dz):
        return lax.rem(y + dy + 2 * SIDE, SIDE) * SIDE + lax.rem(z + dz + 2 * SIDE, SIDE)

    def leg(i, sign):
        dy, dz = STEPS[i]
        return {"lon": place(
            way_y if dy == 2 else sign * dy, way_z if dz == 2 else sign * dz)}

    def onward(i):
        dy, dz = STEPS[i]
        return {"lon": place(-way_y if dy == 2 else 0, -way_z if dz == 2 else 0)}

    barrier = pltpu.get_barrier_semaphore()
    for group in (tap1, tap2):
        group.greet(barrier)

    row_ids = lax.broadcasted_iota(jnp.int32, (EXTRA, D), 0)

    def pack(i):
        tile = place(*STEPS[i])
        number = b0 = b1 = c0 = c1 = jnp.int32(0)
        for b in range(blocks):
            hit = dest_ref[0, b] == tile
            one, two = hit & (number == 0), hit & (number == 1)
            number = number + hit.astype(jnp.int32)
            b0, b1 = jnp.where(one, b, b0), jnp.where(two, b, b1)
            c0, c1 = jnp.where(one, count_ref[0, b], c0), jnp.where(two, count_ref[0, b], c1)
        send[i, 0:BLK, :] = obs_ref[b0]
        send[i, BLK:ROWS, :] = obs_ref[b1]
        send[i, ROWS:, :] = jnp.where(row_ids == 0, c0, c1).astype(F32).astype(BF)

    edges(cot_ref[...], edge.at[0])
    pl.semaphore_wait(barrier, nlat + n - 2)

    def remote(src, dst, ssem, rsem, whom):
        return pltpu.make_async_remote_copy(
            src_ref=src, dst_ref=dst, send_sem=ssem, recv_sem=rsem, device_id=whom, device_id_type=MESH)

    def x_copy(i):
        if i < NEAR:
            return remote(send.at[i], xs.at[i + 1], x_ssem.at[i], x_rsem.at[i], leg(i, 1))
        j = i - NEAR
        return remote(send.at[i], relay.at[j], x_ssem.at[i], r_rsem.at[j], leg(i, 1))

    def x_onward(i):
        j = i - NEAR
        return remote(relay.at[j], xs.at[i + 1], r_ssem.at[j], x_rsem.at[i], onward(i))

    def g_copy(i):
        tokens = send.at[i, pl.ds(0, ROWS)]
        if i < NEAR:
            return remote(tokens, ret.at[i], g_ssem.at[i], g_rsem.at[i], leg(i, -1))
        j = i - NEAR
        return remote(tokens, relay_back.at[j], g_ssem.at[i], b_rsem.at[j], leg(i, -1))

    def g_onward(i):
        j = i - NEAR
        return remote(relay_back.at[j], ret.at[i], b_ssem.at[j], g_rsem.at[i], onward(i))

    def x_arrived(i):
        remote(send.at[0], xs.at[i + 1], x_ssem.at[0], x_rsem.at[i], {"lon": me}).wait_recv()

    def h_copies(which):
        whom = (
            {"lat": lax.rem(lat + 1, nlat)}, {"lat": lax.rem(lat + nlat - 1, nlat)},
            {"lon": lax.rem(me + 1, n)}, {"lon": lax.rem(me + n - 1, n)},
        )
        return [
            remote(edge.at[which, k], halo.at[which, k], h_ssem.at[which, k], h_rsem.at[which, k], whom[k])
            for k in range(4)
        ]

    for copy in h_copies(0):
        copy.start()

    for i in (*range(NEAR, n), *range(1, NEAR)):
        pack(i)
        x_copy(i).start()
    pack(0)

    xs[0, 0:ROWS, :] = grid_ref[...]
    xs[1] = send[0]
    wkv[:, :D] = wk_ref[...]
    wkv[:, D:] = wv_ref[...]
    wkvt[:D, :] = wk_ref[...].astype(F32).T.astype(BF)
    wkvt[D:, :] = wv_ref[...].astype(F32).T.astype(BF)
    lanes = lax.broadcasted_iota(jnp.int32, (CELLS, 2 * HD), 1)
    queries = dot(grid_ref[...], wq_ref[...]).astype(BF).astype(F32) * SCALING
    for copy in h_copies(0):
        copy.wait_recv()
    up = cot_ref[...].astype(F32)
    around_up = around(cot_ref[...], halo.at[0], lat == 0, lat == nlat - 1)
    for k in range(4):
        sides[k] = around_up[k].astype(BF)
    up_north, up_south, up_west, up_east = around_up
    gm_ref[...] = (
        (1.0 + sten_ref[0:1, :]) * up + sten_ref[1:2, :] * up_south + sten_ref[2:3, :] * up_north
        + sten_ref[3:4, :] * up_east + sten_ref[4:5, :] * up_west
    ).astype(BF)
    ups = dot_nt(gm_ref[...], wo_ref[...]).astype(BF).astype(F32)
    dot_t[...] = ups.T
    for h in range(HEADS):
        p, e = h // 2, h % 2
        mine = (lanes >= HD) if e else (lanes < HD)
        picked = jnp.where(mine, queries[:, p * 2 * HD : (p + 1) * 2 * HD], 0.0)
        qz[h] = picked.astype(BF)
        qzt[h] = picked.T.astype(BF)
        picked = jnp.where(mine, ups[:, p * 2 * HD : (p + 1) * 2 * HD], 0.0)
        doz[h] = picked.astype(BF)
        dozt[h] = picked.T.astype(BF)
    acc_o[...] = jnp.zeros_like(acc_o)
    acc_q[...] = jnp.zeros_like(acc_q)
    dwkv[...] = jnp.zeros_like(dwkv)
    m_ref[...] = jnp.full(m_ref.shape, -1e30, F32)
    l_ref[...] = jnp.zeros_like(l_ref)
    key_ids = lax.broadcasted_iota(jnp.int32, (BLK, 128), 0).astype(F32)

    def masked(width):
        part = bias[0:width, :]
        return jnp.concatenate([part, part], 1)

    def mark(c, w):
        if w == 1:
            bias[0:ROWS, :] = jnp.zeros((ROWS, 128), F32)
            return
        for k in range(w):
            tile = xs[c + k, ROWS:, 0:128].astype(F32)
            for r in range(CAP):
                at = k * ROWS + r * BLK
                bias[at : at + BLK, :] = jnp.where(key_ids < tile[r : r + 1, :], 0.0, -1e30)

    def project(c, w, g):
        width = w * ROWS
        rows = pl.ds(pl.multiple_of(c * ROWS, ROWS), width)
        tokens = xs[pl.ds(c, w), 0:ROWS, :].reshape(width, D)
        for j in range(4):
            cols = slice(j * 256, (j + 1) * 256)
            part = dot(tokens, wkv[:, cols]).astype(BF)
            kv[rows, cols] = part
            if j < 2:
                kt[g, cols, :width] = part.T
            else:
                vt[j * 256 - D : (j + 1) * 256 - D, :width] = part.T

    def attend(c, w):
        width = w * ROWS
        mark(c, w)
        rows = pl.ds(pl.multiple_of(c * ROWS, ROWS), width)

        def pair(p, carry):
            keys = kv[rows, pl.ds(pl.multiple_of(p * 128, 128), 128)]
            for e in range(2):
                h = 2 * p + e
                mine = pl.ds(pl.multiple_of(h * HD, HD), HD)
                scores = dot(keys, qzt[h]) + masked(width)
                old = m_ref[h]
                new = jnp.maximum(old, jnp.max(scores, 0, keepdims=True))
                raised = jnp.exp(scores - new)
                shrink = jnp.exp(old - new)
                l_ref[h] = l_ref[h] * shrink + jnp.sum(raised, 0, keepdims=True)
                m_ref[h] = new
                acc_o[mine, :] = acc_o[mine, :] * shrink + dot(vt[mine, :width], raised.astype(BF))
            return carry

        lax.fori_loop(0, HEADS // 2, pair, 0)

    project(0, 1, 0)
    attend(0, 1)

    for i in range(NEAR, n):
        x_copy(i).wait_recv()
        x_onward(i).start()

    def forward(g, carry):
        c = CAP * g - 1

        @pl.when(g >= 2)
        def _():
            x_arrived(c - 1)

        x_arrived(c)
        project(c, 2, g)
        attend(c, 2)
        return carry

    lax.fori_loop(1, groups + 1, forward, 0)

    def up_of():
        return cot_ref[...].astype(F32)

    def finish(h, carry):
        rows = pl.ds(pl.multiple_of(h * HD, HD), HD)
        total = l_ref[h]
        mixed = acc_o[rows, :] / total
        acc_o[rows, :] = mixed
        m_ref[h] = m_ref[h] + jnp.log(total)
        d_ref[h] = jnp.sum(mixed * dot_t[rows, :], 0, keepdims=True)
        return carry

    lax.fori_loop(0, HEADS, finish, 0)
    mid_ref[...] = (
        grid_ref[...].astype(F32) + dot(acc_o[...].T.astype(BF), wo_ref[...])
    ).astype(BF)
    edges(mid_ref[...], edge.at[1])
    for copy in h_copies(1):
        copy.start()
    centre = mid_ref[...].astype(F32)
    t0[lat] = jnp.zeros((8, D), F32)
    for row, side in enumerate((up_of(), *(sides[k].astype(F32) for k in (1, 0, 3, 2)))):
        t0[lat, row : row + 1, :] = jnp.sum(centre * side, 0, keepdims=True)
    tap1.start()
    attended = acc_o[...].astype(BF)
    early.load(0, lambda rows, cols: dot(attended[rows, :], gm_ref[:, cols]))
    early.begin()

    for i in range(1, n):
        x_copy(i).wait_send()

    def differentiate(c, w, parts):
        width = w * ROWS
        mark(c, w)
        rows = pl.ds(pl.multiple_of(c * ROWS, ROWS), width)

        def pair(p, carry):
            here = pl.ds(pl.multiple_of(p * 128, 128), 128)
            there = pl.ds(pl.multiple_of(D + p * 128, 128), 128)
            keys, values = kv[rows, here], kv[rows, there]
            grad_k = grad_v = None
            for e in range(2):
                h = 2 * p + e
                mine = pl.ds(pl.multiple_of(h * HD, HD), HD)
                weights = jnp.exp(dot(keys, qzt[h]) + masked(width) - m_ref[h])
                grads = (weights * (dot(values, dozt[h]) - d_ref[h])).astype(BF)
                part_k, part_v = dot(grads, qz[h]), dot(weights.astype(BF), doz[h])
                grad_k = part_k if e == 0 else grad_k + part_k
                grad_v = part_v if e == 0 else grad_v + part_v
                total = acc_q[mine, :]
                for k, g in enumerate(parts):
                    span = min(width, 2 * ROWS)
                    total = total + dot(kt[g, mine, :span], grads[k * span : (k + 1) * span, :])
                acc_q[mine, :] = total
            dkv[:width, here] = grad_k.astype(BF)
            dkv[:width, there] = grad_v.astype(BF)
            return carry

        lax.fori_loop(0, HEADS // 2, pair, 0)
        xt[:, :width] = xs[pl.ds(c, w), 0:ROWS, :].reshape(width, D).T

        def weigh(j, carry):
            cols = pl.ds(pl.multiple_of(j * 256, 256), 256)
            dwkv[:, cols] += dot(xt[:, :width], dkv[:width, cols])
            return carry

        lax.fori_loop(0, 4, weigh, 0)

    def backward(step, carry):
        g = groups - step
        differentiate(CAP * g - 1, 2, (g,))

        def turn(j, inner):
            cols = pl.ds(pl.multiple_of(j * 256, 256), 256)
            part = dot(dkv[...], wkvt[:, cols]).astype(BF)
            send[pl.ds(CAP * g - 2, 2), 0:ROWS, cols] = part.reshape(2, ROWS, 256)
            return inner

        lax.fori_loop(0, 2, turn, 0)
        for k in range(groups):
            @pl.when(step == k)
            def _(k=k):
                first = CAP * (groups - k) - 2
                if first:
                    g_copy(first).start()
                else:
                    ret[0] = send[0, 0:ROWS, :]
                g_copy(first + 1).start()
                if k >= 2:
                    for i in (first + 4, first + 5):
                        if i >= NEAR:
                            g_copy(i).wait_recv()
                            g_onward(i).start()

        @pl.when(step == 2)
        def _():
            tap1.wait()
            total = t0[0]
            for i in range(1, nlat):
                total = total + t0[i]
            t1[me] = total
            tap2.start()

        for stage in range(5):
            pl.when(step == stage + 2)(functools.partial(early.step, stage))

        return carry

    lax.fori_loop(0, groups, backward, 0)
    differentiate(0, 1, (0,))

    grad_q = (acc_q[...].T * SCALING).astype(BF)
    dwq = dot(grid_ref[...].T, grad_q)
    late.load(0, lambda rows, cols: dwq[rows, cols])
    late.load(1, lambda rows, cols: dwkv[rows, cols])
    late.load(2, lambda rows, cols: dwkv[rows, D + cols.start : D + cols.stop])
    late.begin()
    ggrid_ref[...] = (
        gm_ref[...].astype(F32) + dot_nt(grad_q, wq_ref[...]) + dot(dkv[:CELLS, :], wkvt[...])
    ).astype(BF)
    for copy in h_copies(1):
        copy.wait_recv()
    north, south, west, east = around(mid_ref[...], halo.at[1], lat == 0, lat == nlat - 1)
    enc_ref[...] = (
        (1.0 + sten_ref[0:1, :]) * mid_ref[...].astype(F32) + sten_ref[1:2, :] * north
        + sten_ref[2:3, :] * south + sten_ref[3:4, :] * west + sten_ref[4:5, :] * east
    ).astype(BF)
    late.step(0)

    for i in range(1, n):
        if i < NEAR:
            g_copy(i).wait_recv()
        else:
            g_onward(i).wait_recv()
        g_copy(i).wait_send()
        if i >= NEAR:
            x_onward(i).wait_send()
            g_onward(i).wait_send()

    late.step(1)

    def unpack(b, carry):
        tile = dest_ref[0, b]
        rank = jnp.int32(0)
        for other in range(blocks):
            rank = rank + ((dest_ref[0, other] == tile) & (other < b)).astype(jnp.int32)
        dy = lax.rem(tile // SIDE - y + SIDE, SIDE)
        dz = lax.rem(lax.rem(tile, SIDE) - z + SIDE, SIDE)
        at = jnp.int32(0)
        for i, (sy, sz) in enumerate(STEPS):
            at = jnp.where((dy == sy) & (dz == sz), i, at)
        both = ret[at]
        gobs_ref[b] = jnp.where(rank == 0, both[:BLK], both[BLK:])
        return carry

    lax.fori_loop(0, blocks, unpack, 0)
    late.step(2)
    tap2.wait()
    total = t1[0]
    for i in range(1, n):
        total = total + t1[i]
    taps_ref[...] = total
    late.step(3)
    early.step(5)
    late.step(4)
    late.step(5)
    for part in (tap1, tap2):
        part.sent()
    for part in (early, late):
        part.close()
    for which in range(2):
        for copy in h_copies(which):
            copy.wait_send()


def write_kernel(
    enc, gobs, ggrid, late, early, taps, enc_o, gobs_o, ggrid_o, wq, wk, wv, wo, taps_o,
    enc_v, gobs_v, ggrid_v, late_v, early_v, sums_v, in_sems, out_sems,
):
    pairs = ((late, late_v, None), (early, early_v, None), (gobs, gobs_v, gobs_o), (enc, enc_v, enc_o),
             (ggrid, ggrid_v, ggrid_o))
    loads = [pltpu.make_async_copy(a, b, in_sems.at[k]) for k, (a, b, _) in enumerate(pairs)]
    stores = []

    def store(source, out):
        stores.append(pltpu.make_async_copy(source, out, out_sems.at[len(stores)]))
        stores[-1].start()

    for load in loads:
        load.start()
    taps_o[...] = taps[0:5, :]
    loads[0].wait()
    for k, (out, source, number) in enumerate(
            ((wq, late_v, 0), (wk, late_v, 1), (wv, late_v, 2), (wo, early_v, 0))):
        if k == 3:
            loads[1].wait()
        for f in range(8):
            rows, cols = slice((f % 2) * 256, (f % 2 + 1) * 256), slice((f // 2) * 128, (f // 2 + 1) * 128)
            sums_v[k, rows, cols] = source[f // 4, f % 4, :, number].reshape(256, 128).astype(F32)
        store(sums_v.at[k], out)
        if k < 3:
            loads[2 + k].wait()
            store(pairs[2 + k][1], pairs[2 + k][2])
    for copy in stores:
        copy.wait()


def on_device(
    grid_tokens, obs_tokens, destinations, valid_counts, w_query, w_key, w_value, w_out,
    stencil_taps, cotangent,
):
    tile_shape = grid_tokens.shape
    blocks = obs_tokens.shape[0]
    nlat, n = lax.axis_size("lat"), lax.axis_size("lon")
    vmem = pl.BlockSpec(memory_space=pltpu.VMEM)
    smem = pl.BlockSpec(memory_space=pltpu.SMEM)
    lat_sem, lon_sem = pltpu.SemaphoreType.DMA((nlat,)), pltpu.SemaphoreType.DMA((n,))
    far_sem = pltpu.SemaphoreType.DMA((n - NEAR,))
    halo_sem = pltpu.SemaphoreType.DMA((2, 4))
    x_sem, core_sem = pltpu.SemaphoreType.DMA((nlat // 2,)), pltpu.SemaphoreType.DMA((2,))
    sums = []
    for number in (3, 1):
        whole, part, piece = (
            pltpu.VMEM((*lead, number, 16, 128), BF) for lead in ((2, nlat // 2, n), (nlat // 2, n), (n,))
        )
        sums += [whole, whole, part, part, piece, piece]
        sums += [core_sem, core_sem, x_sem, x_sem, lon_sem, lon_sem]
        sums += [lon_sem, lon_sem, x_sem, x_sem, core_sem, core_sem]
    tile = jax.ShapeDtypeStruct((CELLS, D), BF)
    results = pl.pallas_call(
        functools.partial(kernel, nlat, n),
        out_shape=(
            tile, jax.ShapeDtypeStruct((blocks, BLK, D), BF), tile,
            jax.ShapeDtypeStruct((2, nlat // 2, n, 3, 16, 128), BF),
            jax.ShapeDtypeStruct((2, nlat // 2, n, 1, 16, 128), BF),
            jax.ShapeDtypeStruct((8, D), F32),
        ),
        in_specs=[smem] * 2 + [vmem] * 8,
        out_specs=(vmem,) * 6,
        scratch_shapes=[
            pltpu.VMEM((n, ROWS + EXTRA, D), BF),
            pltpu.VMEM((n + 1, ROWS + EXTRA, D), BF),
            pltpu.VMEM((n, ROWS, D), BF),
            pltpu.VMEM((n - NEAR, ROWS + EXTRA, D), BF),
            pltpu.VMEM((n - NEAR, ROWS, D), BF),
            pltpu.VMEM(((n + 1) * ROWS, 2 * D), BF),
            pltpu.VMEM((n // 2 + 1, D, 2 * ROWS), BF),
            pltpu.VMEM((D, 2 * ROWS), BF),
            pltpu.VMEM((D, 2 * ROWS), BF),
            pltpu.VMEM((2 * ROWS, 128), F32),
            pltpu.VMEM((D, 2 * D), BF),
            pltpu.VMEM((2 * D, D), BF),
            pltpu.VMEM((HEADS, CELLS, 2 * HD), BF),
            pltpu.VMEM((HEADS, 2 * HD, CELLS), BF),
            pltpu.VMEM((HEADS, CELLS, 2 * HD), BF),
            pltpu.VMEM((HEADS, 2 * HD, CELLS), BF),
            pltpu.VMEM((D, CELLS), F32),
            pltpu.VMEM((D, CELLS), F32),
            pltpu.VMEM((D, CELLS), F32),
            pltpu.VMEM((HEADS, 1, CELLS), F32),
            pltpu.VMEM((HEADS, 1, CELLS), F32),
            pltpu.VMEM((HEADS, 1, CELLS), F32),
            pltpu.VMEM((2 * ROWS, 2 * D), BF),
            pltpu.VMEM((D, 2 * D), F32),
            pltpu.VMEM((CELLS, D), BF),
            pltpu.VMEM((CELLS, D), BF),
            pltpu.VMEM((4, CELLS, D), BF),
            pltpu.VMEM((2, 4, TILE, D), BF),
            pltpu.VMEM((2, 4, TILE, D), BF),
            pltpu.VMEM((nlat, 8, D), F32),
            pltpu.VMEM((n, 8, D), F32),
            lon_sem, lon_sem, far_sem, far_sem, lon_sem, lon_sem, far_sem, far_sem, halo_sem, halo_sem,
            lat_sem, lat_sem, lon_sem, lon_sem,
            *sums,
        ],
        compiler_params=pltpu.CompilerParams(
            collective_id=0, has_side_effects=True, vmem_limit_bytes=62 * 2**20
        ),
        name="encoder_step",
    )(
        destinations.reshape(1, blocks), valid_counts, obs_tokens, grid_tokens.reshape(CELLS, D),
        cotangent.reshape(CELLS, D), w_query, w_key, w_value, w_out, stencil_taps,
    )
    anywhere = pl.BlockSpec(memory_space=pl.ANY)
    matrix = jax.ShapeDtypeStruct((D, D), F32)
    encoded, grad_obs, grad_grid, *sums = pl.pallas_call(
        write_kernel,
        out_shape=(
            tile, jax.ShapeDtypeStruct((blocks, BLK, D), BF), tile, matrix, matrix, matrix, matrix,
            jax.ShapeDtypeStruct((5, D), F32),
        ),
        in_specs=[anywhere] * 5 + [vmem],
        out_specs=(anywhere,) * 7 + (vmem,),
        scratch_shapes=[
            pltpu.VMEM((CELLS, D), BF), pltpu.VMEM((blocks, BLK, D), BF), pltpu.VMEM((CELLS, D), BF),
            pltpu.VMEM((2, nlat // 2, n, 3, 16, 128), BF), pltpu.VMEM((2, nlat // 2, n, 1, 16, 128), BF),
            pltpu.VMEM((4, D, D), F32), pltpu.SemaphoreType.DMA((5,)), pltpu.SemaphoreType.DMA((7,)),
        ],
        compiler_params=pltpu.CompilerParams(vmem_limit_bytes=62 * 2**20),
        name="write_results",
    )(*results)
    return (encoded.reshape(tile_shape), grad_grid.reshape(tile_shape), grad_obs, *sums)


def solution(mesh):
    in_specs = (
        P("lat", "lon", None),
        P(("lat", "lon"), None, None),
        P(("lat", "lon"), None),
        P(("lat", "lon"), None),
        P(),
        P(),
        P(),
        P(),
        P(),
        P("lat", "lon", None),
    )
    out_specs = (
        P("lat", "lon", None),
        P("lat", "lon", None),
        P(("lat", "lon"), None, None),
        P(),
        P(),
        P(),
        P(),
        P(),
    )
    return jax.shard_map(
        on_device, mesh=mesh, in_specs=in_specs, out_specs=out_specs, check_vma=False
    )
```

time: 283 us -> 224 us (0.79)
  Pallas kernels: 273 us -> 223 us
  local copies, waits for them, and re-layouts: 4.68 us -> 0 us
  other arithmetic: 4.47 us -> 0 us
    pallas_call x1, Pallas kernels: 273 us -> 217 us  [on_device(): pl.pallas_call(functools.partial(kernel, nlat, n), out_shape=(tile, jax.S...]
    pallas_call x0 -> x1, Pallas kernels: none -> 6.13 us  [on_device(): pl.pallas_call(write_kernel, out_shape=(tile, jax.ShapeDtypeStruct((block...]
    unnamed x17 -> x0, local copies, waits for them, and re-layouts: 4.68 us -> none
    convert_element_type x2 -> x0, other arithmetic: 4.47 us -> none  [on_device(): part.reshape(4, D, 128).transpose(1, 0, 2).reshape(D, D).astype(F32)]
where the time goes in v3:
time: 224 us
  Pallas kernels  223 us (100%)
    pallas_call x1, Pallas kernels, on_device(): pl.pallas_call(functools.partial(kernel, nlat, n), out_shape=(tile, jax.S...  217 us
    pallas_call x1, Pallas kernels, on_device(): pl.pallas_call(write_kernel, out_shape=(tile, jax.ShapeDtypeStruct((block...  6.13 us

profile of v3, /device:TPU:1, one launch (start us, length us, event | category | flops | bytes accessed | tf_op | source)
XLA Modules:
  0.0 224.0 jit_solution(11931819393671655615)
XLA Ops:
  0.6 217.2 %encoder_step.1 = (bf16[256,512]{1,0:T(8,128)(2,1)}, bf16[16,128,512]{2,1,0:T(8,128)(2,1)}, bf16[256,512]{1,0:T(8,128)(2,1)}, bf16[2,4,16,3,16,128]{5,4,3,2,1,0:...) custom-call(s32[1,16]{1,0:T(1,128)} %bitcast.7, s32[1,16]{1,0:T(1,128)} %count_ref.1, ...), custom_call_target="tpu_custom_call" | custom-call | tf_op jit(solution)/shard_map/encoder_step/pallas_call | solution.py:605
  217.9 6.1 %write_results.1 = (bf16[256,512]{1,0:T(8,128)(2,1)}, bf16[16,128,512]{2,1,0:T(8,128)(2,1)}, bf16[256,512]{1,0:T(8,128)(2,1)}, f32[512,512]{1,0:T(8,128)}, f32[5...) custom-call(bf16[256,512]{1,0:T(8,128)(2,1)} %get-tuple-element.22.enc, ...), custom_call_target="tpu_custom_call" | custom-call | tf_op jit(solution)/shard_map/write_results/pallas_call | solution.py:661

commit v4 on v3

--- a/solution.py
+++ b/solution.py
@@ -22,7 +22,7 @@
     (0, 0), (0, 1), (0, 3), (1, 0), (3, 0), (1, 1), (1, 3), (3, 1), (3, 3),
     (0, 2), (2, 0), (1, 2), (3, 2), (2, 1), (2, 3), (2, 2),
 )
-NEAR = 9
+NEXT, NEAR = 5, 9
 EXTRA = 16
 BF = jnp.bfloat16
 F32 = jnp.float32
@@ -163,8 +163,8 @@
 def kernel(
     nlat, n, dest_ref, count_ref, obs_ref, grid_ref, cot_ref, wq_ref, wk_ref, wv_ref, wo_ref, sten_ref,
     enc_ref, gobs_ref, ggrid_ref, late_ref, early_ref, taps_ref,
-    send, xs, ret, relay, relay_back, kv, kt, vt, xt, bias, wkv, wkvt, qz, qzt, doz, dozt, dot_t,
-    acc_o, acc_q, m_ref, l_ref, d_ref, dkv, dwkv, gm_ref, mid_ref, sides, edge, halo, t0, t1,
+    send, xs, ret, relay, relay_back, kv, kt, vt, bias, wkv, qt, qzt, dozt, dot_t,
+    acc_o, acc_q, m_ref, l_ref, d_ref, dkvt, dwt, gm_ref, mid_ref, sides, edge, halo, t0, t1,
     x_ssem, x_rsem, r_ssem, r_rsem, g_ssem, g_rsem, b_ssem, b_rsem, h_ssem, h_rsem, t1s, t1r, t2s, t2r,
     *sum_scratch,
 ):
@@ -189,14 +189,18 @@
     def place(dy, dz):
         return lax.rem(y + dy + 2 * SIDE, SIDE) * SIDE + lax.rem(z + dz + 2 * SIDE, SIDE)
 
+    def turned(i):
+        return 1 if STEPS[i] in ((0, 2), (2, 0), (2, 2)) else -1
+
     def leg(i, sign):
         dy, dz = STEPS[i]
         return {"lon": place(
-            way_y if dy == 2 else sign * dy, way_z if dz == 2 else sign * dz)}
+            turned(i) * way_y if dy == 2 else sign * dy, turned(i) * way_z if dz == 2 else sign * dz)}
 
     def onward(i):
         dy, dz = STEPS[i]
-        return {"lon": place(-way_y if dy == 2 else 0, -way_z if dz == 2 else 0)}
+        return {"lon": place(
+            -turned(i) * way_y if dy == 2 else 0, -turned(i) * way_z if dz == 2 else 0)}
 
     barrier = pltpu.get_barrier_semaphore()
     for group in (tap1, tap2):
@@ -261,7 +265,7 @@
     for copy in h_copies(0):
         copy.start()
 
-    for i in (*range(NEAR, n), *range(1, NEAR)):
+    for i in (*range(NEAR, n), *range(1, NEXT)):
         pack(i)
         x_copy(i).start()
     pack(0)
@@ -270,8 +274,6 @@
     xs[1] = send[0]
     wkv[:, :D] = wk_ref[...]
     wkv[:, D:] = wv_ref[...]
-    wkvt[:D, :] = wk_ref[...].astype(F32).T.astype(BF)
-    wkvt[D:, :] = wv_ref[...].astype(F32).T.astype(BF)
     lanes = lax.broadcasted_iota(jnp.int32, (CELLS, 2 * HD), 1)
     queries = dot(grid_ref[...], wq_ref[...]).astype(BF).astype(F32) * SCALING
     for copy in h_copies(0):
@@ -286,19 +288,18 @@
         + sten_ref[3:4, :] * up_east + sten_ref[4:5, :] * up_west
     ).astype(BF)
     ups = dot_nt(gm_ref[...], wo_ref[...]).astype(BF).astype(F32)
-    dot_t[...] = ups.T
+    dot_t[...] = ups.T.astype(BF)
+    qt[...] = queries.T.astype(BF)
     for h in range(HEADS):
         p, e = h // 2, h % 2
         mine = (lanes >= HD) if e else (lanes < HD)
         picked = jnp.where(mine, queries[:, p * 2 * HD : (p + 1) * 2 * HD], 0.0)
-        qz[h] = picked.astype(BF)
         qzt[h] = picked.T.astype(BF)
         picked = jnp.where(mine, ups[:, p * 2 * HD : (p + 1) * 2 * HD], 0.0)
-        doz[h] = picked.astype(BF)
         dozt[h] = picked.T.astype(BF)
     acc_o[...] = jnp.zeros_like(acc_o)
     acc_q[...] = jnp.zeros_like(acc_q)
-    dwkv[...] = jnp.zeros_like(dwkv)
+    dwt[...] = jnp.zeros_like(dwt)
     m_ref[...] = jnp.full(m_ref.shape, -1e30, F32)
     l_ref[...] = jnp.zeros_like(l_ref)
     key_ids = lax.broadcasted_iota(jnp.int32, (BLK, 128), 0).astype(F32)
@@ -335,12 +336,12 @@
         mark(c, w)
         rows = pl.ds(pl.multiple_of(c * ROWS, ROWS), width)
 
-        def pair(p, carry):
-            keys = kv[rows, pl.ds(pl.multiple_of(p * 128, 128), 128)]
-            for e in range(2):
-                h = 2 * p + e
+        def four(q, carry):
+            for e in range(4):
+                h = 4 * q + e
                 mine = pl.ds(pl.multiple_of(h * HD, HD), HD)
-                scores = dot(keys, qzt[h]) + masked(width)
+                here = pl.ds(pl.multiple_of((2 * q + e // 2) * 128, 128), 128)
+                scores = dot(kv[rows, here], qzt[h]) + masked(width)
                 old = m_ref[h]
                 new = jnp.maximum(old, jnp.max(scores, 0, keepdims=True))
                 raised = jnp.exp(scores - new)
@@ -350,7 +351,7 @@
                 acc_o[mine, :] = acc_o[mine, :] * shrink + dot(vt[mine, :width], raised.astype(BF))
             return carry
 
-        lax.fori_loop(0, HEADS // 2, pair, 0)
+        lax.fori_loop(0, HEADS // 4, four, 0)
 
     project(0, 1, 0)
     attend(0, 1)
@@ -359,10 +360,22 @@
         x_copy(i).wait_recv()
         x_onward(i).start()
 
-    def forward(g, carry):
+    for i in range(NEXT, NEAR):
+        pack(i)
+
+    def forward(step, carry):
+        second, third = (step + 6) // 8, (step + 3) // 8
+        g = step + 1 + 3 * second + third * (6 - 2 * step)
         c = CAP * g - 1
 
-        @pl.when(g >= 2)
+        @pl.when(step == 2)
+        def _():
+            for i in range(NEAR, n):
+                x_onward(i).wait_send()
+            for i in range(NEXT, NEAR):
+                x_copy(i).start()
+
+        @pl.when(step >= 1)
         def _():
             x_arrived(c - 1)
 
@@ -371,7 +384,7 @@
         attend(c, 2)
         return carry
 
-    lax.fori_loop(1, groups + 1, forward, 0)
+    lax.fori_loop(0, groups, forward, 0)
 
     def up_of():
         return cot_ref[...].astype(F32)
@@ -382,72 +395,66 @@
         mixed = acc_o[rows, :] / total
         acc_o[rows, :] = mixed
         m_ref[h] = m_ref[h] + jnp.log(total)
-        d_ref[h] = jnp.sum(mixed * dot_t[rows, :], 0, keepdims=True)
+        d_ref[h] = jnp.sum(mixed * dot_t[rows, :].astype(F32), 0, keepdims=True)
         return carry
 
     lax.fori_loop(0, HEADS, finish, 0)
-    mid_ref[...] = (
-        grid_ref[...].astype(F32) + dot(acc_o[...].T.astype(BF), wo_ref[...])
-    ).astype(BF)
-    edges(mid_ref[...], edge.at[1])
-    for copy in h_copies(1):
-        copy.start()
-    centre = mid_ref[...].astype(F32)
-    t0[lat] = jnp.zeros((8, D), F32)
-    for row, side in enumerate((up_of(), *(sides[k].astype(F32) for k in (1, 0, 3, 2)))):
-        t0[lat, row : row + 1, :] = jnp.sum(centre * side, 0, keepdims=True)
-    tap1.start()
-    attended = acc_o[...].astype(BF)
-    early.load(0, lambda rows, cols: dot(attended[rows, :], gm_ref[:, cols]))
-    early.begin()
+    def middle():
+        mid_ref[...] = (
+            grid_ref[...].astype(F32) + dot(acc_o[...].T.astype(BF), wo_ref[...])
+        ).astype(BF)
+        edges(mid_ref[...], edge.at[1])
+        for copy in h_copies(1):
+            copy.start()
+        centre = mid_ref[...].astype(F32)
+        t0[lat] = jnp.zeros((8, D), F32)
+        for row, side in enumerate((up_of(), *(sides[k].astype(F32) for k in (1, 0, 3, 2)))):
+            t0[lat, row : row + 1, :] = jnp.sum(centre * side, 0, keepdims=True)
+        tap1.start()
+        attended = acc_o[...].astype(BF)
+        early.load(0, lambda rows, cols: dot(attended[rows, :], gm_ref[:, cols]))
+        early.begin()
 
     for i in range(1, n):
         x_copy(i).wait_send()
 
-    def differentiate(c, w, parts):
+    def differentiate(c, w, g):
         width = w * ROWS
         mark(c, w)
         rows = pl.ds(pl.multiple_of(c * ROWS, ROWS), width)
 
-        def pair(p, carry):
-            here = pl.ds(pl.multiple_of(p * 128, 128), 128)
-            there = pl.ds(pl.multiple_of(D + p * 128, 128), 128)
-            keys, values = kv[rows, here], kv[rows, there]
-            grad_k = grad_v = None
-            for e in range(2):
-                h = 2 * p + e
+        def four(q, carry):
+            for e in range(4):
+                h = 4 * q + e
+                pair = (2 * q + e // 2) * 128
                 mine = pl.ds(pl.multiple_of(h * HD, HD), HD)
+                also = pl.ds(pl.multiple_of(D + h * HD, HD), HD)
+                keys = kv[rows, pl.ds(pl.multiple_of(pair, 128), 128)]
+                values = kv[rows, pl.ds(pl.multiple_of(D + pair, 128), 128)]
                 weights = jnp.exp(dot(keys, qzt[h]) + masked(width) - m_ref[h])
                 grads = (weights * (dot(values, dozt[h]) - d_ref[h])).astype(BF)
-                part_k, part_v = dot(grads, qz[h]), dot(weights.astype(BF), doz[h])
-                grad_k = part_k if e == 0 else grad_k + part_k
-                grad_v = part_v if e == 0 else grad_v + part_v
-                total = acc_q[mine, :]
-                for k, g in enumerate(parts):
-                    span = min(width, 2 * ROWS)
-                    total = total + dot(kt[g, mine, :span], grads[k * span : (k + 1) * span, :])
-                acc_q[mine, :] = total
-            dkv[:width, here] = grad_k.astype(BF)
-            dkv[:width, there] = grad_v.astype(BF)
+                dkvt[mine, :width] = dot_nt(qt[mine, :], grads).astype(BF)
+                dkvt[also, :width] = dot_nt(dot_t[mine, :], weights.astype(BF)).astype(BF)
+                acc_q[mine, :] += dot(kt[g, mine, :width], grads)
             return carry
 
-        lax.fori_loop(0, HEADS // 2, pair, 0)
-        xt[:, :width] = xs[pl.ds(c, w), 0:ROWS, :].reshape(width, D).T
+        lax.fori_loop(0, HEADS // 4, four, 0)
 
         def weigh(j, carry):
-            cols = pl.ds(pl.multiple_of(j * 256, 256), 256)
-            dwkv[:, cols] += dot(xt[:, :width], dkv[:width, cols])
+            part = pl.ds(pl.multiple_of(j * 256, 256), 256)
+            tokens = xs[pl.ds(c, w), 0:ROWS, :].reshape(width, D)
+            dwt[part, :] += dot(dkvt[part, :width], tokens)
             return carry
 
         lax.fori_loop(0, 4, weigh, 0)
 
     def backward(step, carry):
         g = groups - step
-        differentiate(CAP * g - 1, 2, (g,))
+        differentiate(CAP * g - 1, 2, g)
 
         def turn(j, inner):
             cols = pl.ds(pl.multiple_of(j * 256, 256), 256)
-            part = dot(dkv[...], wkvt[:, cols]).astype(BF)
+            part = dot(wkv[cols, :], dkvt[...]).astype(BF).T
             send[pl.ds(CAP * g - 2, 2), 0:ROWS, cols] = part.reshape(2, ROWS, 256)
             return inner
 
@@ -467,6 +474,8 @@
                             g_copy(i).wait_recv()
                             g_onward(i).start()
 
+        pl.when(step == 0)(middle)
+
         @pl.when(step == 2)
         def _():
             tap1.wait()
@@ -482,17 +491,19 @@
         return carry
 
     lax.fori_loop(0, groups, backward, 0)
-    differentiate(0, 1, (0,))
+    differentiate(0, 1, 0)
 
     grad_q = (acc_q[...].T * SCALING).astype(BF)
     dwq = dot(grid_ref[...].T, grad_q)
     late.load(0, lambda rows, cols: dwq[rows, cols])
-    late.load(1, lambda rows, cols: dwkv[rows, cols])
-    late.load(2, lambda rows, cols: dwkv[rows, D + cols.start : D + cols.stop])
+    late.load(1, lambda rows, cols: dwt[cols, rows].astype(BF).T)
+    late.load(2, lambda rows, cols: dwt[D + cols.start : D + cols.stop, rows].astype(BF).T)
     late.begin()
     ggrid_ref[...] = (
-        gm_ref[...].astype(F32) + dot_nt(grad_q, wq_ref[...]) + dot(dkv[:CELLS, :], wkvt[...])
+        gm_ref[...].astype(F32) + dot_nt(grad_q, wq_ref[...])
+        + dot(wkv[...], dkvt[:, :CELLS]).T
     ).astype(BF)
+    late.step(0)
     for copy in h_copies(1):
         copy.wait_recv()
     north, south, west, east = around(mid_ref[...], halo.at[1], lat == 0, lat == nlat - 1)
@@ -500,8 +511,7 @@
         (1.0 + sten_ref[0:1, :]) * mid_ref[...].astype(F32) + sten_ref[1:2, :] * north
         + sten_ref[2:3, :] * south + sten_ref[3:4, :] * west + sten_ref[4:5, :] * east
     ).astype(BF)
-    late.step(0)
-
+    late.step(1)
     for i in range(1, n):
         if i < NEAR:
             g_copy(i).wait_recv()
@@ -509,10 +519,8 @@
             g_onward(i).wait_recv()
         g_copy(i).wait_send()
         if i >= NEAR:
-            x_onward(i).wait_send()
             g_onward(i).wait_send()
 
-    late.step(1)
 
     def unpack(b, carry):
         tile = dest_ref[0, b]
@@ -621,22 +629,19 @@
             pltpu.VMEM(((n + 1) * ROWS, 2 * D), BF),
             pltpu.VMEM((n // 2 + 1, D, 2 * ROWS), BF),
             pltpu.VMEM((D, 2 * ROWS), BF),
-            pltpu.VMEM((D, 2 * ROWS), BF),
             pltpu.VMEM((2 * ROWS, 128), F32),
             pltpu.VMEM((D, 2 * D), BF),
-            pltpu.VMEM((2 * D, D), BF),
-            pltpu.VMEM((HEADS, CELLS, 2 * HD), BF),
+            pltpu.VMEM((D, CELLS), BF),
             pltpu.VMEM((HEADS, 2 * HD, CELLS), BF),
-            pltpu.VMEM((HEADS, CELLS, 2 * HD), BF),
             pltpu.VMEM((HEADS, 2 * HD, CELLS), BF),
-            pltpu.VMEM((D, CELLS), F32),
+            pltpu.VMEM((D, CELLS), BF),
             pltpu.VMEM((D, CELLS), F32),
             pltpu.VMEM((D, CELLS), F32),
             pltpu.VMEM((HEADS, 1, CELLS), F32),
             pltpu.VMEM((HEADS, 1, CELLS), F32),
             pltpu.VMEM((HEADS, 1, CELLS), F32),
-            pltpu.VMEM((2 * ROWS, 2 * D), BF),
-            pltpu.VMEM((D, 2 * D), F32),
+            pltpu.VMEM((2 * D, 2 * ROWS), BF),
+            pltpu.VMEM((2 * D, D), F32),
             pltpu.VMEM((CELLS, D), BF),
             pltpu.VMEM((CELLS, D), BF),
             pltpu.VMEM((4, CELLS, D), BF),

time: 224 us -> 217 us (0.969)
  Pallas kernels: 223 us -> 216 us
    pallas_call x1, Pallas kernels: 217 us -> 210 us  [on_device(): pl.pallas_call(functools.partial(kernel, nlat, n), out_shape=(tile, jax.S...]
where the time goes in v4:
time: 217 us; the launch traced here: 216 us
  Pallas kernels  216 us (100%)
    pallas_call x1, Pallas kernels, on_device(): pl.pallas_call(functools.partial(kernel, nlat, n), out_shape=(tile, jax.S...  210 us
    pallas_call x1, Pallas kernels, on_device(): pl.pallas_call(write_kernel, out_shape=(tile, jax.ShapeDtypeStruct((block...  6.13 us

profile of v4, /device:TPU:1, one launch (start us, length us, event | category | flops | bytes accessed | tf_op | source)
XLA Modules:
  0.0 216.4 jit_solution(12992942013125433262)
XLA Ops:
  0.6 209.6 %encoder_step.1 = (bf16[256,512]{1,0:T(8,128)(2,1)}, bf16[16,128,512]{2,1,0:T(8,128)(2,1)}, bf16[256,512]{1,0:T(8,128)(2,1)}, bf16[2,4,16,3,16,128]{5,4,3,2,1,0:...) custom-call(s32[1,16]{1,0:T(1,128)} %bitcast.7, s32[1,16]{1,0:T(1,128)} %count_ref.1, ...), custom_call_target="tpu_custom_call" | custom-call | tf_op jit(solution)/shard_map/encoder_step/pallas_call | solution.py:613
  210.2 6.1 %write_results.1 = (bf16[256,512]{1,0:T(8,128)(2,1)}, bf16[16,128,512]{2,1,0:T(8,128)(2,1)}, bf16[256,512]{1,0:T(8,128)(2,1)}, f32[512,512]{1,0:T(8,128)}, f32[5...) custom-call(bf16[256,512]{1,0:T(8,128)(2,1)} %get-tuple-element.22.enc, ...), custom_call_target="tpu_custom_call" | custom-call | tf_op jit(solution)/shard_map/write_results/pallas_call | solution.py:666

commit v5 on v4

--- a/solution.py
+++ b/solution.py
@@ -78,10 +78,6 @@
         else:
             lax.fori_loop(1, self.count, step, 0)
 
-    def greet(self, barrier):
-        self.each(lambda at: pl.semaphore_signal(
-            barrier, inc=1, device_id=self.whom(at), device_id_type=MESH))
-
     def start(self):
         self.each(lambda at: self.copy(at, self.me).start())
 
@@ -107,52 +103,67 @@
 
 
 class MatrixSum:
-    def __init__(self, groups, scratch, out):
-        self.core, self.x, self.lon = (group[1] for group in groups)
-        self.counts = [group[0] for group in groups]
-        self.whole, self.got, self.half, self.got_half, self.piece, self.got_piece = scratch[:6]
+    def __init__(self, groups, buffers, sems, out):
+        self.me = [group[1] for group in groups]
+        self.bufs = buffers
         self.out = out
-        sems = scratch[6:]
-        self.stages = [
-            scatter(groups[0], self.whole, self.got, *sems[0:2]),
-            scatter(groups[1], self.half, self.got_half, *sems[2:4]),
-            scatter(groups[2], self.piece, self.got_piece, *sems[4:6]),
-            gather(groups[2], out.at[self.core, self.x], *sems[6:8]),
-            gather(groups[1], out.at[self.core], *sems[8:10]),
-            gather(groups[0], out, *sems[10:12]),
-        ]
-
-    def load(self, number, source):
+        at, self.stages = out, []
+        for k, group in enumerate(groups):
+            self.stages.append(scatter(group, buffers[2 * k], buffers[2 * k + 1], *sems[2 * k : 2 * k + 2]))
+        for k, group in enumerate(groups):
+            self.stages.insert(4, gather(group, at, *sems[8 + 2 * k : 10 + 2 * k]))
+            at = at.at[group[1]]
+        self.place = at
+
+    def load(self, source):
         per = D // 256
         for c in range(2):
             for x in range(4):
                 f = 4 * c + x
                 rows = slice((f % per) * 256, (f % per + 1) * 256)
                 cols = slice((f // per) * 128, (f // per + 1) * 128)
-                self.whole[c, x, :, number] = source(rows, cols).astype(BF).reshape(16, 16, 128)
-
-    def total(self, stage, own, got):
-        group = self.stages[stage]
-        held = own[group.me].astype(F32)
-        for o in range(1, group.count):
-            held = held + got[lax.rem(group.me + o, group.count)].astype(F32)
-        return held.astype(BF)
+                self.bufs[0][c, x] = source(rows, cols).astype(BF).reshape(4, 4, 16, 128)
 
     def begin(self):
         self.stages[0].start()
 
     def step(self, stage):
         self.stages[stage].wait()
-        if stage == 0:
-            for x in range(4):
-                self.half[x] = (
-                    self.whole[self.core, x].astype(F32) + self.got[1 - self.core, x].astype(F32)
-                ).astype(BF)
-        elif stage == 1:
-            self.piece[...] = self.total(1, self.half, self.got_half)
-        elif stage == 2:
-            self.out[self.core, self.x, self.lon] = self.total(2, self.piece, self.got_piece)
-        if stage < 5:
+        if stage < 4:
+            me, count = self.me[stage], self.stages[stage].count
+            own, got = self.bufs[2 * stage], self.bufs[2 * stage + 1]
+            held = own[me].astype(F32)
+            for o in range(1, count):
+                held = held + got[lax.rem(me + o, count)].astype(F32)
+            target = self.place if stage == 3 else self.bufs[2 * stage + 2]
+            target[...] = held.astype(BF)
+        if stage < 7:
+            self.stages[stage + 1].start()
+
+    def close(self):
+        for stage in self.stages:
+            stage.sent()
+
+
+class TapSum:
+    def __init__(self, groups, buffers, sems):
+        self.bufs = buffers
+        self.stages = [
+            gather(group, buffers[k], *sems[2 * k : 2 * k + 2]) for k, group in enumerate(groups)
+        ]
+
+    def begin(self):
+        self.stages[0].start()
+
+    def step(self, stage, out=None):
+        self.stages[stage].wait()
+        total = self.bufs[stage][0]
+        for k in range(1, self.stages[stage].count):
+            total = total + self.bufs[stage][k]
+        if stage == 3:
+            out[...] = total
+        else:
+            self.bufs[stage + 1][self.stages[stage + 1].me] = total
             self.stages[stage + 1].start()
 
     def close(self):
@@ -164,26 +175,28 @@
     nlat, n, dest_ref, count_ref, obs_ref, grid_ref, cot_ref, wq_ref, wk_ref, wv_ref, wo_ref, sten_ref,
     enc_ref, gobs_ref, ggrid_ref, late_ref, early_ref, taps_ref,
     send, xs, ret, relay, relay_back, kv, kt, vt, bias, wkv, qt, qzt, dozt, dot_t,
-    acc_o, acc_q, m_ref, l_ref, d_ref, dkvt, dwt, gm_ref, mid_ref, sides, edge, halo, t0, t1,
-    x_ssem, x_rsem, r_ssem, r_rsem, g_ssem, g_rsem, b_ssem, b_rsem, h_ssem, h_rsem, t1s, t1r, t2s, t2r,
+    acc_o, acc_q, m_ref, l_ref, d_ref, dkvt, dwt, gm_ref, mid_ref, sides, edge, halo,
+    x_ssem, x_rsem, r_ssem, r_rsem, g_ssem, g_rsem, b_ssem, b_rsem, h_ssem, h_rsem,
     *sum_scratch,
 ):
     lat, me = lax.axis_index("lat"), lax.axis_index("lon")
     groups = n // 2
     blocks = obs_ref.shape[0]
     x_at, core = lat // 2, lax.rem(lat, 2)
-    rings = (
-        (2, core, lambda at: {"lat": 2 * x_at + at}),
-        (nlat // 2, x_at, lambda at: {"lat": 2 * at + core}),
-        (n, me, lambda at: {"lon": at}),
+    y, z = me // SIDE, lax.rem(me, SIDE)
+    on_core = (2, core, lambda at: {"lat": 2 * x_at + at})
+    on_x = (SIDE, x_at, lambda at: {"lat": 2 * at + core})
+    on_y = (SIDE, y, lambda at: {"lon": at * SIDE + z})
+    on_z = (SIDE, z, lambda at: {"lon": y * SIDE + at})
+    orders = ((on_x, on_y, on_z), (on_y, on_z, on_x), (on_z, on_x, on_y), (on_x, on_y, on_z))
+    *late, early = (
+        MatrixSum(
+            (on_core, *order), sum_scratch[24 * k : 24 * k + 8], sum_scratch[24 * k + 8 : 24 * k + 24],
+            late_ref.at[k] if k < 3 else early_ref)
+        for k, order in enumerate(orders)
     )
-    half = len(sum_scratch) // 2
-    late = MatrixSum(rings, sum_scratch[:half], late_ref)
-    early = MatrixSum(rings, sum_scratch[half:], early_ref)
-    tap1 = gather((nlat, lat, lambda at: {"lat": at}), t0, t1s, t1r)
-    tap2 = gather(rings[2], t1, t2s, t2r)
-
-    y, z = me // SIDE, lax.rem(me, SIDE)
+    tap_sum = TapSum((on_core, on_x, on_y, on_z), sum_scratch[96:100], sum_scratch[100:108])
+
     way_y, way_z = 1 - 2 * lax.rem(y, 2), 1 - 2 * lax.rem(z, 2)
 
     def place(dy, dz):
@@ -203,8 +216,13 @@
             -turned(i) * way_y if dy == 2 else 0, -turned(i) * way_z if dz == 2 else 0)}
 
     barrier = pltpu.get_barrier_semaphore()
-    for group in (tap1, tap2):
-        group.greet(barrier)
+    def greet(o, carry, axis, count, at):
+        pl.semaphore_signal(
+            barrier, inc=1, device_id={axis: lax.rem(at + o, count)}, device_id_type=MESH)
+        return carry
+
+    lax.fori_loop(1, nlat, functools.partial(greet, axis="lat", count=nlat, at=lat), 0)
+    lax.fori_loop(1, n, functools.partial(greet, axis="lon", count=n, at=me), 0)
 
     row_ids = lax.broadcasted_iota(jnp.int32, (EXTRA, D), 0)
 
@@ -407,12 +425,13 @@
         for copy in h_copies(1):
             copy.start()
         centre = mid_ref[...].astype(F32)
-        t0[lat] = jnp.zeros((8, D), F32)
+        terms = tap_sum.bufs[0]
+        terms[core] = jnp.zeros((8, D), F32)
         for row, side in enumerate((up_of(), *(sides[k].astype(F32) for k in (1, 0, 3, 2)))):
-            t0[lat, row : row + 1, :] = jnp.sum(centre * side, 0, keepdims=True)
-        tap1.start()
+            terms[core, row : row + 1, :] = jnp.sum(centre * side, 0, keepdims=True)
+        tap_sum.begin()
         attended = acc_o[...].astype(BF)
-        early.load(0, lambda rows, cols: dot(attended[rows, :], gm_ref[:, cols]))
+        early.load(lambda rows, cols: dot(attended[rows, :], gm_ref[:, cols]))
         early.begin()
 
     for i in range(1, n):
@@ -476,17 +495,10 @@
 
         pl.when(step == 0)(middle)
 
-        @pl.when(step == 2)
-        def _():
-            tap1.wait()
-            total = t0[0]
-            for i in range(1, nlat):
-                total = total + t0[i]
-            t1[me] = total
-            tap2.start()
-
-        for stage in range(5):
+        for stage in range(6):
             pl.when(step == stage + 2)(functools.partial(early.step, stage))
+        for stage in range(3):
+            pl.when(step == stage + 3)(functools.partial(tap_sum.step, stage))
 
         return carry
 
@@ -495,15 +507,21 @@
 
     grad_q = (acc_q[...].T * SCALING).astype(BF)
     dwq = dot(grid_ref[...].T, grad_q)
-    late.load(0, lambda rows, cols: dwq[rows, cols])
-    late.load(1, lambda rows, cols: dwt[cols, rows].astype(BF).T)
-    late.load(2, lambda rows, cols: dwt[D + cols.start : D + cols.stop, rows].astype(BF).T)
-    late.begin()
+    late[0].load(lambda rows, cols: dwq[rows, cols])
+    late[1].load(lambda rows, cols: dwt[cols, rows].astype(BF).T)
+    late[2].load(lambda rows, cols: dwt[D + cols.start : D + cols.stop, rows].astype(BF).T)
+    for part in late:
+        part.begin()
+
+    def late_step(stage):
+        for part in late:
+            part.step(stage)
+
     ggrid_ref[...] = (
         gm_ref[...].astype(F32) + dot_nt(grad_q, wq_ref[...])
         + dot(wkv[...], dkvt[:, :CELLS]).T
     ).astype(BF)
-    late.step(0)
+    late_step(0)
     for copy in h_copies(1):
         copy.wait_recv()
     north, south, west, east = around(mid_ref[...], halo.at[1], lat == 0, lat == nlat - 1)
@@ -511,7 +529,7 @@
         (1.0 + sten_ref[0:1, :]) * mid_ref[...].astype(F32) + sten_ref[1:2, :] * north
         + sten_ref[2:3, :] * south + sten_ref[3:4, :] * west + sten_ref[4:5, :] * east
     ).astype(BF)
-    late.step(1)
+    late_step(1)
     for i in range(1, n):
         if i < NEAR:
             g_copy(i).wait_recv()
@@ -536,20 +554,17 @@
         gobs_ref[b] = jnp.where(rank == 0, both[:BLK], both[BLK:])
         return carry
 
+    late_step(2)
     lax.fori_loop(0, blocks, unpack, 0)
-    late.step(2)
-    tap2.wait()
-    total = t1[0]
-    for i in range(1, n):
-        total = total + t1[i]
-    taps_ref[...] = total
-    late.step(3)
-    early.step(5)
-    late.step(4)
-    late.step(5)
-    for part in (tap1, tap2):
-        part.sent()
-    for part in (early, late):
+    late_step(3)
+    tap_sum.step(3, taps_ref)
+    early.step(6)
+    late_step(4)
+    early.step(7)
+    for stage in range(5, 8):
+        late_step(stage)
+    tap_sum.close()
+    for part in (early, *late):
         part.close()
     for which in range(2):
         for copy in h_copies(which):
@@ -573,13 +588,13 @@
         load.start()
     taps_o[...] = taps[0:5, :]
     loads[0].wait()
-    for k, (out, source, number) in enumerate(
-            ((wq, late_v, 0), (wk, late_v, 1), (wv, late_v, 2), (wo, early_v, 0))):
+    for out, source, k in (
+            (wq, late_v.at[0], 0), (wk, late_v.at[1], 1), (wv, late_v.at[2], 2), (wo, early_v, 3)):
         if k == 3:
             loads[1].wait()
         for f in range(8):
             rows, cols = slice((f % 2) * 256, (f % 2 + 1) * 256), slice((f // 2) * 128, (f // 2 + 1) * 128)
-            sums_v[k, rows, cols] = source[f // 4, f % 4, :, number].reshape(256, 128).astype(F32)
+            sums_v[k, rows, cols] = source[f // 4, f % 4].reshape(256, 128).astype(F32)
         store(sums_v.at[k], out)
         if k < 3:
             loads[2 + k].wait()
@@ -597,25 +612,24 @@
     nlat, n = lax.axis_size("lat"), lax.axis_size("lon")
     vmem = pl.BlockSpec(memory_space=pltpu.VMEM)
     smem = pl.BlockSpec(memory_space=pltpu.SMEM)
-    lat_sem, lon_sem = pltpu.SemaphoreType.DMA((nlat,)), pltpu.SemaphoreType.DMA((n,))
+    lon_sem = pltpu.SemaphoreType.DMA((n,))
     far_sem = pltpu.SemaphoreType.DMA((n - NEAR,))
     halo_sem = pltpu.SemaphoreType.DMA((2, 4))
-    x_sem, core_sem = pltpu.SemaphoreType.DMA((nlat // 2,)), pltpu.SemaphoreType.DMA((2,))
+    ring_sem, core_sem = pltpu.SemaphoreType.DMA((SIDE,)), pltpu.SemaphoreType.DMA((2,))
+    sems = [core_sem] * 2 + [ring_sem] * 6
     sums = []
-    for number in (3, 1):
-        whole, part, piece = (
-            pltpu.VMEM((*lead, number, 16, 128), BF) for lead in ((2, nlat // 2, n), (nlat // 2, n), (n,))
-        )
-        sums += [whole, whole, part, part, piece, piece]
-        sums += [core_sem, core_sem, x_sem, x_sem, lon_sem, lon_sem]
-        sums += [lon_sem, lon_sem, x_sem, x_sem, core_sem, core_sem]
+    for _ in range(4):
+        for lead in ((2, SIDE, SIDE, SIDE), (SIDE,) * 3, (SIDE,) * 2, (SIDE,)):
+            sums += [pltpu.VMEM((*lead, 16, 128), BF)] * 2
+        sums += sems * 2
+    sums += [pltpu.VMEM((2, 8, D), F32)] + [pltpu.VMEM((SIDE, 8, D), F32)] * 3 + sems
     tile = jax.ShapeDtypeStruct((CELLS, D), BF)
     results = pl.pallas_call(
         functools.partial(kernel, nlat, n),
         out_shape=(
             tile, jax.ShapeDtypeStruct((blocks, BLK, D), BF), tile,
-            jax.ShapeDtypeStruct((2, nlat // 2, n, 3, 16, 128), BF),
-            jax.ShapeDtypeStruct((2, nlat // 2, n, 1, 16, 128), BF),
+            jax.ShapeDtypeStruct((3, 2, SIDE, SIDE, SIDE, 16, 128), BF),
+            jax.ShapeDtypeStruct((2, SIDE, SIDE, SIDE, 16, 128), BF),
             jax.ShapeDtypeStruct((8, D), F32),
         ),
         in_specs=[smem] * 2 + [vmem] * 8,
@@ -647,10 +661,7 @@
             pltpu.VMEM((4, CELLS, D), BF),
             pltpu.VMEM((2, 4, TILE, D), BF),
             pltpu.VMEM((2, 4, TILE, D), BF),
-            pltpu.VMEM((nlat, 8, D), F32),
-            pltpu.VMEM((n, 8, D), F32),
             lon_sem, lon_sem, far_sem, far_sem, lon_sem, lon_sem, far_sem, far_sem, halo_sem, halo_sem,
-            lat_sem, lat_sem, lon_sem, lon_sem,
             *sums,
         ],
         compiler_params=pltpu.CompilerParams(
@@ -673,7 +684,7 @@
         out_specs=(anywhere,) * 7 + (vmem,),
         scratch_shapes=[
             pltpu.VMEM((CELLS, D), BF), pltpu.VMEM((blocks, BLK, D), BF), pltpu.VMEM((CELLS, D), BF),
-            pltpu.VMEM((2, nlat // 2, n, 3, 16, 128), BF), pltpu.VMEM((2, nlat // 2, n, 1, 16, 128), BF),
+            pltpu.VMEM((3, 2, SIDE, SIDE, SIDE, 16, 128), BF), pltpu.VMEM((2, SIDE, SIDE, SIDE, 16, 128), BF),
             pltpu.VMEM((4, D, D), F32), pltpu.SemaphoreType.DMA((5,)), pltpu.SemaphoreType.DMA((7,)),
         ],
         compiler_params=pltpu.CompilerParams(vmem_limit_bytes=62 * 2**20),

time: 217 us -> 209 us (0.963)
  Pallas kernels: 216 us -> 208 us
    pallas_call x1, Pallas kernels: 210 us -> 202 us  [on_device(): pl.pallas_call(functools.partial(kernel, nlat, n), out_shape=(tile, jax.S...]
where the time goes in v5:
time: 209 us
  Pallas kernels  208 us (100%)
    pallas_call x1, Pallas kernels, on_device(): pl.pallas_call(functools.partial(kernel, nlat, n), out_shape=(tile, jax.S...  202 us
    pallas_call x1, Pallas kernels, on_device(): pl.pallas_call(write_kernel, out_shape=(tile, jax.ShapeDtypeStruct((block...  6.13 us

profile of v5, /device:TPU:1, one launch (start us, length us, event | category | flops | bytes accessed | tf_op | source)
XLA Modules:
  0.0 208.9 jit_solution(7384042905639965140)
XLA Ops:
  0.6 202.1 %encoder_step.1 = (bf16[256,512]{1,0:T(8,128)(2,1)}, bf16[16,128,512]{2,1,0:T(8,128)(2,1)}, bf16[256,512]{1,0:T(8,128)(2,1)}, bf16[3,2,4,4,4,16,128]{6,5,4,3,2,1...) custom-call(s32[1,16]{1,0:T(1,128)} %bitcast.7, s32[1,16]{1,0:T(1,128)} %count_ref.1, ...), custom_call_target="tpu_custom_call" | custom-call | tf_op jit(solution)/shard_map/encoder_step/pallas_call | solution.py:627
  202.7 6.1 %write_results.1 = (bf16[256,512]{1,0:T(8,128)(2,1)}, bf16[16,128,512]{2,1,0:T(8,128)(2,1)}, bf16[256,512]{1,0:T(8,128)(2,1)}, f32[512,512]{1,0:T(8,128)}, f32[5...) custom-call(bf16[256,512]{1,0:T(8,128)(2,1)} %get-tuple-element.22.enc, ...), custom_call_target="tpu_custom_call" | custom-call | tf_op jit(solution)/shard_map/write_results/pallas_call | solution.py:677

commit v6 on v5

--- a/solution.py
+++ b/solution.py
@@ -139,10 +139,7 @@
             target[...] = held.astype(BF)
         if stage < 7:
             self.stages[stage + 1].start()
-
-    def close(self):
-        for stage in self.stages:
-            stage.sent()
+        self.stages[stage].sent()
 
 
 class TapSum:
@@ -165,10 +162,7 @@
         else:
             self.bufs[stage + 1][self.stages[stage + 1].me] = total
             self.stages[stage + 1].start()
-
-    def close(self):
-        for stage in self.stages:
-            stage.sent()
+        self.stages[stage].sent()
 
 
 def kernel(
@@ -487,18 +481,17 @@
                 else:
                     ret[0] = send[0, 0:ROWS, :]
                 g_copy(first + 1).start()
-                if k >= 2:
-                    for i in (first + 4, first + 5):
+                if k >= 4:
+                    for i in (first + 8, first + 9):
                         if i >= NEAR:
                             g_copy(i).wait_recv()
                             g_onward(i).start()
 
         pl.when(step == 0)(middle)
 
-        for stage in range(6):
-            pl.when(step == stage + 2)(functools.partial(early.step, stage))
         for stage in range(3):
-            pl.when(step == stage + 3)(functools.partial(tap_sum.step, stage))
+            pl.when(step == 2 * stage + 2)(functools.partial(early.step, stage))
+            pl.when(step == 2 * stage + 3)(functools.partial(tap_sum.step, stage))
 
         return carry
 
@@ -512,8 +505,11 @@
     late[2].load(lambda rows, cols: dwt[D + cols.start : D + cols.stop, rows].astype(BF).T)
     for part in late:
         part.begin()
+    early.step(3)
 
     def late_step(stage):
+        if stage < 4:
+            early.step(stage + 4)
         for part in late:
             part.step(stage)
 
@@ -558,14 +554,8 @@
     lax.fori_loop(0, blocks, unpack, 0)
     late_step(3)
     tap_sum.step(3, taps_ref)
-    early.step(6)
-    late_step(4)
-    early.step(7)
-    for stage in range(5, 8):
+    for stage in range(4, 8):
         late_step(stage)
-    tap_sum.close()
-    for part in (early, *late):
-        part.close()
     for which in range(2):
         for copy in h_copies(which):
             copy.wait_send()

time: 209 us -> 201 us (0.962)
  Pallas kernels: 208 us -> 200 us
    pallas_call x1, Pallas kernels: 202 us -> 194 us  [on_device(): pl.pallas_call(functools.partial(kernel, nlat, n), out_shape=(tile, jax.S...]
where the time goes in v6:
time: 201 us
  Pallas kernels  200 us (100%)
    pallas_call x1, Pallas kernels, on_device(): pl.pallas_call(functools.partial(kernel, nlat, n), out_shape=(tile, jax.S...  194 us
    pallas_call x1, Pallas kernels, on_device(): pl.pallas_call(write_kernel, out_shape=(tile, jax.ShapeDtypeStruct((block...  6.13 us

profile of v6, /device:TPU:1, one launch (start us, length us, event | category | flops | bytes accessed | tf_op | source)
XLA Modules:
  0.0 200.9 jit_solution(11623882001366598177)
XLA Ops:
  0.6 194.1 %encoder_step.1 = (bf16[256,512]{1,0:T(8,128)(2,1)}, bf16[16,128,512]{2,1,0:T(8,128)(2,1)}, bf16[256,512]{1,0:T(8,128)(2,1)}, bf16[3,2,4,4,4,16,128]{6,5,4,3,2,1...) custom-call(s32[1,16]{1,0:T(1,128)} %bitcast.7, s32[1,16]{1,0:T(1,128)} %count_ref.1, ...), custom_call_target="tpu_custom_call" | custom-call | tf_op jit(solution)/shard_map/encoder_step/pallas_call | solution.py:617
  194.8 6.1 %write_results.1 = (bf16[256,512]{1,0:T(8,128)(2,1)}, bf16[16,128,512]{2,1,0:T(8,128)(2,1)}, bf16[256,512]{1,0:T(8,128)(2,1)}, f32[512,512]{1,0:T(8,128)}, f32[5...) custom-call(bf16[256,512]{1,0:T(8,128)(2,1)} %get-tuple-element.22.enc, ...), custom_call_target="tpu_custom_call" | custom-call | tf_op jit(solution)/shard_map/write_results/pallas_call | solution.py:667

commit v7 on v6

--- a/solution.py
+++ b/solution.py
@@ -19,10 +19,13 @@
 MESH = pl.DeviceIdType.MESH
 SIDE = 4
 STEPS = (
-    (0, 0), (0, 1), (0, 3), (1, 0), (3, 0), (1, 1), (1, 3), (3, 1), (3, 3),
+    (0, 0), (0, 1), (0, 3), (1, 0), (3, 0),
     (0, 2), (2, 0), (1, 2), (3, 2), (2, 1), (2, 3), (2, 2),
+    (1, 1), (1, 3), (3, 1), (3, 3),
 )
-NEXT, NEAR = 5, 9
+FAR = range(5, 12)
+DIAGONAL = range(12, 16)
+BACK = (6, 5, 4, 3, 8, 7, 2, 1)
 EXTRA = 16
 BF = jnp.bfloat16
 F32 = jnp.float32
@@ -166,16 +169,28 @@
 
 
 def kernel(
-    nlat, n, dest_ref, count_ref, obs_ref, grid_ref, cot_ref, wq_ref, wk_ref, wv_ref, wo_ref, sten_ref,
-    enc_ref, gobs_ref, ggrid_ref, late_ref, early_ref, taps_ref,
+    nlat, n, dest_ref, count_ref, grid_ref, cot_ref, sten_ref, obs_in, wq_in, wk_in, wv_in, wo_in,
+    enc_out, gobs_out, ggrid_out, late_ref, early_ref, taps_ref,
     send, xs, ret, relay, relay_back, kv, kt, vt, bias, wkv, qt, qzt, dozt, dot_t,
     acc_o, acc_q, m_ref, l_ref, d_ref, dkvt, dwt, gm_ref, mid_ref, sides, edge, halo,
+    obs_ref, wq_ref, wo_ref, enc_ref, gobs_ref, ggrid_ref, in_sem, out_sem,
     x_ssem, x_rsem, r_ssem, r_rsem, g_ssem, g_rsem, b_ssem, b_rsem, h_ssem, h_rsem,
     *sum_scratch,
 ):
     lat, me = lax.axis_index("lat"), lax.axis_index("lon")
     groups = n // 2
     blocks = obs_ref.shape[0]
+    loads = [
+        pltpu.make_async_copy(source, target, in_sem.at[k])
+        for k, (source, target) in enumerate((
+            (obs_in, obs_ref), (wq_in, wq_ref), (wk_in, wkv.at[:, pl.ds(0, D)]),
+            (wv_in, wkv.at[:, pl.ds(D, D)]), (wo_in, wo_ref)))
+    ]
+    stores = [
+        pltpu.make_async_copy(source, target, out_sem.at[k])
+        for k, (source, target) in enumerate((
+            (ggrid_ref, ggrid_out), (enc_ref, enc_out), (gobs_ref, gobs_out)))
+    ]
     x_at, core = lat // 2, lax.rem(lat, 2)
     y, z = me // SIDE, lax.rem(me, SIDE)
     on_core = (2, core, lambda at: {"lat": 2 * x_at + at})
@@ -209,6 +224,8 @@
         return {"lon": place(
             -turned(i) * way_y if dy == 2 else 0, -turned(i) * way_z if dz == 2 else 0)}
 
+    for load in loads:
+        load.start()
     barrier = pltpu.get_barrier_semaphore()
     def greet(o, carry, axis, count, at):
         pl.semaphore_signal(
@@ -234,6 +251,7 @@
         send[i, ROWS:, :] = jnp.where(row_ids == 0, c0, c1).astype(F32).astype(BF)
 
     edges(cot_ref[...], edge.at[0])
+    loads[0].wait()
     pl.semaphore_wait(barrier, nlat + n - 2)
 
     def remote(src, dst, ssem, rsem, whom):
@@ -241,24 +259,24 @@
             src_ref=src, dst_ref=dst, send_sem=ssem, recv_sem=rsem, device_id=whom, device_id_type=MESH)
 
     def x_copy(i):
-        if i < NEAR:
+        if i not in FAR:
             return remote(send.at[i], xs.at[i + 1], x_ssem.at[i], x_rsem.at[i], leg(i, 1))
-        j = i - NEAR
+        j = i - FAR.start
         return remote(send.at[i], relay.at[j], x_ssem.at[i], r_rsem.at[j], leg(i, 1))
 
     def x_onward(i):
-        j = i - NEAR
+        j = i - FAR.start
         return remote(relay.at[j], xs.at[i + 1], r_ssem.at[j], x_rsem.at[i], onward(i))
 
     def g_copy(i):
         tokens = send.at[i, pl.ds(0, ROWS)]
-        if i < NEAR:
+        if i not in FAR:
             return remote(tokens, ret.at[i], g_ssem.at[i], g_rsem.at[i], leg(i, -1))
-        j = i - NEAR
+        j = i - FAR.start
         return remote(tokens, relay_back.at[j], g_ssem.at[i], b_rsem.at[j], leg(i, -1))
 
     def g_onward(i):
-        j = i - NEAR
+        j = i - FAR.start
         return remote(relay_back.at[j], ret.at[i], b_ssem.at[j], g_rsem.at[i], onward(i))
 
     def x_arrived(i):
@@ -277,15 +295,15 @@
     for copy in h_copies(0):
         copy.start()
 
-    for i in (*range(NEAR, n), *range(1, NEXT)):
+    for i in (*FAR, *range(1, FAR.start)):
         pack(i)
         x_copy(i).start()
     pack(0)
 
     xs[0, 0:ROWS, :] = grid_ref[...]
     xs[1] = send[0]
-    wkv[:, :D] = wk_ref[...]
-    wkv[:, D:] = wv_ref[...]
+    for load in loads[1:]:
+        load.wait()
     lanes = lax.broadcasted_iota(jnp.int32, (CELLS, 2 * HD), 1)
     queries = dot(grid_ref[...], wq_ref[...]).astype(BF).astype(F32) * SCALING
     for copy in h_copies(0):
@@ -368,23 +386,22 @@
     project(0, 1, 0)
     attend(0, 1)
 
-    for i in range(NEAR, n):
+    for i in FAR:
         x_copy(i).wait_recv()
         x_onward(i).start()
 
-    for i in range(NEXT, NEAR):
+    for i in DIAGONAL:
         pack(i)
 
     def forward(step, carry):
-        second, third = (step + 6) // 8, (step + 3) // 8
-        g = step + 1 + 3 * second + third * (6 - 2 * step)
+        g = step + 1
         c = CAP * g - 1
 
         @pl.when(step == 2)
         def _():
-            for i in range(NEAR, n):
+            for i in FAR:
                 x_onward(i).wait_send()
-            for i in range(NEXT, NEAR):
+            for i in DIAGONAL:
                 x_copy(i).start()
 
         @pl.when(step >= 1)
@@ -462,7 +479,7 @@
         lax.fori_loop(0, 4, weigh, 0)
 
     def backward(step, carry):
-        g = groups - step
+        g = 6 - step + 6 * ((step + 4) // 8) - 4 * ((step + 2) // 8)
         differentiate(CAP * g - 1, 2, g)
 
         def turn(j, inner):
@@ -475,21 +492,21 @@
         for k in range(groups):
             @pl.when(step == k)
             def _(k=k):
-                first = CAP * (groups - k) - 2
+                first = CAP * BACK[k] - 2
                 if first:
                     g_copy(first).start()
                 else:
                     ret[0] = send[0, 0:ROWS, :]
                 g_copy(first + 1).start()
                 if k >= 4:
-                    for i in (first + 8, first + 9):
-                        if i >= NEAR:
+                    for i in (CAP * BACK[k - 4] - 2, CAP * BACK[k - 4] - 1):
+                        if i in FAR:
                             g_copy(i).wait_recv()
                             g_onward(i).start()
 
         pl.when(step == 0)(middle)
 
-        for stage in range(3):
+        for stage in range(2):
             pl.when(step == 2 * stage + 2)(functools.partial(early.step, stage))
             pl.when(step == 2 * stage + 3)(functools.partial(tap_sum.step, stage))
 
@@ -505,11 +522,11 @@
     late[2].load(lambda rows, cols: dwt[D + cols.start : D + cols.stop, rows].astype(BF).T)
     for part in late:
         part.begin()
-    early.step(3)
+    tap_sum.step(2)
 
     def late_step(stage):
-        if stage < 4:
-            early.step(stage + 4)
+        if stage < 6:
+            early.step(stage + 2)
         for part in late:
             part.step(stage)
 
@@ -517,6 +534,7 @@
         gm_ref[...].astype(F32) + dot_nt(grad_q, wq_ref[...])
         + dot(wkv[...], dkvt[:, :CELLS]).T
     ).astype(BF)
+    stores[0].start()
     late_step(0)
     for copy in h_copies(1):
         copy.wait_recv()
@@ -525,14 +543,15 @@
         (1.0 + sten_ref[0:1, :]) * mid_ref[...].astype(F32) + sten_ref[1:2, :] * north
         + sten_ref[2:3, :] * south + sten_ref[3:4, :] * west + sten_ref[4:5, :] * east
     ).astype(BF)
+    stores[1].start()
     late_step(1)
     for i in range(1, n):
-        if i < NEAR:
+        if i not in FAR:
             g_copy(i).wait_recv()
         else:
             g_onward(i).wait_recv()
         g_copy(i).wait_send()
-        if i >= NEAR:
+        if i in FAR:
             g_onward(i).wait_send()
 
 
@@ -552,6 +571,7 @@
 
     late_step(2)
     lax.fori_loop(0, blocks, unpack, 0)
+    stores[2].start()
     late_step(3)
     tap_sum.step(3, taps_ref)
     for stage in range(4, 8):
@@ -559,36 +579,47 @@
     for which in range(2):
         for copy in h_copies(which):
             copy.wait_send()
+    for copy in stores:
+        copy.wait()
 
 
 def write_kernel(
     enc, gobs, ggrid, late, early, taps, enc_o, gobs_o, ggrid_o, wq, wk, wv, wo, taps_o,
     enc_v, gobs_v, ggrid_v, late_v, early_v, sums_v, in_sems, out_sems,
 ):
-    pairs = ((late, late_v, None), (early, early_v, None), (gobs, gobs_v, gobs_o), (enc, enc_v, enc_o),
-             (ggrid, ggrid_v, ggrid_o))
-    loads = [pltpu.make_async_copy(a, b, in_sems.at[k]) for k, (a, b, _) in enumerate(pairs)]
-    stores = []
+    part = gobs.shape[0] // 4
+    loads, stores = [], []
+
+    def load(source, target):
+        loads.append(pltpu.make_async_copy(source, target, in_sems.at[len(loads)]))
+        loads[-1].start()
 
     def store(source, out):
         stores.append(pltpu.make_async_copy(source, out, out_sems.at[len(stores)]))
         stores[-1].start()
 
-    for load in loads:
-        load.start()
+    load(early, early_v)
+    for k in range(3):
+        load(late.at[k], late_v.at[k])
+    for k in range(4):
+        load(gobs.at[pl.ds(k * part, part)], gobs_v.at[pl.ds(k * part, part)])
+    load(enc, enc_v)
+    load(ggrid, ggrid_v)
     taps_o[...] = taps[0:5, :]
-    loads[0].wait()
-    for out, source, k in (
-            (wq, late_v.at[0], 0), (wk, late_v.at[1], 1), (wv, late_v.at[2], 2), (wo, early_v, 3)):
-        if k == 3:
-            loads[1].wait()
+    for k, (out, source) in enumerate(
+            ((wo, early_v), (wq, late_v.at[0]), (wk, late_v.at[1]), (wv, late_v.at[2]))):
+        loads[k].wait()
         for f in range(8):
             rows, cols = slice((f % 2) * 256, (f % 2 + 1) * 256), slice((f // 2) * 128, (f // 2 + 1) * 128)
             sums_v[k, rows, cols] = source[f // 4, f % 4].reshape(256, 128).astype(F32)
         store(sums_v.at[k], out)
-        if k < 3:
-            loads[2 + k].wait()
-            store(pairs[2 + k][1], pairs[2 + k][2])
+    for k in range(4):
+        loads[4 + k].wait()
+        store(gobs_v.at[pl.ds(k * part, part)], gobs_o.at[pl.ds(k * part, part)])
+    loads[8].wait()
+    store(enc_v, enc_o)
+    loads[9].wait()
+    store(ggrid_v, ggrid_o)
     for copy in stores:
         copy.wait()
 
@@ -602,8 +633,9 @@
     nlat, n = lax.axis_size("lat"), lax.axis_size("lon")
     vmem = pl.BlockSpec(memory_space=pltpu.VMEM)
     smem = pl.BlockSpec(memory_space=pltpu.SMEM)
+    anywhere = pl.BlockSpec(memory_space=pl.ANY)
     lon_sem = pltpu.SemaphoreType.DMA((n,))
-    far_sem = pltpu.SemaphoreType.DMA((n - NEAR,))
+    far_sem = pltpu.SemaphoreType.DMA((len(FAR),))
     halo_sem = pltpu.SemaphoreType.DMA((2, 4))
     ring_sem, core_sem = pltpu.SemaphoreType.DMA((SIDE,)), pltpu.SemaphoreType.DMA((2,))
     sems = [core_sem] * 2 + [ring_sem] * 6
@@ -622,14 +654,14 @@
             jax.ShapeDtypeStruct((2, SIDE, SIDE, SIDE, 16, 128), BF),
             jax.ShapeDtypeStruct((8, D), F32),
         ),
-        in_specs=[smem] * 2 + [vmem] * 8,
-        out_specs=(vmem,) * 6,
+        in_specs=[smem] * 2 + [vmem] * 3 + [anywhere] * 5,
+        out_specs=(anywhere,) * 3 + (vmem,) * 3,
         scratch_shapes=[
             pltpu.VMEM((n, ROWS + EXTRA, D), BF),
             pltpu.VMEM((n + 1, ROWS + EXTRA, D), BF),
             pltpu.VMEM((n, ROWS, D), BF),
-            pltpu.VMEM((n - NEAR, ROWS + EXTRA, D), BF),
-            pltpu.VMEM((n - NEAR, ROWS, D), BF),
+            pltpu.VMEM((len(FAR), ROWS + EXTRA, D), BF),
+            pltpu.VMEM((len(FAR), ROWS, D), BF),
             pltpu.VMEM(((n + 1) * ROWS, 2 * D), BF),
             pltpu.VMEM((n // 2 + 1, D, 2 * ROWS), BF),
             pltpu.VMEM((D, 2 * ROWS), BF),
@@ -651,6 +683,14 @@
             pltpu.VMEM((4, CELLS, D), BF),
             pltpu.VMEM((2, 4, TILE, D), BF),
             pltpu.VMEM((2, 4, TILE, D), BF),
+            pltpu.VMEM((blocks, BLK, D), BF),
+            pltpu.VMEM((D, D), BF),
+            pltpu.VMEM((D, D), BF),
+            pltpu.VMEM((CELLS, D), BF),
+            pltpu.VMEM((blocks, BLK, D), BF),
+            pltpu.VMEM((CELLS, D), BF),
+            pltpu.SemaphoreType.DMA((5,)),
+            pltpu.SemaphoreType.DMA((3,)),
             lon_sem, lon_sem, far_sem, far_sem, lon_sem, lon_sem, far_sem, far_sem, halo_sem, halo_sem,
             *sums,
         ],
@@ -659,10 +699,9 @@
         ),
         name="encoder_step",
     )(
-        destinations.reshape(1, blocks), valid_counts, obs_tokens, grid_tokens.reshape(CELLS, D),
-        cotangent.reshape(CELLS, D), w_query, w_key, w_value, w_out, stencil_taps,
+        destinations.reshape(1, blocks), valid_counts, grid_tokens.reshape(CELLS, D),
+        cotangent.reshape(CELLS, D), stencil_taps, obs_tokens, w_query, w_key, w_value, w_out,
     )
-    anywhere = pl.BlockSpec(memory_space=pl.ANY)
     matrix = jax.ShapeDtypeStruct((D, D), F32)
     encoded, grad_obs, grad_grid, *sums = pl.pallas_call(
         write_kernel,
@@ -675,7 +714,7 @@
         scratch_shapes=[
             pltpu.VMEM((CELLS, D), BF), pltpu.VMEM((blocks, BLK, D), BF), pltpu.VMEM((CELLS, D), BF),
             pltpu.VMEM((3, 2, SIDE, SIDE, SIDE, 16, 128), BF), pltpu.VMEM((2, SIDE, SIDE, SIDE, 16, 128), BF),
-            pltpu.VMEM((4, D, D), F32), pltpu.SemaphoreType.DMA((5,)), pltpu.SemaphoreType.DMA((7,)),
+            pltpu.VMEM((4, D, D), F32), pltpu.SemaphoreType.DMA((10,)), pltpu.SemaphoreType.DMA((10,)),
         ],
         compiler_params=pltpu.CompilerParams(vmem_limit_bytes=62 * 2**20),
         name="write_results",

time: 201 us -> 188 us (0.935)
  Pallas kernels: 200 us -> 187 us
    pallas_call x1, Pallas kernels: 194 us -> 182 us  [on_device(): pl.pallas_call(functools.partial(kernel, nlat, n), out_shape=(tile, jax.S...]
where the time goes in v7:
time: 188 us
  Pallas kernels  187 us (99%)
    pallas_call x1, Pallas kernels, on_device(): pl.pallas_call(functools.partial(kernel, nlat, n), out_shape=(tile, jax.S...  182 us
    pallas_call x1, Pallas kernels, on_device(): pl.pallas_call(write_kernel, out_shape=(tile, jax.ShapeDtypeStruct((block...  5.47 us

profile of v7, /device:TPU:1, one launch (start us, length us, event | category | flops | bytes accessed | tf_op | source)
XLA Modules:
  0.0 187.6 jit_solution(3795718846806508993)
XLA Ops:
  0.6 181.5 %encoder_step.1 = (bf16[256,512]{1,0:T(8,128)(2,1)}, bf16[16,128,512]{2,1,0:T(8,128)(2,1)}, bf16[256,512]{1,0:T(8,128)(2,1)}, bf16[3,2,4,4,4,16,128]{6,5,4,3,2,1...) custom-call(s32[1,16]{1,0:T(1,128)} %bitcast.7, s32[1,16]{1,0:T(1,128)} %count_ref.1, ...), custom_call_target="tpu_custom_call" | custom-call | tf_op jit(solution)/shard_map/encoder_step/pallas_call | solution.py:649
  182.1 5.5 %write_results.1 = (bf16[256,512]{1,0:T(8,128)(2,1)}, bf16[16,128,512]{2,1,0:T(8,128)(2,1)}, bf16[256,512]{1,0:T(8,128)(2,1)}, f32[512,512]{1,0:T(8,128)}, f32[5...) custom-call(bf16[256,512]{1,0:T(8,128)(2,1)} %get-tuple-element.22.enc, ...), custom_call_target="tpu_custom_call" | custom-call | tf_op jit(solution)/shard_map/write_results/pallas_call | solution.py:706

commit v8 on v7

--- a/solution.py
+++ b/solution.py
@@ -470,6 +470,9 @@
 
         lax.fori_loop(0, HEADS // 4, four, 0)
 
+    def accumulate(c, w):
+        width = w * ROWS
+
         def weigh(j, carry):
             part = pl.ds(pl.multiple_of(j * 256, 256), 256)
             tokens = xs[pl.ds(c, w), 0:ROWS, :].reshape(width, D)
@@ -504,6 +507,7 @@
                             g_copy(i).wait_recv()
                             g_onward(i).start()
 
+        accumulate(CAP * g - 1, 2)
         pl.when(step == 0)(middle)
 
         for stage in range(2):
@@ -514,20 +518,22 @@
 
     lax.fori_loop(0, groups, backward, 0)
     differentiate(0, 1, 0)
-
+    accumulate(0, 1)
+
+    late[1].load(lambda rows, cols: dwt[cols, rows].astype(BF).T)
+    late[1].begin()
+    late[2].load(lambda rows, cols: dwt[D + cols.start : D + cols.stop, rows].astype(BF).T)
+    late[2].begin()
     grad_q = (acc_q[...].T * SCALING).astype(BF)
     dwq = dot(grid_ref[...].T, grad_q)
     late[0].load(lambda rows, cols: dwq[rows, cols])
-    late[1].load(lambda rows, cols: dwt[cols, rows].astype(BF).T)
-    late[2].load(lambda rows, cols: dwt[D + cols.start : D + cols.stop, rows].astype(BF).T)
-    for part in late:
-        part.begin()
+    late[0].begin()
     tap_sum.step(2)
 
     def late_step(stage):
         if stage < 6:
             early.step(stage + 2)
-        for part in late:
+        for part in (late[1], late[2], late[0]):
             part.step(stage)
 
     ggrid_ref[...] = (
@@ -545,6 +551,11 @@
     ).astype(BF)
     stores[1].start()
     late_step(1)
+    late_step(2)
+    late_step(3)
+    tap_sum.step(3, taps_ref)
+    late_step(4)
+    late_step(5)
     for i in range(1, n):
         if i not in FAR:
             g_copy(i).wait_recv()
@@ -569,13 +580,10 @@
         gobs_ref[b] = jnp.where(rank == 0, both[:BLK], both[BLK:])
         return carry
 
-    late_step(2)
     lax.fori_loop(0, blocks, unpack, 0)
     stores[2].start()
-    late_step(3)
-    tap_sum.step(3, taps_ref)
-    for stage in range(4, 8):
-        late_step(stage)
+    late_step(6)
+    late_step(7)
     for which in range(2):
         for copy in h_copies(which):
             copy.wait_send()

time: 188 us -> 186 us (0.989)
  no operation moved by 1% of the time
where the time goes in v8:
time: 186 us
  Pallas kernels  186 us (100%)
    pallas_call x1, Pallas kernels, on_device(): pl.pallas_call(functools.partial(kernel, nlat, n), out_shape=(tile, jax.S...  180 us
    pallas_call x1, Pallas kernels, on_device(): pl.pallas_call(write_kernel, out_shape=(tile, jax.ShapeDtypeStruct((block...  5.47 us

profile of v8, /device:TPU:1, one launch (start us, length us, event | category | flops | bytes accessed | tf_op | source)
XLA Modules:
  0.0 186.2 jit_solution(3676337175096791920)
XLA Ops:
  0.6 180.1 %encoder_step.1 = (bf16[256,512]{1,0:T(8,128)(2,1)}, bf16[16,128,512]{2,1,0:T(8,128)(2,1)}, bf16[256,512]{1,0:T(8,128)(2,1)}, bf16[3,2,4,4,4,16,128]{6,5,4,3,2,1...) custom-call(s32[1,16]{1,0:T(1,128)} %bitcast.7, s32[1,16]{1,0:T(1,128)} %count_ref.1, ...), custom_call_target="tpu_custom_call" | custom-call | tf_op jit(solution)/shard_map/encoder_step/pallas_call | solution.py:657
  180.7 5.5 %write_results.1 = (bf16[256,512]{1,0:T(8,128)(2,1)}, bf16[16,128,512]{2,1,0:T(8,128)(2,1)}, bf16[256,512]{1,0:T(8,128)(2,1)}, f32[512,512]{1,0:T(8,128)}, f32[5...) custom-call(bf16[256,512]{1,0:T(8,128)(2,1)} %get-tuple-element.22.enc, ...), custom_call_target="tpu_custom_call" | custom-call | tf_op jit(solution)/shard_map/write_results/pallas_call | solution.py:714

commit v9 on v8

--- a/solution.py
+++ b/solution.py
@@ -68,18 +68,13 @@
 
 
 class Exchange:
-    def __init__(self, count, me, whom, copy):
-        self.count, self.me, self.whom, self.copy = count, me, whom, copy
+    def __init__(self, group, copy):
+        self.count, self.me, self.peers, _ = group
+        self.copy = copy
 
     def each(self, body):
-        def step(o, carry):
-            body(lax.rem(self.me + o, self.count))
-            return carry
-
-        if self.count == 2:
-            body(1 - self.me)
-        else:
-            lax.fori_loop(1, self.count, step, 0)
+        for at in self.peers:
+            body(at)
 
     def start(self):
         self.each(lambda at: self.copy(at, self.me).start())
@@ -92,15 +87,15 @@
 
 
 def scatter(group, src, dst, ssem, rsem):
-    count, me, whom = group
-    return Exchange(count, me, whom, lambda to, frm: pltpu.make_async_remote_copy(
+    whom = group[3]
+    return Exchange(group, lambda to, frm: pltpu.make_async_remote_copy(
         src_ref=src.at[to], dst_ref=dst.at[frm], send_sem=ssem.at[to], recv_sem=rsem.at[frm],
         device_id=whom(to), device_id_type=MESH))
 
 
 def gather(group, buf, ssem, rsem):
-    count, me, whom = group
-    return Exchange(count, me, whom, lambda to, frm: pltpu.make_async_remote_copy(
+    _, me, _, whom = group
+    return Exchange(group, lambda to, frm: pltpu.make_async_remote_copy(
         src_ref=buf.at[me], dst_ref=buf.at[frm], send_sem=ssem.at[to], recv_sem=rsem.at[frm],
         device_id=whom(to), device_id_type=MESH))
 
@@ -133,11 +128,11 @@
     def step(self, stage):
         self.stages[stage].wait()
         if stage < 4:
-            me, count = self.me[stage], self.stages[stage].count
+            me = self.me[stage]
             own, got = self.bufs[2 * stage], self.bufs[2 * stage + 1]
             held = own[me].astype(F32)
-            for o in range(1, count):
-                held = held + got[lax.rem(me + o, count)].astype(F32)
+            for at in self.stages[stage].peers:
+                held = held + got[at].astype(F32)
             target = self.place if stage == 3 else self.bufs[2 * stage + 2]
             target[...] = held.astype(BF)
         if stage < 7:
@@ -193,10 +188,14 @@
     ]
     x_at, core = lat // 2, lax.rem(lat, 2)
     y, z = me // SIDE, lax.rem(me, SIDE)
-    on_core = (2, core, lambda at: {"lat": 2 * x_at + at})
-    on_x = (SIDE, x_at, lambda at: {"lat": 2 * at + core})
-    on_y = (SIDE, y, lambda at: {"lon": at * SIDE + z})
-    on_z = (SIDE, z, lambda at: {"lon": y * SIDE + at})
+
+    def ring(me, whom):
+        return SIDE, me, [lax.rem(me + o, SIDE) for o in range(1, SIDE)], whom
+
+    on_core = (2, core, [1 - core], lambda at: {"lat": 2 * x_at + at})
+    on_x = ring(x_at, lambda at: {"lat": 2 * at + core})
+    on_y = ring(y, lambda at: {"lon": at * SIDE + z})
+    on_z = ring(z, lambda at: {"lon": y * SIDE + at})
     orders = ((on_x, on_y, on_z), (on_y, on_z, on_x), (on_z, on_x, on_y), (on_x, on_y, on_z))
     *late, early = (
         MatrixSum(
@@ -481,6 +480,12 @@
 
         lax.fori_loop(0, 4, weigh, 0)
 
+    def forward_back(k):
+        for i in (CAP * BACK[k] - 2, CAP * BACK[k] - 1):
+            if i in FAR:
+                g_copy(i).wait_recv()
+                g_onward(i).start()
+
     def backward(step, carry):
         g = 6 - step + 6 * ((step + 4) // 8) - 4 * ((step + 2) // 8)
         differentiate(CAP * g - 1, 2, g)
@@ -501,11 +506,8 @@
                 else:
                     ret[0] = send[0, 0:ROWS, :]
                 g_copy(first + 1).start()
-                if k >= 4:
-                    for i in (CAP * BACK[k - 4] - 2, CAP * BACK[k - 4] - 1):
-                        if i in FAR:
-                            g_copy(i).wait_recv()
-                            g_onward(i).start()
+                if k >= 6:
+                    forward_back(k - 6)
 
         accumulate(CAP * g - 1, 2)
         pl.when(step == 0)(middle)
@@ -517,6 +519,8 @@
         return carry
 
     lax.fori_loop(0, groups, backward, 0)
+    forward_back(2)
+    forward_back(3)
     differentiate(0, 1, 0)
     accumulate(0, 1)
 

time: 186 us -> 185 us (level)
  Pallas kernels: 186 us -> 184 us
where the time goes in v9:
time: 185 us
  Pallas kernels  184 us (99%)
    pallas_call x1, Pallas kernels, on_device(): pl.pallas_call(functools.partial(kernel, nlat, n), out_shape=(tile, jax.S...  179 us
    pallas_call x1, Pallas kernels, on_device(): pl.pallas_call(write_kernel, out_shape=(tile, jax.ShapeDtypeStruct((block...  5.47 us

profile of v9, /device:TPU:1, one launch (start us, length us, event | category | flops | bytes accessed | tf_op | source)
XLA Modules:
  0.0 185.0 jit_solution(8216403791285619990)
XLA Ops:
  0.6 178.8 %encoder_step.1 = (bf16[256,512]{1,0:T(8,128)(2,1)}, bf16[16,128,512]{2,1,0:T(8,128)(2,1)}, bf16[256,512]{1,0:T(8,128)(2,1)}, bf16[3,2,4,4,4,16,128]{6,5,4,3,2,1...) custom-call(s32[1,16]{1,0:T(1,128)} %bitcast.7, s32[1,16]{1,0:T(1,128)} %count_ref.1, ...), custom_call_target="tpu_custom_call" | custom-call | tf_op jit(solution)/shard_map/encoder_step/pallas_call | solution.py:661
  179.4 5.5 %write_results.1 = (bf16[256,512]{1,0:T(8,128)(2,1)}, bf16[16,128,512]{2,1,0:T(8,128)(2,1)}, bf16[256,512]{1,0:T(8,128)(2,1)}, f32[512,512]{1,0:T(8,128)}, f32[5...) custom-call(bf16[256,512]{1,0:T(8,128)(2,1)} %get-tuple-element.22.enc, ...), custom_call_target="tpu_custom_call" | custom-call | tf_op jit(solution)/shard_map/write_results/pallas_call | solution.py:718

commit v10 on v9

--- a/solution.py
+++ b/solution.py
@@ -68,36 +68,39 @@
 
 
 class Exchange:
-    def __init__(self, group, copy):
+    def __init__(self, group, copy, every):
         self.count, self.me, self.peers, _ = group
-        self.copy = copy
-
-    def each(self, body):
+        self.copy, self.every = copy, every
+
+    def start(self):
         for at in self.peers:
-            body(at)
-
-    def start(self):
-        self.each(lambda at: self.copy(at, self.me).start())
+            self.copy(at).start()
 
     def wait(self):
-        self.each(lambda at: self.copy(at, at).wait_recv())
+        self.every.wait_recv()
 
     def sent(self):
-        self.each(lambda at: self.copy(at, self.me).wait_send())
+        self.every.wait_send()
+
+
+def exchange(group, pieces, dst, ssem, rsem):
+    count, me, peers, whom = group
+
+    def copy(src, into, to):
+        return pltpu.make_async_remote_copy(
+            src_ref=src, dst_ref=into, send_sem=ssem, recv_sem=rsem, device_id=whom(to),
+            device_id_type=MESH)
+
+    whole = dst.at[pl.ds(0, count - 1)]
+    return Exchange(group, lambda to: copy(pieces(to), dst.at[me], to), copy(whole, whole, peers[0]))
 
 
 def scatter(group, src, dst, ssem, rsem):
-    whom = group[3]
-    return Exchange(group, lambda to, frm: pltpu.make_async_remote_copy(
-        src_ref=src.at[to], dst_ref=dst.at[frm], send_sem=ssem.at[to], recv_sem=rsem.at[frm],
-        device_id=whom(to), device_id_type=MESH))
+    return exchange(group, lambda to: src.at[to], dst, ssem, rsem)
 
 
 def gather(group, buf, ssem, rsem):
-    _, me, _, whom = group
-    return Exchange(group, lambda to, frm: pltpu.make_async_remote_copy(
-        src_ref=buf.at[me], dst_ref=buf.at[frm], send_sem=ssem.at[to], recv_sem=rsem.at[frm],
-        device_id=whom(to), device_id_type=MESH))
+    return exchange(group, lambda to: buf.at[group[1]], buf, ssem, rsem)
 
 
 class MatrixSum:
@@ -447,8 +450,9 @@
     for i in range(1, n):
         x_copy(i).wait_send()
 
-    def differentiate(c, w, g):
+    def differentiate(c, w, g, half):
         width = w * ROWS
+        lanes = pl.ds(pl.multiple_of(half * 2 * ROWS, 2 * ROWS), width)
         mark(c, w)
         rows = pl.ds(pl.multiple_of(c * ROWS, ROWS), width)
 
@@ -462,8 +466,8 @@
                 values = kv[rows, pl.ds(pl.multiple_of(D + pair, 128), 128)]
                 weights = jnp.exp(dot(keys, qzt[h]) + masked(width) - m_ref[h])
                 grads = (weights * (dot(values, dozt[h]) - d_ref[h])).astype(BF)
-                dkvt[mine, :width] = dot_nt(qt[mine, :], grads).astype(BF)
-                dkvt[also, :width] = dot_nt(dot_t[mine, :], weights.astype(BF)).astype(BF)
+                dkvt[mine, lanes] = dot_nt(qt[mine, :], grads).astype(BF)
+                dkvt[also, lanes] = dot_nt(dot_t[mine, :], weights.astype(BF)).astype(BF)
                 acc_q[mine, :] += dot(kt[g, mine, :width], grads)
             return carry
 
@@ -488,11 +492,13 @@
 
     def backward(step, carry):
         g = 6 - step + 6 * ((step + 4) // 8) - 4 * ((step + 2) // 8)
-        differentiate(CAP * g - 1, 2, g)
+        half = 1 - lax.rem(step, 2)
+        differentiate(CAP * g - 1, 2, g, half)
+        lanes = pl.ds(pl.multiple_of(half * 2 * ROWS, 2 * ROWS), 2 * ROWS)
 
         def turn(j, inner):
             cols = pl.ds(pl.multiple_of(j * 256, 256), 256)
-            part = dot(wkv[cols, :], dkvt[...]).astype(BF).T
+            part = dot(wkv[cols, :], dkvt[:, lanes]).astype(BF).T
             send[pl.ds(CAP * g - 2, 2), 0:ROWS, cols] = part.reshape(2, ROWS, 256)
             return inner
 
@@ -509,7 +515,10 @@
                 if k >= 6:
                     forward_back(k - 6)
 
-        accumulate(CAP * g - 1, 2)
+        @pl.when(half == 0)
+        def _():
+            accumulate(CAP * g - 1, 4)
+
         pl.when(step == 0)(middle)
 
         for stage in range(2):
@@ -521,7 +530,7 @@
     lax.fori_loop(0, groups, backward, 0)
     forward_back(2)
     forward_back(3)
-    differentiate(0, 1, 0)
+    differentiate(0, 1, 0, 0)
     accumulate(0, 1)
 
     late[1].load(lambda rows, cols: dwt[cols, rows].astype(BF).T)
@@ -649,8 +658,7 @@
     lon_sem = pltpu.SemaphoreType.DMA((n,))
     far_sem = pltpu.SemaphoreType.DMA((len(FAR),))
     halo_sem = pltpu.SemaphoreType.DMA((2, 4))
-    ring_sem, core_sem = pltpu.SemaphoreType.DMA((SIDE,)), pltpu.SemaphoreType.DMA((2,))
-    sems = [core_sem] * 2 + [ring_sem] * 6
+    sems = [pltpu.SemaphoreType.DMA] * 8
     sums = []
     for _ in range(4):
         for lead in ((2, SIDE, SIDE, SIDE), (SIDE,) * 3, (SIDE,) * 2, (SIDE,)):
@@ -688,7 +696,7 @@
             pltpu.VMEM((HEADS, 1, CELLS), F32),
             pltpu.VMEM((HEADS, 1, CELLS), F32),
             pltpu.VMEM((HEADS, 1, CELLS), F32),
-            pltpu.VMEM((2 * D, 2 * ROWS), BF),
+            pltpu.VMEM((2 * D, 4 * ROWS), BF),
             pltpu.VMEM((2 * D, D), F32),
             pltpu.VMEM((CELLS, D), BF),
             pltpu.VMEM((CELLS, D), BF),

time: 185 us -> 182 us (0.984)
  Pallas kernels: 184 us -> 181 us
    pallas_call x1, Pallas kernels: 179 us -> 176 us  [on_device(): pl.pallas_call(functools.partial(kernel, nlat, n), out_shape=(tile, jax.S...]
where the time goes in v10:
time: 182 us
  Pallas kernels  181 us (99%)
    pallas_call x1, Pallas kernels, on_device(): pl.pallas_call(functools.partial(kernel, nlat, n), out_shape=(tile, jax.S...  176 us
    pallas_call x1, Pallas kernels, on_device(): pl.pallas_call(write_kernel, out_shape=(tile, jax.ShapeDtypeStruct((block...  5.47 us

profile of v10, /device:TPU:1, one launch (start us, length us, event | category | flops | bytes accessed | tf_op | source)
XLA Modules:
  0.0 181.8 jit_solution(15285116663859507164)
XLA Ops:
  0.6 175.5 %encoder_step.1 = (bf16[256,512]{1,0:T(8,128)(2,1)}, bf16[16,128,512]{2,1,0:T(8,128)(2,1)}, bf16[256,512]{1,0:T(8,128)(2,1)}, bf16[3,2,4,4,4,16,128]{6,5,4,3,2,1...) custom-call(s32[1,16]{1,0:T(1,128)} %bitcast.7, s32[1,16]{1,0:T(1,128)} %count_ref.1, ...), custom_call_target="tpu_custom_call" | custom-call | tf_op jit(solution)/shard_map/encoder_step/pallas_call | solution.py:669
  176.2 5.5 %write_results.1 = (bf16[256,512]{1,0:T(8,128)(2,1)}, bf16[16,128,512]{2,1,0:T(8,128)(2,1)}, bf16[256,512]{1,0:T(8,128)(2,1)}, f32[512,512]{1,0:T(8,128)}, f32[5...) custom-call(bf16[256,512]{1,0:T(8,128)(2,1)} %get-tuple-element.22.enc, ...), custom_call_target="tpu_custom_call" | custom-call | tf_op jit(solution)/shard_map/write_results/pallas_call | solution.py:726

commit v11 on v10

--- a/solution.py
+++ b/solution.py
@@ -15,6 +15,7 @@
 ROWS = CAP * BLK
 CELLS = 256
 TILE = 16
+VROWS = HD + 16
 SCALING = HD ** (-0.5)
 MESH = pl.DeviceIdType.MESH
 SIDE = 4
@@ -334,6 +335,8 @@
     dwt[...] = jnp.zeros_like(dwt)
     m_ref[...] = jnp.full(m_ref.shape, -1e30, F32)
     l_ref[...] = jnp.zeros_like(l_ref)
+    for h in range(HEADS):
+        vt[h * VROWS + HD : (h + 1) * VROWS, :] = jnp.ones((VROWS - HD, 2 * ROWS), BF)
     key_ids = lax.broadcasted_iota(jnp.int32, (BLK, 128), 0).astype(F32)
 
     def masked(width):
@@ -361,29 +364,28 @@
             if j < 2:
                 kt[g, cols, :width] = part.T
             else:
-                vt[j * 256 - D : (j + 1) * 256 - D, :width] = part.T
+                turned_part = part.T
+                for e in range(4):
+                    h = (j - 2) * 4 + e
+                    vt[h * VROWS : h * VROWS + HD, :width] = turned_part[e * HD : (e + 1) * HD, :]
 
     def attend(c, w):
         width = w * ROWS
         mark(c, w)
         rows = pl.ds(pl.multiple_of(c * ROWS, ROWS), width)
 
-        def four(q, carry):
-            for e in range(4):
-                h = 4 * q + e
-                mine = pl.ds(pl.multiple_of(h * HD, HD), HD)
-                here = pl.ds(pl.multiple_of((2 * q + e // 2) * 128, 128), 128)
-                scores = dot(kv[rows, here], qzt[h]) + masked(width)
-                old = m_ref[h]
-                new = jnp.maximum(old, jnp.max(scores, 0, keepdims=True))
-                raised = jnp.exp(scores - new)
-                shrink = jnp.exp(old - new)
-                l_ref[h] = l_ref[h] * shrink + jnp.sum(raised, 0, keepdims=True)
-                m_ref[h] = new
-                acc_o[mine, :] = acc_o[mine, :] * shrink + dot(vt[mine, :width], raised.astype(BF))
-            return carry
-
-        lax.fori_loop(0, HEADS // 4, four, 0)
+        for h in range(HEADS):
+            mine = slice(h * HD, (h + 1) * HD)
+            here = slice((h // 2) * 128, (h // 2 + 1) * 128)
+            scores = dot(kv[rows, here], qzt[h]) + masked(width)
+            old = m_ref[h]
+            new = jnp.maximum(old, jnp.max(scores, 0, keepdims=True))
+            raised = jnp.exp(scores - new).astype(BF)
+            shrink = jnp.exp(old - new)
+            mixed = dot(vt[h * VROWS : (h + 1) * VROWS, :width], raised)
+            l_ref[h] = l_ref[h] * shrink + mixed[HD : HD + 1, :]
+            m_ref[h] = new
+            acc_o[mine, :] = acc_o[mine, :] * shrink + mixed[:HD, :]
 
     project(0, 1, 0)
     attend(0, 1)
@@ -684,7 +686,7 @@
             pltpu.VMEM((len(FAR), ROWS, D), BF),
             pltpu.VMEM(((n + 1) * ROWS, 2 * D), BF),
             pltpu.VMEM((n // 2 + 1, D, 2 * ROWS), BF),
-            pltpu.VMEM((D, 2 * ROWS), BF),
+            pltpu.VMEM((HEADS * VROWS, 2 * ROWS), BF),
             pltpu.VMEM((2 * ROWS, 128), F32),
             pltpu.VMEM((D, 2 * D), BF),
             pltpu.VMEM((D, CELLS), BF),

time: 182 us -> 182 us (level)
  no operation moved by 1% of the time
where the time goes in v11:
time: 182 us
  Pallas kernels  181 us (99%)
    pallas_call x1, Pallas kernels, on_device(): pl.pallas_call(functools.partial(kernel, nlat, n), out_shape=(tile, jax.S...  175 us
    pallas_call x1, Pallas kernels, on_device(): pl.pallas_call(write_kernel, out_shape=(tile, jax.ShapeDtypeStruct((block...  5.47 us

profile of v11, /device:TPU:1, one launch (start us, length us, event | category | flops | bytes accessed | tf_op | source)
XLA Modules:
  0.0 181.6 jit_solution(2551288004940828306)
XLA Ops:
  0.6 175.4 %encoder_step.1 = (bf16[256,512]{1,0:T(8,128)(2,1)}, bf16[16,128,512]{2,1,0:T(8,128)(2,1)}, bf16[256,512]{1,0:T(8,128)(2,1)}, bf16[3,2,4,4,4,16,128]{6,5,4,3,2,1...) custom-call(s32[1,16]{1,0:T(1,128)} %bitcast.7, s32[1,16]{1,0:T(1,128)} %count_ref.1, ...), custom_call_target="tpu_custom_call" | custom-call | tf_op jit(solution)/shard_map/encoder_step/pallas_call | solution.py:671
  176.0 5.5 %write_results.1 = (bf16[256,512]{1,0:T(8,128)(2,1)}, bf16[16,128,512]{2,1,0:T(8,128)(2,1)}, bf16[256,512]{1,0:T(8,128)(2,1)}, f32[512,512]{1,0:T(8,128)}, f32[5...) custom-call(bf16[256,512]{1,0:T(8,128)(2,1)} %get-tuple-element.22.enc, ...), custom_call_target="tpu_custom_call" | custom-call | tf_op jit(solution)/shard_map/write_results/pallas_call | solution.py:728
